TPU v7x, 128 devices: a whole 4x4x4 slice. The times are simulated.
128 devices in a mesh: role: 2 (over z_hi), gx: 8 (over y, z_lo), gy: 8 (over x, core).
Axes of the slice: x: 4, y: 4, z: 4 (z_hi: 2, z_lo: 2; z = z_hi * 2 + z_lo), core: 2. Of those that a mesh axis runs over, the one named last changes fastest.
Arguments:
- design: float32 [256, 256, 256], P(('gx', 'gy'), None, 'role'), may hold values from 0 to 1
- force: float32 [3, 128, 128, 256], P(None, 'gx', 'gy', 'role'), may hold values from -6 to 6
- clamped_dof_mask: int32 [3, 128, 128, 256], P(None, 'gx', 'gy', 'role'), may hold values 0 or 1
- stiffness: float32 [81, 81], replicated, may hold values from -1 to 70, as said below
Outputs:
- sensitivity: float32 [256, 256, 256], P(('gx', 'gy'), None, 'role')
- displacement: float32 [3, 128, 128, 256], P(None, 'gx', 'gy', 'role')
Inputs may be any that keep to these rules, and one draw needn't show every extreme that they name: `stiffness`: symmetric, and each diagonal entry exceeds the sum of the magnitudes of the other entries of its row.
All inputs are finite; a program needn't handle non-finite values. No bound on the sum of `clamped_dof_mask` on one device may be relied on, other than what follows from the above.
Results may differ from a plain program's by a relative error of at most 0.00013.
Values sent between devices are 32-bit elements; how exact they have to be, the bound alone decides.
A program may use at most 64 MiB of HBM per device.

v0:
```python
import jax
import jax.numpy as jnp
from jax import lax
from jax.sharding import Mesh
from jax.sharding import PartitionSpec as P

ITERS = 3
RADIUS = 2
GX_GY = ("gx_0", "gx_1", "gy_0", "gy_1")
ROLE_GX_GY = ("role", "gx_0", "gx_1", "gy_0", "gy_1")
GX = ("gx_0", "gx_1")
GY = ("gy_0", "gy_1")


sharpness = 4.0
threshold = 0.5
floor_stiff = 0.001


def with_halo(block, sides, width):
    for axis, dim in sides:
        count = lax.axis_size(axis)
        forward = [(i, i + 1) for i in range(count - 1)]
        backward = [(target, source) for source, target in forward]
        low = lax.ppermute(
            lax.slice_in_dim(block, block.shape[dim] - width, None, axis=dim), axis, forward
        )
        high = lax.ppermute(lax.slice_in_dim(block, 0, width, axis=dim), axis, backward)
        block = jnp.concatenate([low, block, high], axis=dim)
    return block


def over_axes(shard, axes):
    for axis in axes:
        shard = lax.psum(shard, axis)
    return shard


def hat_list():
    return [float(RADIUS + 1 - abs(shift_idx - RADIUS)) for shift_idx in range(2 * RADIUS + 1)]


def smooth_axis(padded, axis_num, length):
    result = None
    for offset_idx, weight in enumerate(hat_list()):
        portion = weight * lax.slice_in_dim(padded, offset_idx, offset_idx + length, axis=axis_num)
        result = portion if result is None else result + portion
    return result


def axis_count(start, length, extent):
    places = start + jnp.arange(length, dtype=jnp.int32)
    counted = jnp.zeros((length,), jnp.float32)
    for offset_idx, weight in enumerate(hat_list()):
        target = places + (offset_idx - RADIUS)
        inside = jnp.logical_and(target >= 0, target < extent)
        counted = counted + weight * inside.astype(jnp.float32)
    return counted


def slab_weight(shape):
    extent_x, extent_y, extent_z = shape
    along_x = axis_count(
        lax.axis_index(GX_GY) * extent_x, extent_x, extent_x * lax.axis_size(GX_GY)
    )
    along_y = axis_count(0, extent_y, extent_y)
    along_z = axis_count(
        lax.axis_index("role") * extent_z, extent_z, extent_z * lax.axis_size("role")
    )
    return along_x[:, None, None] * along_y[None, :, None] * along_z[None, None, :]


def slab_smooth(field):
    extent_x, extent_y, extent_z = field.shape
    padded = with_halo(field, (("role", 2), (GX_GY, 0)), RADIUS)
    padded = jnp.pad(padded, ((0, 0), (RADIUS, RADIUS), (0, 0)))
    return smooth_axis(smooth_axis(smooth_axis(padded, 2, extent_z), 1, extent_y), 0, extent_x)


def heaviside_projection(values):
    scaled = jnp.tanh(sharpness * threshold) + jnp.tanh(sharpness * (1.0 - threshold))
    return (jnp.tanh(sharpness * threshold) + jnp.tanh(sharpness * (values - threshold))) / scaled


def slope(values):
    scaled = jnp.tanh(sharpness * threshold) + jnp.tanh(sharpness * (1.0 - threshold))
    bent = jnp.tanh(sharpness * (values - threshold))
    return sharpness * (1.0 - bent * bent) / scaled


def element_mean(fine):
    count_x = fine.shape[0] // 4
    count_y = fine.shape[1] // 4
    count_z = fine.shape[2] // 2
    return fine.reshape(count_x, 4, count_y, 4, count_z, 2).mean(axis=(1, 3, 5))


def spread(elements):
    count_x, count_y, count_z = elements.shape
    widened = jnp.broadcast_to(
        elements[:, None, :, None, :, None], (count_x, 4, count_y, 4, count_z, 2)
    )
    return widened.reshape(4 * count_x, 4 * count_y, 2 * count_z)


def corner_table(node_len):
    elem_len = (node_len - 1) // 2
    nodes = jnp.arange(node_len, dtype=jnp.int32)[None, :, None]
    elems = jnp.arange(elem_len, dtype=jnp.int32)[None, None, :]
    corners = jnp.arange(3, dtype=jnp.int32)[:, None, None]
    return (nodes == 2 * elems + corners).astype(jnp.float32)


def fold_table(node_len):
    rows = jnp.arange(node_len + 2, dtype=jnp.int32)[:, None]
    cols = jnp.arange(node_len, dtype=jnp.int32)[None, :]
    target = jnp.clip(rows - 1, 0, node_len - 1)
    return (target == cols).astype(jnp.float32)


def split_axis(values, axis_num):
    half_len = (values.shape[axis_num] - 1) // 2
    pieces = [
        lax.slice_in_dim(values, corner, corner + 2 * half_len - 1, stride=2, axis=axis_num)
        for corner in range(3)
    ]
    return jnp.stack(pieces, axis=0)


def split_nodes(values):
    stacked = split_axis(values, 1)
    stacked = split_axis(stacked, 3)
    table = corner_table(values.shape[3])
    stacked = jnp.einsum(
        "baqxyk,ckg->cbaqxyg",
        stacked,
        table,
        precision=lax.Precision.HIGHEST,
        preferred_element_type=jnp.float32,
    )
    return stacked.reshape(81, -1)


def merge_axis(parts, axis_num):
    opening = parts[0]
    middle = parts[1]
    closing = parts[2]
    length = opening.shape[axis_num]
    before = [(0, 0)] * opening.ndim
    before[axis_num] = (0, 1)
    behind = [(0, 0)] * opening.ndim
    behind[axis_num] = (1, 0)
    evens = jnp.pad(opening, before) + jnp.pad(closing, behind)
    leading = lax.slice_in_dim(evens, 0, length, axis=axis_num)
    ending = lax.slice_in_dim(evens, length, length + 1, axis=axis_num)
    braided = jnp.stack([leading, middle], axis=axis_num + 1)
    new_shape = list(leading.shape)
    new_shape[axis_num] = 2 * length
    return jnp.concatenate([braided.reshape(new_shape), ending], axis=axis_num)


def merge_nodes(stiffness_product, element_shape):
    reshaped = stiffness_product.reshape((3, 3, 3, 3) + tuple(element_shape))
    table = corner_table(2 * element_shape[2] + 1)
    merged = jnp.einsum(
        "cbaqxyg,ckg->baqxyk",
        reshaped,
        table,
        precision=lax.Precision.HIGHEST,
        preferred_element_type=jnp.float32,
    )
    merged = merge_axis(merged, 3)
    return merge_axis(merged, 1)


def fold_axis(padded, axis_num):
    inner_len = padded.shape[axis_num] - 2
    below = lax.slice_in_dim(padded, 0, 1, axis=axis_num)
    above = lax.slice_in_dim(padded, inner_len + 1, inner_len + 2, axis=axis_num)
    lowest = lax.slice_in_dim(padded, 1, 2, axis=axis_num) + below
    highest = lax.slice_in_dim(padded, inner_len, inner_len + 1, axis=axis_num) + above
    centre = lax.slice_in_dim(padded, 2, inner_len, axis=axis_num)
    return jnp.concatenate([lowest, centre, highest], axis=axis_num)


def shared_sum(values):
    padded = with_halo(values, (("role", 3), (GX, 1), (GY, 2)), 1)
    folded = fold_axis(fold_axis(padded, 1), 2)
    table = fold_table(values.shape[3])
    return jnp.einsum(
        "qxyk,kn->qxyn",
        folded,
        table,
        precision=lax.Precision.HIGHEST,
        preferred_element_type=jnp.float32,
    )


def inner_sum(left, right):
    local_part = jnp.sum((left * right)[:, :-1, :-1, :-1])
    return over_axes(local_part, ROLE_GX_GY)


def conjugate_gradient_solve(operate, rhs):
    solution = jnp.zeros_like(rhs)
    residual = rhs
    direction = rhs
    current = inner_sum(residual, residual)
    for sweep in range(ITERS):
        applied = operate(direction)
        step_len = current / inner_sum(direction, applied)
        solution = solution + step_len * direction
        residual = residual - step_len * applied
        updated = inner_sum(residual, residual)
        direction = residual + updated / current * direction
        current = updated
    return solution


def on_device(design, force, clamped_dof_mask, stiffness):
    filter_weight_grid = slab_weight(design.shape)
    filtered = slab_smooth(design) / filter_weight_grid
    density_slab = element_mean(heaviside_projection(filtered))
    density = lax.all_to_all(density_slab, GY, split_axis=1, concat_axis=0, tiled=True)
    factor = floor_stiff + (1.0 - floor_stiff) * density**3
    behind = ((0, 0), (0, 1), (0, 1), (0, 1))
    owned = jnp.concatenate([force, (1 - clamped_dof_mask).astype(jnp.float32)], axis=0)
    shared = shared_sum(jnp.pad(owned, behind))
    free = shared[3:]
    rhs = free * shared[:3]
    scales = factor.reshape(-1)

    def operate(values):
        columns = split_nodes(free * values)
        stiffness_product = (
            jnp.dot(
                stiffness,
                columns,
                precision=lax.Precision.HIGHEST,
                preferred_element_type=jnp.float32,
            )
            * scales[None, :]
        )
        return free * shared_sum(merge_nodes(stiffness_product, factor.shape))

    solution = conjugate_gradient_solve(operate, rhs)
    columns = split_nodes(solution)
    energy = jnp.sum(
        columns
        * jnp.dot(
            stiffness, columns, precision=lax.Precision.HIGHEST, preferred_element_type=jnp.float32
        ),
        axis=0,
    ).reshape(factor.shape)
    element_grad = -3.0 * density**2 * (1.0 - floor_stiff) * energy / 32.0
    slab_grad = lax.all_to_all(element_grad, GY, split_axis=0, concat_axis=1, tiled=True)
    voxel_grad = spread(slab_grad) * slope(filtered)
    sensitivity = slab_smooth(voxel_grad / filter_weight_grid)
    return (sensitivity, solution[:, :-1, :-1, :-1])


def solution(mesh):
    torus = Mesh(
        mesh.devices.reshape(mesh.shape["role"], 4, 2, 4, 2),
        ("role", "gx_0", "gx_1", "gy_0", "gy_1"),
    )
    return jax.shard_map(
        on_device,
        mesh=torus,
        in_specs=(P(GX_GY, None, "role"), P(None, GX, GY, "role"), P(None, GX, GY, "role"), P()),
        out_specs=(P(GX_GY, None, "role"), P(None, GX, GY, "role")),
        check_vma=False,
    )
```

profile of v0, /device:TPU:1, one launch (start us, length us, event | category | flops | bytes accessed | tf_op | source)
XLA Modules:
  0.0 571.2 jit_solution(5358044814999670989)
XLA Ops:
  0.7 6.5 %collective-permute-start.4 = (f32[6,17,17,1]{2,3,1,0:T(1,128)S(1)}, f32[6,17,17,1]{2,3,1,0:T(1,128)S(1)}, u32[]{:S(2)}, u32[]{:S(2)}) collective-permute-start(f32[6,17,17,1]{2,3,1,0:T(1,128)S(1)} %slice.514), channel_id=1, source_target_pairs={{0,64},{1,65},{2,66},{3,67},{4,68},{5,69},{6,70},{7,71},{8,72},{9,... | collective-permute-start | bytes 20816 | tf_op jit(solution)/shard_map/ppermute | solution.py:25
  19.6 9.4 %collective-permute-done.5 = f32[6,17,17,1]{2,3,1,0:T(1,128)S(1)} collective-permute-done((f32[6,17,17,1]{2,3,1,0:T(1,128)S(1)}, f32[6,17,17,1]{2,3,1,0:T(1,128)S(1)}, u32[]{:S(2)}, u32[]{:S(2)}) %collective-permute-start.5) | collective-permute-done | bytes 6968 | tf_op jit(solution)/shard_map/ppermute | solution.py:28
  41.7 5.9 %collective-permute-start.8 = (f32[6,19,1,131]{3,2,1,0:T(1,128)S(1)}, f32[6,19,1,131]{3,2,1,0:T(1,128)S(1)}, u32[]{:S(2)}, u32[]{:S(2)}) collective-permute-start(f32[6,19,1,131]{3,2,1,0:T(1,128)S(1)} %get-tuple-element.22), channel_id=1, source_target_pairs={{0,1},{1,2},{2,3},{3,4},{4,5},{5,6},{6,7},{8,9},{9,10},{10,11},{11... | collective-permute-start | bytes 179216 | tf_op jit(solution)/shard_map/ppermute | solution.py:25
  50.6 3.6 collective-permute-start.2
  63.8 5.8 %slice.538 = f32[3,3,8,8,129]{4,3,2,1,0:T(8,128)} slice(f32[3,3,8,17,129]{4,3,2,1,0:T(8,128)} %pad_maximum_fusion.2), slice={[0:3:1], [0:3:1], [0:8:1], [2:17:2], [0:129:1]} | slice | bytes 594432 | tf_op jit(solution)/shard_map/slice | solution.py:124
  69.6 5.7 slice.537
  75.2 5.7 slice.536
  85.9 5.7 reduce_sum.80
  96.6 5.1 all-to-all-start
  101.7 4.4 fusion.40
  111.5 3.9 fusion.3
  135.9 4.3 collective-permute-done.11
  142.6 4.1 collective-permute-start.12
  148.1 3.7 collective-permute-done.13
  152.2 6.1 %collective-permute-start.14 = (f32[3,19,1,131]{3,2,1,0:T(1,128)S(1)}, f32[3,19,1,131]{3,2,1,0:T(1,128)S(1)}, u32[]{:S(2)}, u32[]{:S(2)}) collective-permute-start(f32[3,19,1,131]{3,2,1,0:T(1,128)S(1)} %get-tuple-element.30), channel_id=1, source_target_pairs={{0,1},{1,2},{2,3},{3,4},{4,5},{5,6},{6,7},{8,9},{9,10},{10,11},{11... | collective-permute-start | bytes 89612 | tf_op jit(solution)/shard_map/ppermute | solution.py:25
  160.3 3.6 collective-permute-done.15
  168.8 5.9 %all-reduce.19 = (f32[]{:T(128)}, f32[]{:T(128)}) all-reduce(f32[]{:T(128)} %get-tuple-element.3, f32[]{:T(128)} %get-tuple-element.2), channel_id=1, replica_groups=mesh['role'=2,'gx_0'=4,'gx_1'=2,'gy_0'=4,'gy_1'=2] {'role'}, use_global_device_ids=true, to_apply=%region_3.4 | all-reduce | flops 2 | bytes 16 | tf_op jit(solution)/shard_map/psum | solution.py:35
  174.8 8.3 %all-reduce.16 = (f32[]{:T(128)}, f32[]{:T(128)}) all-reduce(f32[]{:T(128)} %get-tuple-element.12, f32[]{:T(128)} %get-tuple-element.13), channel_id=1, replica_groups=mesh['role'=2,'gx_0'=4,'gx_1'=2,'gy_0'=4,'gy_1'=2] {'gx_0'}, use_global_device_ids=true, to_apply=%region_4.5 | all-reduce | flops 2 | bytes 16 | tf_op jit(solution)/shard_map/psum | solution.py:35
  183.0 4.6 all-reduce.18
  187.7 7.8 %all-reduce.15 = (f32[]{:T(128)}, f32[]{:T(128)}) all-reduce(f32[]{:T(128)} %get-tuple-element.10, f32[]{:T(128)} %get-tuple-element.11), channel_id=1, replica_groups=mesh['role'=2,'gx_0'=4,'gx_1'=2,'gy_0'=4,'gy_1'=2] {'gy_0'}, use_global_device_ids=true, to_apply=%region_6.7 | all-reduce | flops 2 | bytes 16 | tf_op jit(solution)/shard_map/psum | solution.py:35
  195.5 9.0 %all-reduce.17 = (f32[]{:T(128)}, f32[]{:T(128)}) all-reduce(f32[]{:T(128)} %get-tuple-element.4, f32[]{:T(128)} %get-tuple-element.5), channel_id=1, replica_groups=mesh['role'=2,'gx_0'=4,'gx_1'=2,'gy_0'=4,'gy_1'=2] {'gy_1'}, use_global_device_ids=true, to_apply=%region_7.8 | all-reduce | flops 2 | bytes 16 | tf_op jit(solution)/shard_map/psum | solution.py:35
  209.4 5.9 %psum.220 = f32[]{:T(128)} all-reduce(f32[]{:T(128)} %fusion.97), channel_id=1, replica_groups=mesh['role'=2,'gx_0'=4,'gx_1'=2,'gy_0'=4,'gy_1'=2] {'role'}, use_global_device_ids=true, to_apply=%region_15.16 | all-reduce | flops 1 | bytes 8 | tf_op jit(solution)/shard_map/psum | solution.py:35
  215.3 6.9 %psum.221 = f32[]{:T(128)} all-reduce(f32[]{:T(128)} %psum.220), channel_id=1, replica_groups=mesh['role'=2,'gx_0'=4,'gx_1'=2,'gy_0'=4,'gy_1'=2] {'gx_0'}, use_global_device_ids=true, to_apply=%region_16.17 | all-reduce | flops 1 | bytes 8 | tf_op jit(solution)/shard_map/psum | solution.py:35
  222.2 4.7 psum.222
  226.9 6.6 %psum.223 = f32[]{:T(128)} all-reduce(f32[]{:T(128)} %psum.222), channel_id=1, replica_groups=mesh['role'=2,'gx_0'=4,'gx_1'=2,'gy_0'=4,'gy_1'=2] {'gy_0'}, use_global_device_ids=true, to_apply=%region_18.19 | all-reduce | flops 1 | bytes 8 | tf_op jit(solution)/shard_map/psum | solution.py:35
  233.5 9.3 %psum.224 = f32[]{:T(128)} all-reduce(f32[]{:T(128)} %psum.223), channel_id=1, replica_groups=mesh['role'=2,'gx_0'=4,'gx_1'=2,'gy_0'=4,'gy_1'=2] {'gy_1'}, use_global_device_ids=true, to_apply=%region_19.20 | all-reduce | flops 1 | bytes 8 | tf_op jit(solution)/shard_map/psum | solution.py:35
  244.1 3.5 slice_multiply_fusion.26
  249.2 4.9 slice.572
  254.1 5.7 slice.571
  259.7 5.7 slice.570
  265.4 4.4 fusion.39
  273.0 3.9 fusion.2
  276.9 3.3 reshape.257
  298.0 4.3 collective-permute-done.17
  309.2 3.7 collective-permute-done.19
  313.3 6.7 %collective-permute-start.20 = (f32[3,19,1,131]{3,2,1,0:T(1,128)S(1)}, f32[3,19,1,131]{3,2,1,0:T(1,128)S(1)}, u32[]{:S(2)}, u32[]{:S(2)}) collective-permute-start(f32[3,19,1,131]{3,2,1,0:T(1,128)S(1)} %get-tuple-element.28), channel_id=1, source_target_pairs={{0,1},{1,2},{2,3},{3,4},{4,5},{5,6},{6,7},{8,9},{9,10},{10,11},{11... | collective-permute-start | bytes 89612 | tf_op jit(solution)/shard_map/ppermute | solution.py:25
  322.2 3.4 collective-permute-done.21
  330.6 6.0 %psum.225 = f32[]{:T(128)} all-reduce(f32[]{:T(128)} %fusion.96), channel_id=1, replica_groups=mesh['role'=2,'gx_0'=4,'gx_1'=2,'gy_0'=4,'gy_1'=2] {'role'}, use_global_device_ids=true, to_apply=%region_21.22 | all-reduce | flops 1 | bytes 8 | tf_op jit(solution)/shard_map/psum | solution.py:35
  336.6 7.7 %psum.226 = f32[]{:T(128)} all-reduce(f32[]{:T(128)} %psum.225), channel_id=1, replica_groups=mesh['role'=2,'gx_0'=4,'gx_1'=2,'gy_0'=4,'gy_1'=2] {'gx_0'}, use_global_device_ids=true, to_apply=%region_22.23 | all-reduce | flops 1 | bytes 8 | tf_op jit(solution)/shard_map/psum | solution.py:35
  344.3 4.5 psum.227
  348.7 6.7 %psum.228 = f32[]{:T(128)} all-reduce(f32[]{:T(128)} %psum.227), channel_id=1, replica_groups=mesh['role'=2,'gx_0'=4,'gx_1'=2,'gy_0'=4,'gy_1'=2] {'gy_0'}, use_global_device_ids=true, to_apply=%region_24.25 | all-reduce | flops 1 | bytes 8 | tf_op jit(solution)/shard_map/psum | solution.py:35
  355.4 9.2 %psum.229 = f32[]{:T(128)} all-reduce(f32[]{:T(128)} %psum.228), channel_id=1, replica_groups=mesh['role'=2,'gx_0'=4,'gx_1'=2,'gy_0'=4,'gy_1'=2] {'gy_1'}, use_global_device_ids=true, to_apply=%region_25.26 | all-reduce | flops 1 | bytes 8 | tf_op jit(solution)/shard_map/psum | solution.py:35
  369.6 6.0 %psum.230 = f32[]{:T(128)} all-reduce(f32[]{:T(128)} %fusion.95), channel_id=1, replica_groups=mesh['role'=2,'gx_0'=4,'gx_1'=2,'gy_0'=4,'gy_1'=2] {'role'}, use_global_device_ids=true, to_apply=%region_27.28 | all-reduce | flops 1 | bytes 8 | tf_op jit(solution)/shard_map/psum | solution.py:35
  375.6 7.3 %psum.231 = f32[]{:T(128)} all-reduce(f32[]{:T(128)} %psum.230), channel_id=1, replica_groups=mesh['role'=2,'gx_0'=4,'gx_1'=2,'gy_0'=4,'gy_1'=2] {'gx_0'}, use_global_device_ids=true, to_apply=%region_28.29 | all-reduce | flops 1 | bytes 8 | tf_op jit(solution)/shard_map/psum | solution.py:35
  382.8 4.7 psum.232
  387.6 6.7 %psum.233 = f32[]{:T(128)} all-reduce(f32[]{:T(128)} %psum.232), channel_id=1, replica_groups=mesh['role'=2,'gx_0'=4,'gx_1'=2,'gy_0'=4,'gy_1'=2] {'gy_0'}, use_global_device_ids=true, to_apply=%region_30.31 | all-reduce | flops 1 | bytes 8 | tf_op jit(solution)/shard_map/psum | solution.py:35
  394.2 8.9 %psum.234 = f32[]{:T(128)} all-reduce(f32[]{:T(128)} %psum.233), channel_id=1, replica_groups=mesh['role'=2,'gx_0'=4,'gx_1'=2,'gy_0'=4,'gy_1'=2] {'gy_1'}, use_global_device_ids=true, to_apply=%region_31.32 | all-reduce | flops 1 | bytes 8 | tf_op jit(solution)/shard_map/psum | solution.py:35
  419.8 3.9 fusion.1
  436.9 4.3 collective-permute-done.23
  446.3 3.7 collective-permute-done.25
  450.4 6.7 %collective-permute-start.26 = (f32[3,19,1,131]{3,2,1,0:T(1,128)S(1)}, f32[3,19,1,131]{3,2,1,0:T(1,128)S(1)}, u32[]{:S(2)}, u32[]{:S(2)}) collective-permute-start(f32[3,19,1,131]{3,2,1,0:T(1,128)S(1)} %get-tuple-element.26), channel_id=1, source_target_pairs={{0,1},{1,2},{2,3},{3,4},{4,5},{5,6},{6,7},{8,9},{9,10},{10,11},{11... | collective-permute-start | bytes 89612 | tf_op jit(solution)/shard_map/ppermute | solution.py:25
  459.3 3.4 collective-permute-done.27
  466.6 5.9 %psum.235 = f32[]{:T(128)} all-reduce(f32[]{:T(128)} %fusion.94), channel_id=1, replica_groups=mesh['role'=2,'gx_0'=4,'gx_1'=2,'gy_0'=4,'gy_1'=2] {'role'}, use_global_device_ids=true, to_apply=%region_33.34 | all-reduce | flops 1 | bytes 8 | tf_op jit(solution)/shard_map/psum | solution.py:35
  472.5 6.7 %psum.236 = f32[]{:T(128)} all-reduce(f32[]{:T(128)} %psum.235), channel_id=1, replica_groups=mesh['role'=2,'gx_0'=4,'gx_1'=2,'gy_0'=4,'gy_1'=2] {'gx_0'}, use_global_device_ids=true, to_apply=%region_34.35 | all-reduce | flops 1 | bytes 8 | tf_op jit(solution)/shard_map/psum | solution.py:35
  479.3 4.4 psum.237
  483.7 6.6 %psum.238 = f32[]{:T(128)} all-reduce(f32[]{:T(128)} %psum.237), channel_id=1, replica_groups=mesh['role'=2,'gx_0'=4,'gx_1'=2,'gy_0'=4,'gy_1'=2] {'gy_0'}, use_global_device_ids=true, to_apply=%region_36.37 | all-reduce | flops 1 | bytes 8 | tf_op jit(solution)/shard_map/psum | solution.py:35
  490.3 8.7 %psum.239 = f32[]{:T(128)} all-reduce(f32[]{:T(128)} %psum.238), channel_id=1, replica_groups=mesh['role'=2,'gx_0'=4,'gx_1'=2,'gy_0'=4,'gy_1'=2] {'gy_1'}, use_global_device_ids=true, to_apply=%region_37.38 | all-reduce | flops 1 | bytes 8 | tf_op jit(solution)/shard_map/psum | solution.py:35
  515.1 3.3 fusion.41
  518.6 7.3 %all_to_all.21 = f32[8,1,512]{2,1,0:T(1,128)S(1)} all-to-all(f32[8,1,512]{2,1,0:T(1,128)S(1)} %reshape.286), channel_id=1, replica_groups=mesh['role'=2,'gx_0'=4,'gx_1'=2,'gy_0'=4,'gy_1'=2] {'gy_0','gy_1'}, dimensions={0} | all-to-all | bytes 32768 | tf_op jit(solution)/shard_map/all_to_all | solution.py:256
  529.5 5.0 mul.384
  538.3 9.2 %collective-permute-done.28 = f32[4,256,2]{2,1,0:T(8,128)S(1)} collective-permute-done((f32[4,256,2]{2,1,0:T(8,128)S(1)}, f32[4,256,2]{2,1,0:T(8,128)S(1)}, u32[]{:S(2)}, u32[]{:S(2)}) %collective-permute-start.28) | collective-permute-done | bytes 8224 | tf_op jit(solution)/shard_map/ppermute | solution.py:25
  547.5 5.3 collective-permute-done.29
  553.3 4.0 collective-permute-start.30
  563.5 4.4 collective-permute-done.31
  (275 shorter events, 199.8 us)
Async XLA Ops:
  0.6 110.8 %copy-start = (f32[81,81]{1,0:T(8,128)S(1)}, f32[81,81]{1,0:T(8,128)}, u32[]{:S(2)}) copy-start(f32[81,81]{1,0:T(8,128)} %param.7) | copy-start | bytes 78736
  0.6 12.3 %copy-start.20 = (s32[3,16,16,128]{3,2,1,0:T(8,128)S(1)}, s32[3,16,16,128]{3,2,1,0:T(8,128)}, u32[]{:S(2)}) copy-start(s32[3,16,16,128]{3,2,1,0:T(8,128)} %param.6) | copy-start | bytes 1179652
  0.7 12.3 %copy-start.19 = (f32[3,16,16,128]{3,2,1,0:T(8,128)S(1)}, f32[3,16,16,128]{3,2,1,0:T(8,128)}, u32[]{:S(2)}) copy-start(f32[3,16,16,128]{3,2,1,0:T(8,128)} %param.5) | copy-start | bytes 1179652
  0.7 17.1 %collective-permute-start.4 = (f32[6,17,17,1]{2,3,1,0:T(1,128)S(1)}, f32[6,17,17,1]{2,3,1,0:T(1,128)S(1)}, u32[]{:S(2)}, u32[]{:S(2)}) collective-permute-start(f32[6,17,17,1]{2,3,1,0:T(1,128)S(1)} %slice.514), channel_id=1, source_target_pairs={{0,64},{1,65},{2,66},{3,67},{4,68},{5,69},{6,70},{7,71},{8,72},{9,... | collective-permute-start | bytes 20816 | tf_op jit(solution)/shard_map/ppermute | solution.py:25
  9.6 26.5 %collective-permute-start = (f32[4,256,2]{2,1,0:T(8,128)}, f32[4,256,2]{2,1,0:T(8,128)}, u32[]{:S(2)}, u32[]{:S(2)}) collective-permute-start(f32[4,256,2]{2,1,0:T(8,128)} %get-tuple-element.92), channel_id=1, source_target_pairs={{0,64},{1,65},{2,66},{3,67},{4,68},{5,69},{6,70},{7,71},{8,72},{9,... | collective-permute-start | bytes 24584 | tf_op jit(solution)/shard_map/ppermute | solution.py:25
  11.7 24.4 %collective-permute-start.1 = (f32[4,256,2]{2,1,0:T(8,128)}, f32[4,256,2]{2,1,0:T(8,128)}, u32[]{:S(2)}, u32[]{:S(2)}) collective-permute-start(f32[4,256,2]{2,1,0:T(8,128)} %get-tuple-element.93), channel_id=1, source_target_pairs={{64,0},{65,1},{66,2},{67,3},{68,4},{69,5},{70,6},{71,7},{72,8},{73... | collective-permute-start | bytes 24584 | tf_op jit(solution)/shard_map/ppermute | solution.py:28
  16.3 12.7 %collective-permute-start.5 = (f32[6,17,17,1]{2,3,1,0:T(1,128)S(1)}, f32[6,17,17,1]{2,3,1,0:T(1,128)S(1)}, u32[]{:S(2)}, u32[]{:S(2)}) collective-permute-start(f32[6,17,17,1]{2,3,1,0:T(1,128)S(1)} %copy.52), channel_id=1, source_target_pairs={{64,0},{65,1},{66,2},{67,3},{68,4},{69,5},{70,6},{71,7},{72,8},{73... | collective-permute-start | bytes 20816 | tf_op jit(solution)/shard_map/ppermute | solution.py:28
  30.7 5.4 copy-start.13
  32.0 9.0 %copy-start.1 = (f32[6,17,17,1]{3,2,1,0:T(8,128)S(1)}, f32[6,17,17,1]{3,2,1,0:T(8,128)}, u32[]{:S(2)}) copy-start(f32[6,17,17,1]{3,2,1,0:T(8,128)} %copy.53) | copy-start | bytes 20812
  32.0 9.0 %copy-start.2 = (f32[6,17,17,1]{3,2,1,0:T(8,128)S(1)}, f32[6,17,17,1]{3,2,1,0:T(8,128)}, u32[]{:S(2)}) copy-start(f32[6,17,17,1]{3,2,1,0:T(8,128)} %copy.54) | copy-start | bytes 20812
  32.0 5.8 %collective-permute-start.6 = (f32[6,1,17,131]{3,2,1,0:T(8,128)S(1)}, f32[6,1,17,131]{3,2,1,0:T(8,128)S(1)}, u32[]{:S(2)}, u32[]{:S(2)}) collective-permute-start(f32[6,1,17,131]{3,2,1,0:T(8,128)S(1)} %get-tuple-element.24), channel_id=1, source_target_pairs={{0,8},{8,16},{16,24},{24,32},{32,40},{40,48},{48,56},{1,9},{9,17},... | collective-permute-start | bytes 160352 | tf_op jit(solution)/shard_map/ppermute | solution.py:25
  34.8 6.2 %collective-permute-start.7 = (f32[6,1,17,131]{3,2,1,0:T(8,128)S(1)}, f32[6,1,17,131]{3,2,1,0:T(8,128)S(1)}, u32[]{:S(2)}, u32[]{:S(2)}) collective-permute-start(f32[6,1,17,131]{3,2,1,0:T(8,128)S(1)} %get-tuple-element.25), channel_id=1, source_target_pairs={{8,0},{16,8},{24,16},{32,24},{40,32},{48,40},{56,48},{9,1},{17,9},... | collective-permute-start | bytes 160352 | tf_op jit(solution)/shard_map/ppermute | solution.py:28
  41.7 14.9 %collective-permute-start.8 = (f32[6,19,1,131]{3,2,1,0:T(1,128)S(1)}, f32[6,19,1,131]{3,2,1,0:T(1,128)S(1)}, u32[]{:S(2)}, u32[]{:S(2)}) collective-permute-start(f32[6,19,1,131]{3,2,1,0:T(1,128)S(1)} %get-tuple-element.22), channel_id=1, source_target_pairs={{0,1},{1,2},{2,3},{3,4},{4,5},{5,6},{6,7},{8,9},{9,10},{10,11},{11... | collective-permute-start | bytes 179216 | tf_op jit(solution)/shard_map/ppermute | solution.py:25
  47.6 9.0 %collective-permute-start.9 = (f32[6,19,1,131]{3,2,1,0:T(1,128)S(1)}, f32[6,19,1,131]{3,2,1,0:T(1,128)S(1)}, u32[]{:S(2)}, u32[]{:S(2)}) collective-permute-start(f32[6,19,1,131]{3,2,1,0:T(1,128)S(1)} %get-tuple-element.23), channel_id=1, source_target_pairs={{1,0},{2,1},{3,2},{4,3},{5,4},{6,5},{7,6},{9,8},{10,9},{11,10},{12... | collective-permute-start | bytes 179216 | tf_op jit(solution)/shard_map/ppermute | solution.py:28
  50.6 30.3 %collective-permute-start.2 = (f32[2,256,132]{2,1,0:T(8,128)}, f32[2,256,132]{2,1,0:T(8,128)}, u32[]{:S(2)}, u32[]{:S(2)}) collective-permute-start(f32[2,256,132]{2,1,0:T(8,128)} %get-tuple-element.88), channel_id=1, source_target_pairs={{0,1},{1,2},{2,3},{3,4},{4,5},{5,6},{6,7},{7,8},{8,9},{9,10},{10,1... | collective-permute-start | bytes 811016 | tf_op jit(solution)/shard_map/ppermute | solution.py:25
  54.3 26.7 %collective-permute-start.3 = (f32[2,256,132]{2,1,0:T(8,128)}, f32[2,256,132]{2,1,0:T(8,128)}, u32[]{:S(2)}, u32[]{:S(2)}) collective-permute-start(f32[2,256,132]{2,1,0:T(8,128)} %get-tuple-element.89), channel_id=1, source_target_pairs={{1,0},{2,1},{3,2},{4,3},{5,4},{6,5},{7,6},{8,7},{9,8},{10,9},{11,1... | collective-permute-start | bytes 811016 | tf_op jit(solution)/shard_map/ppermute | solution.py:28
  91.5 10.2 %copy-start.17 = (f32[3,3,8,8,129]{4,3,2,1,0:T(8,128)S(1)}, f32[3,3,8,8,129]{4,3,2,1,0:T(8,128)}, u32[]{:S(2)}) copy-start(f32[3,3,8,8,129]{4,3,2,1,0:T(8,128)} %slice.538) | copy-start | bytes 891652
  96.6 12.7 %all-to-all-start = ((f32[8,1,512]{2,1,0:T(1,128)}), f32[8,1,512]{2,1,0:T(1,128)S(1)}, u32[]{:S(2)}, u32[]{:S(2)}) async-start(f32[8,1,512]{2,1,0:T(1,128)} %reshape.284), calls=%async_computation | async-start | bytes 32768 | tf_op jit(solution)/shard_map/all_to_all | solution.py:224
  128.5 1.0 copy-start.3
  132.0 3.5 collective-permute-start.10
  134.1 6.1 %collective-permute-start.11 = (f32[3,17,17,1]{2,3,1,0:T(1,128)S(1)}, f32[3,17,17,1]{2,3,1,0:T(1,128)S(1)}, u32[]{:S(2)}, u32[]{:S(2)}) collective-permute-start(f32[3,17,17,1]{2,3,1,0:T(1,128)S(1)} %copy.64), channel_id=1, source_target_pairs={{64,0},{65,1},{66,2},{67,3},{68,4},{69,5},{70,6},{71,7},{72,8},{73... | collective-permute-start | bytes 10412 | tf_op jit(solution)/shard_map/ppermute | solution.py:28
  141.5 10.4 %copy-start.4 = (f32[3,8,2,17,129]{4,3,2,1,0:T(8,128)S(1)}, f32[3,8,2,17,129]{4,3,2,1,0:T(8,128)}, u32[]{:S(2)}) copy-start(f32[3,8,2,17,129]{4,3,2,1,0:T(8,128)} %copy-done.3) | copy-start | bytes 1263172
  141.5 10.4 %copy-start.10 = (f32[3,17,17,1]{3,2,1,0:T(8,128)S(1)}, f32[3,17,17,1]{3,2,1,0:T(8,128)}, u32[]{:S(2)}) copy-start(f32[3,17,17,1]{3,2,1,0:T(8,128)} %copy.66) | copy-start | bytes 10408
  142.6 5.5 collective-permute-start.12
  146.7 5.1 collective-permute-start.13
  152.2 8.1 %collective-permute-start.14 = (f32[3,19,1,131]{3,2,1,0:T(1,128)S(1)}, f32[3,19,1,131]{3,2,1,0:T(1,128)S(1)}, u32[]{:S(2)}, u32[]{:S(2)}) collective-permute-start(f32[3,19,1,131]{3,2,1,0:T(1,128)S(1)} %get-tuple-element.30), channel_id=1, source_target_pairs={{0,1},{1,2},{2,3},{3,4},{4,5},{5,6},{6,7},{8,9},{9,10},{10,11},{11... | collective-permute-start | bytes 89612 | tf_op jit(solution)/shard_map/ppermute | solution.py:25
  158.3 5.5 collective-permute-start.15
  166.0 1.1 copy-start.15
  207.7 1.0 copy-start.9
  290.2 1.1 copy-start.5
  293.6 3.9 collective-permute-start.16
  296.2 6.1 %collective-permute-start.17 = (f32[3,17,17,1]{2,3,1,0:T(1,128)S(1)}, f32[3,17,17,1]{2,3,1,0:T(1,128)S(1)}, u32[]{:S(2)}, u32[]{:S(2)}) collective-permute-start(f32[3,17,17,1]{2,3,1,0:T(1,128)S(1)} %copy.76), channel_id=1, source_target_pairs={{64,0},{65,1},{66,2},{67,3},{68,4},{69,5},{70,6},{71,7},{72,8},{73... | collective-permute-start | bytes 10412 | tf_op jit(solution)/shard_map/ppermute | solution.py:28
  303.6 9.4 %copy-start.6 = (f32[3,8,2,17,129]{4,3,2,1,0:T(8,128)S(1)}, f32[3,8,2,17,129]{4,3,2,1,0:T(8,128)}, u32[]{:S(2)}) copy-start(f32[3,8,2,17,129]{4,3,2,1,0:T(8,128)} %copy-done.5) | copy-start | bytes 1263172
  303.6 9.4 %copy-start.11 = (f32[3,17,17,1]{3,2,1,0:T(8,128)S(1)}, f32[3,17,17,1]{3,2,1,0:T(8,128)}, u32[]{:S(2)}) copy-start(f32[3,17,17,1]{3,2,1,0:T(8,128)} %copy.78) | copy-start | bytes 10408
  304.8 4.5 collective-permute-start.18
  307.8 5.1 collective-permute-start.19
  313.3 8.8 %collective-permute-start.20 = (f32[3,19,1,131]{3,2,1,0:T(1,128)S(1)}, f32[3,19,1,131]{3,2,1,0:T(1,128)S(1)}, u32[]{:S(2)}, u32[]{:S(2)}) collective-permute-start(f32[3,19,1,131]{3,2,1,0:T(1,128)S(1)} %get-tuple-element.28), channel_id=1, source_target_pairs={{0,1},{1,2},{2,3},{3,4},{4,5},{5,6},{6,7},{8,9},{9,10},{10,11},{11... | collective-permute-start | bytes 89612 | tf_op jit(solution)/shard_map/ppermute | solution.py:25
  320.1 5.5 collective-permute-start.21
  327.7 1.1 copy-start.16
  367.8 1.1 copy-start.14
  432.5 3.9 collective-permute-start.22
  435.1 6.1 %collective-permute-start.23 = (f32[3,17,17,1]{2,3,1,0:T(1,128)S(1)}, f32[3,17,17,1]{2,3,1,0:T(1,128)S(1)}, u32[]{:S(2)}, u32[]{:S(2)}) collective-permute-start(f32[3,17,17,1]{2,3,1,0:T(1,128)S(1)} %copy.88), channel_id=1, source_target_pairs={{64,0},{65,1},{66,2},{67,3},{68,4},{69,5},{70,6},{71,7},{72,8},{73... | collective-permute-start | bytes 10412 | tf_op jit(solution)/shard_map/ppermute | solution.py:28
  441.8 4.5 collective-permute-start.24
  444.9 5.1 collective-permute-start.25
  450.4 8.9 %collective-permute-start.26 = (f32[3,19,1,131]{3,2,1,0:T(1,128)S(1)}, f32[3,19,1,131]{3,2,1,0:T(1,128)S(1)}, u32[]{:S(2)}, u32[]{:S(2)}) collective-permute-start(f32[3,19,1,131]{3,2,1,0:T(1,128)S(1)} %get-tuple-element.26), channel_id=1, source_target_pairs={{0,1},{1,2},{2,3},{3,4},{4,5},{5,6},{6,7},{8,9},{9,10},{10,11},{11... | collective-permute-start | bytes 89612 | tf_op jit(solution)/shard_map/ppermute | solution.py:25
  457.1 5.5 collective-permute-start.27
  463.8 36.5 %copy-start.7 = (f32[3,17,17,129]{3,2,1,0:T(8,128)S(1)}, f32[3,17,17,129]{3,2,1,0:T(8,128)}, u32[]{:S(2)}) copy-start(f32[3,17,17,129]{3,2,1,0:T(8,128)} %get-tuple-element.21) | copy-start | bytes 1342120
  463.8 36.5 %copy-start.8 = (f32[3,17,17,129]{3,2,1,0:T(8,128)S(1)}, f32[3,17,17,129]{3,2,1,0:T(8,128)}, u32[]{:S(2)}) copy-start(f32[3,17,17,129]{3,2,1,0:T(8,128)} %get-tuple-element.17) | copy-start | bytes 1342120
  501.9 1.0 copy-start.12
  529.5 5.1 copy-start.18
  535.0 12.5 %collective-permute-start.28 = (f32[4,256,2]{2,1,0:T(8,128)S(1)}, f32[4,256,2]{2,1,0:T(8,128)S(1)}, u32[]{:S(2)}, u32[]{:S(2)}) collective-permute-start(f32[4,256,2]{2,1,0:T(8,128)S(1)} %get-tuple-element.90), channel_id=1, source_target_pairs={{0,64},{1,65},{2,66},{3,67},{4,68},{5,69},{6,70},{7,71},{8,72},{9,... | collective-permute-start | bytes 24584 | tf_op jit(solution)/shard_map/ppermute | solution.py:25
  537.0 15.8 %collective-permute-start.29 = (f32[4,256,2]{2,1,0:T(8,128)S(1)}, f32[4,256,2]{2,1,0:T(8,128)S(1)}, u32[]{:S(2)}, u32[]{:S(2)}) collective-permute-start(f32[4,256,2]{2,1,0:T(8,128)S(1)} %get-tuple-element.91), channel_id=1, source_target_pairs={{64,0},{65,1},{66,2},{67,3},{68,4},{69,5},{70,6},{71,7},{72,8},{73... | collective-permute-start | bytes 24584 | tf_op jit(solution)/shard_map/ppermute | solution.py:28
  553.3 10.1 %collective-permute-start.30 = (f32[2,256,132]{2,1,0:T(8,128)S(1)}, f32[2,256,132]{2,1,0:T(8,128)S(1)}, u32[]{:S(2)}, u32[]{:S(2)}) collective-permute-start(f32[2,256,132]{2,1,0:T(8,128)S(1)} %get-tuple-element.86), channel_id=1, source_target_pairs={{0,1},{1,2},{2,3},{3,4},{4,5},{5,6},{6,7},{7,8},{8,9},{9,10},{10,1... | collective-permute-start | bytes 811016 | tf_op jit(solution)/shard_map/ppermute | solution.py:25
  557.3 10.5 %collective-permute-start.31 = (f32[2,256,132]{2,1,0:T(8,128)S(1)}, f32[2,256,132]{2,1,0:T(8,128)S(1)}, u32[]{:S(2)}, u32[]{:S(2)}) collective-permute-start(f32[2,256,132]{2,1,0:T(8,128)S(1)} %get-tuple-element.87), channel_id=1, source_target_pairs={{1,0},{2,1},{3,2},{4,3},{5,4},{6,5},{7,6},{8,7},{9,8},{10,9},{11,1... | collective-permute-start | bytes 811016 | tf_op jit(solution)/shard_map/ppermute | solution.py:28
where the time goes:
time: 581 us; the launch traced here: 571 us
  blocking collectives  176 us (30%)
  local copies, waits for them, and re-layouts  131 us (23%)
  starting transfers between devices  93.2 us (16%)
  waiting for transfers between devices  68.7 us (12%)
  other arithmetic  52.8 us (9%)
  matrix products  40.7 us (7%)
  between operations  8.97 us (2%)
    psum x25, blocking collectives, over_axes(): shard = lax.psum(shard, axis)  169 us
    ppermute x16, starting transfers between devices, with_halo(): lax.ppermute(lax.slice_in_dim(block, block.shape[dim] - width, None, axis...  62.8 us
    ppermute x16, waiting for transfers between devices, with_halo(): lax.ppermute(lax.slice_in_dim(block, 0, width, axis=dim), axis, backward)  56.8 us
    slice x12, local copies, waits for them, and re-layouts, split_axis(): lax.slice_in_dim(values, corner, corner + 2 * half_len - 1, stride=2, axi...  47.5 us
    ppermute x16, starting transfers between devices, with_halo(): lax.ppermute(lax.slice_in_dim(block, 0, width, axis=dim), axis, backward)  25.2 us
    dot_general x4, matrix products, split_nodes(): jnp.einsum('baqxyk,ckg->cbaqxyg', stacked, table, precision=lax.Precision...  14.6 us
    unnamed x54, local copies, waits for them, and re-layouts  12.2 us
    ppermute x16, waiting for transfers between devices, with_halo(): lax.ppermute(lax.slice_in_dim(block, block.shape[dim] - width, None, axis...  11.9 us
  transfers between devices with their start and end apart: 33, of which 18 were waited for; matrix products, arithmetic and copies ran while one was open for 9% of the time, Pallas kernels for 0%

commit v1 on v0

v1 whole, which is shorter than its diff:
```python
import jax
import jax.numpy as jnp
import numpy as np
from jax import lax
from jax.experimental import pallas as pl
from jax.experimental.pallas import tpu as pltpu
from jax.sharding import PartitionSpec as P

ITERS = 3
RADIUS = 2
GX_GY = ("gx", "gy")


sharpness = 4.0
threshold = 0.5
floor_stiff = 0.001


def with_halo(block, sides, width):
    for axis, dim in sides:
        count = lax.axis_size(axis)
        forward = [(i, i + 1) for i in range(count - 1)]
        backward = [(target, source) for source, target in forward]
        low = lax.ppermute(
            lax.slice_in_dim(block, block.shape[dim] - width, None, axis=dim), axis, forward
        )
        high = lax.ppermute(lax.slice_in_dim(block, 0, width, axis=dim), axis, backward)
        block = jnp.concatenate([low, block, high], axis=dim)
    return block


def hat_list():
    return [float(RADIUS + 1 - abs(shift_idx - RADIUS)) for shift_idx in range(2 * RADIUS + 1)]


def smooth_axis(padded, axis_num, length):
    result = None
    for offset_idx, weight in enumerate(hat_list()):
        portion = weight * lax.slice_in_dim(padded, offset_idx, offset_idx + length, axis=axis_num)
        result = portion if result is None else result + portion
    return result


def axis_count(start, length, extent):
    places = start + jnp.arange(length, dtype=jnp.int32)
    counted = jnp.zeros((length,), jnp.float32)
    for offset_idx, weight in enumerate(hat_list()):
        target = places + (offset_idx - RADIUS)
        inside = jnp.logical_and(target >= 0, target < extent)
        counted = counted + weight * inside.astype(jnp.float32)
    return counted


def slab_weight(shape):
    extent_x, extent_y, extent_z = shape
    along_x = axis_count(
        lax.axis_index(GX_GY) * extent_x, extent_x, extent_x * lax.axis_size(GX_GY)
    )
    along_y = axis_count(0, extent_y, extent_y)
    along_z = axis_count(
        lax.axis_index("role") * extent_z, extent_z, extent_z * lax.axis_size("role")
    )
    return along_x[:, None, None] * along_y[None, :, None] * along_z[None, None, :]


def slab_smooth(field):
    extent_x, extent_y, extent_z = field.shape
    padded = with_halo(field, (("role", 2), (GX_GY, 0)), RADIUS)
    padded = jnp.pad(padded, ((0, 0), (RADIUS, RADIUS), (0, 0)))
    return smooth_axis(smooth_axis(smooth_axis(padded, 2, extent_z), 1, extent_y), 0, extent_x)


def heaviside_projection(values):
    scaled = jnp.tanh(sharpness * threshold) + jnp.tanh(sharpness * (1.0 - threshold))
    return (jnp.tanh(sharpness * threshold) + jnp.tanh(sharpness * (values - threshold))) / scaled


def slope(values):
    scaled = jnp.tanh(sharpness * threshold) + jnp.tanh(sharpness * (1.0 - threshold))
    bent = jnp.tanh(sharpness * (values - threshold))
    return sharpness * (1.0 - bent * bent) / scaled


def element_mean(fine):
    count_x = fine.shape[0] // 4
    count_y = fine.shape[1] // 4
    count_z = fine.shape[2] // 2
    return fine.reshape(count_x, 4, count_y, 4, count_z, 2).mean(axis=(1, 3, 5))


def spread(elements):
    count_x, count_y, count_z = elements.shape
    widened = jnp.broadcast_to(
        elements[:, None, :, None, :, None], (count_x, 4, count_y, 4, count_z, 2)
    )
    return widened.reshape(4 * count_x, 4 * count_y, 2 * count_z)


MESH = pl.DeviceIdType.MESH
VMEM = pl.BlockSpec(memory_space=pltpu.VMEM)
ANY = pl.BlockSpec(memory_space=pl.ANY)
F32 = jnp.float32
ROWS = 112
LANES = 128
GXN = 8
YN = 16
CHUNKS = (
    (0, 0, 0), (0, 0, 1), (0, 0, 2), (0, 0, 3), (0, 0, 4), (0, 0, 5),
    (1, 0, 0), (1, 0, 1), (1, 0, 4),
    (0, 1, 0), (0, 1, 2), (0, 1, 6),
    (1, 1, 0), (1, 1, 4),
)
PAIRS = {4: ((0, 0), (0, 1)), 5: ((1, 0), (1, 1)), 6: ((0, 0), (1, 0))}


def row_table():
    table = np.zeros((ROWS, 81), np.float32)
    seen = set()
    for place, (dx, dy, kind) in enumerate(CHUNKS):
        for half in range(2):
            if kind < 4:
                px, py, c = kind // 2, kind % 2, half
            else:
                (px, py), c = PAIRS[kind][half], 2
            if (dx and px) or (dy and py):
                continue
            a, b = px + 2 * dx, py + 2 * dy
            for q in range(3):
                index = ((c * 3 + b) * 3 + a) * 3 + q
                assert index not in seen
                seen.add(index)
                table[place * 8 + half * 4 + q, index] = 1.0
    assert len(seen) == 81
    return table


def place_of():
    role, gx, gy = lax.axis_index("role"), lax.axis_index("gx"), lax.axis_index("gy")
    return role, gx, gy, 2 * gy + role


def device_at(gx, row):
    gx = lax.rem(gx + GXN, GXN)
    row = lax.rem(row + YN, YN)
    return {"role": lax.rem(row, 2), "gx": gx, "gy": lax.div(row, 2)}


def greet(devices):
    barrier = pltpu.get_barrier_semaphore()
    for device in devices:
        pl.semaphore_signal(barrier, inc=1, device_id=device, device_id_type=MESH)
    pl.semaphore_wait(barrier, len(devices))


def remote(src, dst, send, recv, device):
    return pltpu.make_async_remote_copy(
        src_ref=src, dst_ref=dst, send_sem=send, recv_sem=recv, device_id=device, device_id_type=MESH
    )


def params(ident=None):
    if ident is None:
        return pltpu.CompilerParams(vmem_limit_bytes=48 * 1024 * 1024)
    return pltpu.CompilerParams(collective_id=ident, has_side_effects=True, vmem_limit_bytes=32 * 1024 * 1024)


def parity_matrix(role, natural_own):
    rows = lax.broadcasted_iota(jnp.int32, (256, 256), 0)
    cols = lax.broadcasted_iota(jnp.int32, (256, 256), 1)
    half = jnp.where(rows < LANES, role, 1 - role)
    spot = half * LANES + lax.rem(rows, LANES)
    want = 2 * lax.rem(cols, LANES) + lax.div(cols, LANES)
    return (spot == want).astype(F32)


def pack_kernel(force_ref, free_ref, out_ref):
    role = lax.axis_index("role")
    matrix = parity_matrix(role, True)
    upper = lax.broadcasted_iota(jnp.int32, (8, LANES), 0) < 4

    def body(e, _):
        for px in range(2):
            x = 2 * e + px
            both = []
            for ref, precision in ((force_ref, lax.Precision.HIGHEST), (free_ref, None)):
                wide = jnp.dot(
                    ref[x].reshape(64, 256), matrix, precision=precision, preferred_element_type=F32
                )
                both.append(wide)
            for f in range(4):
                for py in range(2):
                    y = 2 * f + py
                    vals = [
                        jnp.where(upper, w[8 * y : 8 * y + 8, :LANES], w[8 * y : 8 * y + 8, LANES:])
                        for w in both
                    ]
                    out_ref[0, e, f, px, py] = vals[0] * vals[1]
                    out_ref[1, e, f, px, py] = vals[1]
        return 0

    lax.fori_loop(0, 8, body, 0)


def start_exchange_kernel(vf_ref, dens_ref, xhi_ref, yhi_ref, corner_ref, dall_ref, send, recv, own):
    role, gx, gy, row = place_of()
    group = [device_at(gx, row + k) for k in range(1, YN)]
    greet(
        group
        + [device_at(gx + 1, row), device_at(gx - 1, row), device_at(gx + 1, row + 1), device_at(gx - 1, row - 1)]
    )
    copies = []
    for k in range(1, YN):
        target = lax.rem(row + k, YN)
        copies.append(
            remote(dens_ref.at[target], dall_ref.at[row], send.at[k], recv.at[k], group[k - 1])
        )
    copies.append(remote(vf_ref.at[:, 0, :, 0], xhi_ref, send.at[16], recv.at[16], device_at(gx - 1, row)))
    copies.append(remote(vf_ref.at[:, :, 0, :, 0], yhi_ref, send.at[17], recv.at[17], device_at(gx, row - 1)))
    copies.append(
        remote(vf_ref.at[:, 0, 0, 0, 0], corner_ref, send.at[18], recv.at[18], device_at(gx - 1, row - 1))
    )
    for copy in copies:
        copy.start()
    mine = pltpu.make_async_copy(dens_ref.at[row], dall_ref.at[row], own)
    mine.start()
    mine.wait()
    for copy in copies:
        copy.wait()


def start_exchange(vf, dens):
    return pl.pallas_call(
        start_exchange_kernel,
        out_shape=(
            jax.ShapeDtypeStruct((2, 4, 2, 8, LANES), F32),
            jax.ShapeDtypeStruct((2, 8, 2, 8, LANES), F32),
            jax.ShapeDtypeStruct((2, 8, LANES), F32),
            jax.ShapeDtypeStruct((YN, 8, LANES), F32),
        ),
        in_specs=[ANY, ANY],
        out_specs=(ANY,) * 4,
        scratch_shapes=[pltpu.SemaphoreType.DMA((19,)), pltpu.SemaphoreType.DMA((19,)), pltpu.SemaphoreType.DMA],
        compiler_params=params(1),
        name="start_exchange",
    )(vf, dens)


def reduce_parts(tile_ref, slots, second, total, send, recv, gx, row, base):
    slots[row] = tile_ref[...]
    copies = []
    for k in range(1, YN):
        copies.append(
            remote(tile_ref, slots.at[row], send.at[base + k], recv.at[base + k], device_at(gx, row + k))
        )
    for copy in copies:
        copy.start()
    for copy in copies:
        copy.wait()
    part = slots[0]
    for k in range(1, YN):
        part = part + slots[k]
    total[...] = part
    second[gx] = part
    base = base + YN
    copies = []
    for k in range(1, GXN):
        copies.append(
            remote(total, second.at[gx], send.at[base + k], recv.at[base + k], device_at(gx + k, row))
        )
    for copy in copies:
        copy.start()
    for copy in copies:
        copy.wait()
    part = second[0]
    for k in range(1, GXN):
        part = part + second[k]
    return part


def face_moves():
    return (
        (1, 0), (-1, 0), (0, 1), (0, -1), (1, 1), (1, -1), (-1, 1), (-1, -1),
    )


def face_exchange_kernel(
    image_ref, tile_ref, xlo, xhi, ylo, yhi, corners, sum_ref, slots, second, total, send, recv
):
    role, gx, gy, row = place_of()
    greet(
        [device_at(gx, row + k) for k in range(1, YN)]
        + [device_at(gx + k, row) for k in range(1, GXN)]
        + [device_at(gx + dx, row + dy) for dx, dy in face_moves()[4:]]
    )
    ends = (
        (image_ref.at[8, :, 0], xlo),
        (image_ref.at[0, :, 0], xhi),
        (image_ref.at[:, 4, :, 0], ylo),
        (image_ref.at[:, 0, :, 0], yhi),
        (image_ref.at[8, 4, 0, 0], corners.at[0]),
        (image_ref.at[8, 0, 0, 0], corners.at[1]),
        (image_ref.at[0, 4, 0, 0], corners.at[2]),
        (image_ref.at[0, 0, 0, 0], corners.at[3]),
    )
    copies = []
    for k, ((dx, dy), (src, dst)) in enumerate(zip(face_moves(), ends)):
        copies.append(remote(src, dst, send.at[k], recv.at[k], device_at(gx + dx, row + dy)))
    for copy in copies:
        copy.start()
    sum_ref[...] = reduce_parts(tile_ref, slots, second, total, send, recv, gx, row, 8)
    for copy in copies:
        copy.wait()


REDUCE_SCRATCH = [
    pltpu.VMEM((YN, 8, LANES), F32),
    pltpu.VMEM((GXN, 8, LANES), F32),
    pltpu.VMEM((8, LANES), F32),
]


def face_exchange(image, tile, ident):
    return pl.pallas_call(
        face_exchange_kernel,
        out_shape=(
            jax.ShapeDtypeStruct((5, 2, 8, LANES), F32),
            jax.ShapeDtypeStruct((5, 2, 8, LANES), F32),
            jax.ShapeDtypeStruct((9, 2, 8, LANES), F32),
            jax.ShapeDtypeStruct((9, 2, 8, LANES), F32),
            jax.ShapeDtypeStruct((4, 8, LANES), F32),
            jax.ShapeDtypeStruct((8, LANES), F32),
        ),
        in_specs=[ANY, VMEM],
        out_specs=(ANY,) * 5 + (VMEM,),
        scratch_shapes=REDUCE_SCRATCH
        + [pltpu.SemaphoreType.DMA((32,)), pltpu.SemaphoreType.DMA((32,))],
        compiler_params=params(ident),
        name="face_exchange",
    )(image, tile)


def reduce_kernel(tile_ref, sum_ref, slots, second, total, send, recv):
    role, gx, gy, row = place_of()
    greet(
        [device_at(gx, row + k) for k in range(1, YN)] + [device_at(gx + k, row) for k in range(1, GXN)]
    )
    sum_ref[...] = reduce_parts(tile_ref, slots, second, total, send, recv, gx, row, 0)


def reduce_all(tile, ident):
    return pl.pallas_call(
        reduce_kernel,
        out_shape=jax.ShapeDtypeStruct((8, LANES), F32),
        in_specs=[VMEM],
        out_specs=VMEM,
        scratch_shapes=REDUCE_SCRATCH
        + [pltpu.SemaphoreType.DMA((24,)), pltpu.SemaphoreType.DMA((24,))],
        compiler_params=params(ident),
        name="reduce_all",
    )(tile)


def gradient_exchange_kernel(grad_ref, all_ref, send, recv, own):
    role, gx, gy, row = place_of()
    greet([device_at(gx, row + k) for k in range(1, YN)])
    copies = []
    for k in range(1, YN):
        target = lax.rem(row + k, YN)
        copies.append(
            remote(
                grad_ref.at[lax.div(target, 2)], all_ref.at[row], send.at[k], recv.at[k], device_at(gx, row + k)
            )
        )
    for copy in copies:
        copy.start()
    mine = pltpu.make_async_copy(grad_ref.at[gy], all_ref.at[row], own)
    mine.start()
    mine.wait()
    for copy in copies:
        copy.wait()


def gradient_exchange(grad):
    return pl.pallas_call(
        gradient_exchange_kernel,
        out_shape=jax.ShapeDtypeStruct((YN, 8, LANES), F32),
        in_specs=[ANY],
        out_specs=ANY,
        scratch_shapes=[pltpu.SemaphoreType.DMA((16,)), pltpu.SemaphoreType.DMA((16,)), pltpu.SemaphoreType.DMA],
        compiler_params=params(5),
        name="gradient_exchange",
    )(grad)


def matrix_pieces(table_ref):
    whole = table_ref[...]
    high = whole.astype(jnp.bfloat16)
    low = (whole - high.astype(F32)).astype(jnp.bfloat16)
    return jnp.concatenate(
        [
            jnp.concatenate([high, high], axis=1),
            jnp.concatenate([low, jnp.zeros_like(low)], axis=1),
        ],
        axis=0,
    )


def build_store(field, store):
    sub = lax.broadcasted_iota(jnp.int32, (8, LANES), 0) < 4
    inside = lax.broadcasted_iota(jnp.int32, (8, LANES), 1) < LANES - 1

    def body(e, _):
        for f in range(5):
            held = [field[e, f, k // 2, k % 2] for k in range(4)]
            shifted = [jnp.where(inside, pltpu.roll(v, LANES - 1, 1), 0.0) for v in held]
            turned = [None] + [pltpu.roll(v, 4, 0) for v in shifted[1:]]
            for k in range(4):
                store[e, f, k] = held[k]
            store[e, f, 4] = jnp.where(sub, shifted[0], turned[1])
            store[e, f, 5] = jnp.where(sub, shifted[2], turned[3])
            store[e, f, 6] = jnp.where(sub, shifted[0], turned[2])
        return 0

    lax.fori_loop(0, 9, body, 0)


def element_product(store, pieces, e):
    columns = []
    for f in range(4):
        columns.append(jnp.concatenate([store[e + dx, f + dy, kind] for dx, dy, kind in CHUNKS], axis=0))
    wide = jnp.concatenate(columns, axis=1)
    high = wide.astype(jnp.bfloat16)
    low = (wide - high.astype(F32)).astype(jnp.bfloat16)
    out = jnp.dot(pieces, jnp.concatenate([high, low], axis=0), preferred_element_type=F32)
    product = out[:ROWS] + out[ROWS:]
    return columns, [product[:, f * LANES : (f + 1) * LANES] for f in range(4)]


def chunk_sum(left, right):
    both = left * right
    total = both[:8]
    for k in range(1, len(CHUNKS)):
        total = total + both[8 * k : 8 * k + 8]
    return total


def density_rows(dall_ref, e):
    return dall_ref[2 * e] + dall_ref[2 * e + 1]


def apply_operator(store, acc, pieces, dall_ref, image_ref):
    acc[...] = jnp.zeros_like(acc)

    def body(e, energy):
        columns, products = element_product(store, pieces, e)
        rho = density_rows(dall_ref, e)
        factor = floor_stiff + (1.0 - floor_stiff) * rho * rho * rho
        for f in range(4):
            scaled = products[f] * factor[f : f + 1, :]
            energy = energy + chunk_sum(columns[f], scaled)
            for place, (dx, dy, kind) in enumerate(CHUNKS):
                acc[e + dx, f + dy, kind] += scaled[8 * place : 8 * place + 8]
        return energy

    energy = lax.fori_loop(0, 8, body, jnp.zeros((8, LANES), F32))
    sub = lax.broadcasted_iota(jnp.int32, (8, LANES), 0) < 4
    inside = lax.broadcasted_iota(jnp.int32, (8, LANES), 1) > 0

    def fold(e, _):
        for f in range(5):
            z0, z1, z2 = acc[e, f, 4], acc[e, f, 5], acc[e, f, 6]
            t0, t1, t2 = (pltpu.roll(v, 4, 0) for v in (z0, z1, z2))
            for k, extra in enumerate((z0 + z2, t0, z1 + t2, t1)):
                extra = jnp.where(jnp.logical_and(sub, inside), pltpu.roll(extra, 1, 1), 0.0)
                image_ref[e, f, k // 2, k % 2] = acc[e, f, k] + extra
        return 0

    lax.fori_loop(0, 9, fold, 0)
    return energy


def element_energy(store, pieces, dall_ref):
    def body(e, energy):
        columns, products = element_product(store, pieces, e)
        rho = density_rows(dall_ref, e)
        factor = floor_stiff + (1.0 - floor_stiff) * rho * rho * rho
        for f in range(4):
            energy = energy + chunk_sum(columns[f], products[f] * factor[f : f + 1, :])
        return energy

    return lax.fori_loop(0, 8, body, jnp.zeros((8, LANES), F32))


def square_sum(field):
    def body(e, total):
        for f in range(4):
            for k in range(4):
                held = field[e, f, k // 2, k % 2]
                total = total + held * held
        return total

    return lax.fori_loop(0, 8, body, jnp.zeros((8, LANES), F32))


def sums_tile(gamma, delta):
    rows = lax.broadcasted_iota(jnp.int32, (8, LANES), 0)
    gamma = jnp.sum(gamma, axis=0, keepdims=True)
    delta = jnp.sum(delta, axis=0, keepdims=True)
    return jnp.where(rows == 0, gamma, jnp.where(rows == 1, delta, 0.0))


def read_sums(sum_ref):
    return (
        jnp.sum(sum_ref[0:1, :], axis=1, keepdims=True),
        jnp.sum(sum_ref[1:2, :], axis=1, keepdims=True),
    )


def first_kernel(vf_ref, xhi, yhi, corner, dall_ref, table_ref, r_ref, free_ref, image_ref, tile_ref, store, acc):
    role, gx, gy, row = place_of()
    has_x, has_y = gx < GXN - 1, row < YN - 1
    has_both = jnp.logical_and(has_x, has_y)
    empty = jnp.zeros((8, LANES), F32)
    for kind, ref in ((0, r_ref), (1, free_ref)):
        ref[8] = jnp.zeros((5, 2, 2, 8, LANES), F32)
        for e in range(8):
            ref[e, 0:4] = vf_ref[kind, e]
            for px in range(2):
                ref[e, 4, px, 0] = jnp.where(has_y, yhi[kind, e, px], 0.0)
                ref[e, 4, px, 1] = empty
        for f in range(4):
            for py in range(2):
                ref[8, f, 0, py] = jnp.where(has_x, xhi[kind, f, py], 0.0)
        ref[8, 4, 0, 0] = jnp.where(has_both, corner[kind], 0.0)
    build_store(r_ref, store)
    delta = apply_operator(store, acc, matrix_pieces(table_ref), dall_ref, image_ref)
    tile_ref[...] = sums_tile(square_sum(r_ref), delta)


def field_struct():
    return jax.ShapeDtypeStruct((9, 5, 2, 2, 8, LANES), F32)


def tile_struct():
    return jax.ShapeDtypeStruct((8, LANES), F32)


STORES = [pltpu.VMEM((9, 5, 7, 8, LANES), F32), pltpu.VMEM((9, 5, 7, 8, LANES), F32)]


def first_step(vf, xhi, yhi, corner, dall, table):
    return pl.pallas_call(
        first_kernel,
        out_shape=(field_struct(), field_struct(), field_struct(), tile_struct()),
        in_specs=[VMEM] * 6,
        out_specs=(VMEM,) * 4,
        scratch_shapes=STORES,
        compiler_params=params(),
        name="first_step",
    )(vf, xhi, yhi, corner, dall, table)


def add_faces(image_ref, work, free_ref, xlo, xhi, ylo, yhi, corners):
    role, gx, gy, row = place_of()
    low_x, low_y = gx > 0, row > 0
    work[...] = image_ref[...]
    for f in range(5):
        for p in range(2):
            work[0, f, 0, p] += jnp.where(low_x, xlo[f, p], 0.0)
            work[8, f, 0, p] += xhi[f, p]
    for e in range(9):
        for p in range(2):
            work[e, 0, p, 0] += jnp.where(low_y, ylo[e, p], 0.0)
            work[e, 4, p, 0] += yhi[e, p]
    work[0, 0, 0, 0] += jnp.where(jnp.logical_and(low_x, low_y), corners[0], 0.0)
    work[0, 4, 0, 0] += jnp.where(low_x, corners[1], 0.0)
    work[8, 0, 0, 0] += jnp.where(low_y, corners[2], 0.0)
    work[8, 4, 0, 0] += corners[3]
    work[...] = work[...] * free_ref[...]


def second_kernel(
    r_in, free_ref, image_in, xlo, xhi, ylo, yhi, corners, sum_ref, dall_ref, table_ref,
    s_ref, r_ref, image_ref, tile_ref, store, acc,
):
    add_faces(image_in, s_ref, free_ref, xlo, xhi, ylo, yhi, corners)
    gamma, delta = read_sums(sum_ref)
    alpha = gamma / delta
    r_ref[...] = r_in[...] - alpha.reshape(1, 1, 1, 1, 1, 1) * s_ref[...]
    build_store(r_ref, store)
    out = apply_operator(store, acc, matrix_pieces(table_ref), dall_ref, image_ref)
    tile_ref[...] = sums_tile(square_sum(r_ref), out)


def second_step(r, free, image, faces, total, dall, table):
    return pl.pallas_call(
        second_kernel,
        out_shape=(field_struct(), field_struct(), field_struct(), tile_struct()),
        in_specs=[VMEM] * 11,
        out_specs=(VMEM,) * 4,
        scratch_shapes=STORES,
        compiler_params=params(),
        name="second_step",
    )(r, free, image, *faces, total, dall, table)


def third_kernel(
    r0, r1, s0, free_ref, image_in, xlo, xhi, ylo, yhi, corners, sum0, sum1, dall_ref, table_ref,
    p_ref, u_ref, r_ref, tile_ref, work, store,
):
    add_faces(image_in, work, free_ref, xlo, xhi, ylo, yhi, corners)
    gamma0, delta0 = read_sums(sum0)
    gamma1, delta1 = read_sums(sum1)
    alpha0 = gamma0 / delta0
    beta1 = gamma1 / gamma0
    alpha1 = gamma1 / (delta1 - beta1 * gamma1 / alpha0)
    alpha0, alpha1, beta1 = (v.reshape(1, 1, 1, 1, 1, 1) for v in (alpha0, alpha1, beta1))
    p_ref[...] = r1[...] + beta1 * r0[...]
    u_ref[...] = alpha0 * r0[...] + alpha1 * p_ref[...]
    r_ref[...] = r1[...] - alpha1 * (work[...] + beta1 * s0[...])
    build_store(r_ref, store)
    delta = element_energy(store, matrix_pieces(table_ref), dall_ref)
    tile_ref[...] = sums_tile(square_sum(r_ref), delta)


def third_step(r0, r1, s0, free, image, faces, total0, total1, dall, table):
    return pl.pallas_call(
        third_kernel,
        out_shape=(field_struct(), field_struct(), field_struct(), tile_struct()),
        in_specs=[VMEM] * 14,
        out_specs=(VMEM,) * 4,
        scratch_shapes=[pltpu.VMEM((9, 5, 2, 2, 8, LANES), F32), STORES[0]],
        compiler_params=params(),
        name="third_step",
    )(r0, r1, s0, free, image, *faces, total0, total1, dall, table)


def last_kernel(p1, u1, r2, sum0, sum1, sum2, dall_ref, table_ref, grad_ref, nodes_ref, work, store):
    gamma0, delta0 = read_sums(sum0)
    gamma1, delta1 = read_sums(sum1)
    gamma2, delta2 = read_sums(sum2)
    alpha0 = gamma0 / delta0
    beta1 = gamma1 / gamma0
    alpha1 = gamma1 / (delta1 - beta1 * gamma1 / alpha0)
    beta2 = gamma2 / gamma1
    alpha2 = gamma2 / (delta2 - beta2 * gamma2 / alpha1)
    alpha2, beta2 = (v.reshape(1, 1, 1, 1, 1, 1) for v in (alpha2, beta2))
    work[...] = u1[...] + alpha2 * (r2[...] + beta2 * p1[...])
    build_store(work, store)
    pieces = matrix_pieces(table_ref)
    rows = lax.broadcasted_iota(jnp.int32, (8, LANES), 0)

    def body(e, _):
        columns, products = element_product(store, pieces, e)
        rho = density_rows(dall_ref, e)
        energy = jnp.zeros((8, LANES), F32)
        for f in range(4):
            one = jnp.sum(chunk_sum(columns[f], products[f]), axis=0, keepdims=True)
            energy = jnp.where(rows == f, one, energy)
        grad_ref[e] = -3.0 * rho * rho * (1.0 - floor_stiff) * energy / 32.0
        return 0

    lax.fori_loop(0, 8, body, 0)
    role = lax.axis_index("role")
    matrix = parity_matrix(role, True)

    def unpack(e, _):
        for px in range(2):
            held = jnp.concatenate(
                [work[e, f, px, py] for f in range(4) for py in range(2)], axis=0
            )
            even = lax.dot_general(
                held, matrix[:, :LANES], (((1,), (1,)), ((), ())),
                precision=lax.Precision.HIGHEST, preferred_element_type=F32,
            )
            odd = lax.dot_general(
                held, matrix[:, LANES:], (((1,), (1,)), ((), ())),
                precision=lax.Precision.HIGHEST, preferred_element_type=F32,
            )
            for y in range(8):
                nodes_ref[2 * e + px, y] = (
                    even[8 * y : 8 * y + 8] + pltpu.roll(odd[8 * y : 8 * y + 8], 4, 0)
                )
        return 0

    lax.fori_loop(0, 8, unpack, 0)


def last_step(p1, u1, r2, total0, total1, total2, dall, table):
    return pl.pallas_call(
        last_kernel,
        out_shape=(
            jax.ShapeDtypeStruct((8, 8, LANES), F32),
            jax.ShapeDtypeStruct((16, 8, 8, 256), F32),
        ),
        in_specs=[VMEM] * 8,
        out_specs=(VMEM,) * 2,
        scratch_shapes=[pltpu.VMEM((9, 5, 2, 2, 8, LANES), F32), STORES[0]],
        compiler_params=params(),
        name="last_step",
    )(p1, u1, r2, total0, total1, total2, dall, table)


def role_swap(values):
    return lax.ppermute(values, "role", [(0, 1), (1, 0)])


def nodal_rows(own, other):
    both = jnp.concatenate([own, other], axis=3)
    both = jnp.pad(jnp.transpose(both, (1, 2, 0, 3)), ((0, 0), (0, 0), (0, 1), (0, 0)))
    return jnp.concatenate([both, both], axis=2)


def halves(block, role):
    first, second = block[:, :, :8], block[:, :, 8:]
    keep = jnp.where(role == 0, first, second)
    give = jnp.where(role == 0, second, first)
    return keep, give


def on_device(design, force, clamped_dof_mask, stiffness):
    role = lax.axis_index("role")
    free = (1 - clamped_dof_mask).astype(F32)
    force_keep, force_give = halves(force, role)
    free_keep, free_give = halves(free, role)
    force_other, free_other = role_swap(force_give), role_swap(free_give)

    filter_weight_grid = slab_weight(design.shape)
    filtered = slab_smooth(design) / filter_weight_grid
    density_slab = element_mean(heaviside_projection(filtered)).reshape(16, 4, 64)
    empty = jnp.zeros_like(density_slab)
    density_slab = jnp.where(
        role == 0,
        jnp.concatenate([density_slab, empty], axis=2),
        jnp.concatenate([empty, density_slab], axis=2),
    )
    density_slab = jnp.pad(density_slab, ((0, 0), (0, 4), (0, 0)))

    chosen = jnp.asarray(row_table())
    table = jnp.dot(
        jnp.dot(chosen, stiffness, precision=lax.Precision.HIGHEST), chosen.T, precision=lax.Precision.HIGHEST
    )
    nodal = pl.pallas_call(
        pack_kernel,
        out_shape=jax.ShapeDtypeStruct((2, 8, 4, 2, 2, 8, LANES), F32),
        in_specs=[VMEM] * 2,
        out_specs=VMEM,
        compiler_params=params(),
        name="pack",
    )(nodal_rows(force_keep, force_other), nodal_rows(free_keep, free_other))
    xhi, yhi, corner, dall = start_exchange(nodal, density_slab)
    r0, free, image, tile = first_step(nodal, xhi, yhi, corner, dall, table)
    *faces, total0 = face_exchange(image, tile, 2)
    s0, r1, image, tile = second_step(r0, free, image, faces, total0, dall, table)
    *faces, total1 = face_exchange(image, tile, 3)
    p1, u1, r2, tile = third_step(r0, r1, s0, free, image, faces, total0, total1, dall, table)
    total2 = reduce_all(tile, 4)
    grad, nodes = last_step(p1, u1, r2, total0, total1, total2, dall, table)
    nodes = jnp.transpose(nodes[:, :, :3], (2, 0, 1, 3))
    mine, theirs = nodes[..., :LANES], role_swap(nodes[..., LANES:])
    displacement = jnp.where(
        role == 0,
        jnp.concatenate([mine, theirs], axis=2),
        jnp.concatenate([theirs, mine], axis=2),
    )
    slab_grad = gradient_exchange(grad)[:, :4]
    slab_grad = jnp.where(role == 0, slab_grad[..., :64], slab_grad[..., 64:]).reshape(1, 64, 64)
    voxel_grad = spread(slab_grad) * slope(filtered)
    sensitivity = slab_smooth(voxel_grad / filter_weight_grid)
    return (sensitivity, displacement)


def solution(mesh):
    return jax.shard_map(
        on_device,
        mesh=mesh,
        in_specs=(P(GX_GY, None, "role"), P(None, "gx", "gy", "role"), P(None, "gx", "gy", "role"), P()),
        out_specs=(P(GX_GY, None, "role"), P(None, "gx", "gy", "role")),
        check_vma=False,
    )
```

time: 581 us -> 196 us (0.34); the launches traced: 571 us -> 194 us
  blocking collectives: 176 us -> 0 us
  local copies, waits for them, and re-layouts: 131 us -> 16.4 us
  Pallas kernels: 0 us -> 93.2 us
  starting transfers between devices: 93.2 us -> 34 us
  matrix products: 40.7 us -> 1.37 us
  other arithmetic: 52.8 us -> 14.9 us
  waiting for transfers between devices: 68.7 us -> 32.9 us
  between operations: 8.97 us -> 1.07 us
    psum x25 -> x0, blocking collectives: 169 us -> none  [over_axes(): shard = lax.psum(shard, axis)]
    pallas_call x0 -> x10, Pallas kernels: none -> 93.2 us  [the longest x2 34 us: face_exchange(): pl.pallas_call(face_exchange_kernel, out_shape=(jax.ShapeDtypeStruct((5,...]
    slice x32 -> x2, local copies, waits for them, and re-layouts: 54.9 us -> 1.24 us  [the longest x1 1.11 us: halves(): first, second = (block[:, :, :8], block[:, :, 8:])]
    ppermute x16 -> x4, waiting for transfers between devices: 56.8 us -> 12.3 us  [with_halo(): lax.ppermute(lax.slice_in_dim(block, 0, width, axis=dim), axis, backward)]
    ppermute x16 -> x4, starting transfers between devices: 62.8 us -> 19.2 us  [with_halo(): lax.ppermute(lax.slice_in_dim(block, block.shape[dim] - width, None, axis...]
    dot_general x15 -> x2, matrix products: 40.7 us -> 1.37 us  [the longest x1 1.09 us: on_device(): jnp.dot(jnp.dot(chosen, stiffness, precision=lax.Precision.HIGHEST), chos...]
    reshape x11 -> x0, local copies, waits for them, and re-layouts: 19.8 us -> none  [the longest x4 10.5 us: split_nodes(): return stacked.reshape(81, -1)]
    ppermute x16 -> x4, starting transfers between devices: 25.2 us -> 6.61 us  [with_halo(): lax.ppermute(lax.slice_in_dim(block, 0, width, axis=dim), axis, backward)]
  transfers between devices with their start and end apart: 33 -> 11, of which waited for: 18 -> 7; matrix products, arithmetic and copies ran while one was open for 9% -> 5% of each run, Pallas kernels for 0% -> 2%
where the time goes in v1:
time: 196 us; the launch traced here: 194 us
  Pallas kernels  93.2 us (48%)
  starting transfers between devices  34 us (17%)
  waiting for transfers between devices  32.9 us (17%)
  local copies, waits for them, and re-layouts  16.4 us (8%)
  other arithmetic  14.9 us (8%)
    pallas_call x2, Pallas kernels, face_exchange(): pl.pallas_call(face_exchange_kernel, out_shape=(jax.ShapeDtypeStruct((5,...  34 us
    ppermute x4, waiting for transfers between devices, with_halo(): lax.ppermute(lax.slice_in_dim(block, block.shape[dim] - width, None, axis...  20.7 us
    ppermute x4, starting transfers between devices, with_halo(): lax.ppermute(lax.slice_in_dim(block, block.shape[dim] - width, None, axis...  19.2 us
    pallas_call x1, Pallas kernels, start_exchange(): pl.pallas_call(start_exchange_kernel, out_shape=(jax.ShapeDtypeStruct((2,...  12.9 us
    pallas_call x1, Pallas kernels, reduce_all(): pl.pallas_call(reduce_kernel, out_shape=jax.ShapeDtypeStruct((8, LANES),...  12.6 us
    ppermute x4, waiting for transfers between devices, with_halo(): lax.ppermute(lax.slice_in_dim(block, 0, width, axis=dim), axis, backward)  12.3 us
    pallas_call x1, Pallas kernels, gradient_exchange(): pl.pallas_call(gradient_exchange_kernel, out_shape=jax.ShapeDtypeStruct((...  9.12 us
    pallas_call x1, Pallas kernels, last_step(): pl.pallas_call(last_kernel, out_shape=(jax.ShapeDtypeStruct((8, 8, LANES)...  8.36 us
  transfers between devices with their start and end apart: 11, of which 7 were waited for; matrix products, arithmetic and copies ran while one was open for 5% of the time, Pallas kernels for 2%

profile of v1, /device:TPU:1, one launch (start us, length us, event | category | flops | bytes accessed | tf_op | source)
XLA Modules:
  0.0 194.0 jit_solution(429525663933862998)
XLA Ops:
  0.7 1.1 fusion.42
  1.8 0.3 copy_select_fusion.1
  2.1 4.5 %collective-permute-start.4 = (f32[3,16,8,128]{3,0,2,1:T(4,128)S(1)}, f32[3,16,8,128]{3,0,2,1:T(4,128)}, u32[]{:S(2)}, u32[]{:S(2)}) collective-permute-start(f32[3,16,8,128]{3,0,2,1:T(4,128)S(1)} %get-tuple-element.83), channel_id=1, source_target_pairs={{0,64},{64,0},{1,65},{65,1},{2,66},{66,2},{3,67},{67,3},{4,68},{68... | collective-permute-start | bytes 589832 | tf_op jit(solution)/shard_map/ppermute | solution.py:705
  6.6 1.3 fusion.22
  7.9 0.8 slice_select_fusion.1
  8.7 0.2 fusion.41
  8.9 4.9 %collective-permute-start = (f32[4,256,2]{2,1,0:T(8,128)S(1)}, f32[4,256,2]{2,1,0:T(8,128)S(1)}, u32[]{:S(2)}, u32[]{:S(2)}) collective-permute-start(f32[4,256,2]{2,1,0:T(8,128)S(1)} %get-tuple-element.80), channel_id=1, source_target_pairs={{0,64},{1,65},{2,66},{3,67},{4,68},{5,69},{6,70},{7,71},{8,72},{9,... | collective-permute-start | bytes 24584 | tf_op jit(solution)/shard_map/ppermute | solution.py:24
  13.8 1.3 collective-permute-start.1
  15.1 0.3 fusion.43
  15.4 1.1 fusion.44.table_ref
  16.6 11.8 %collective-permute-done = f32[4,256,2]{2,1,0:T(8,128)S(1)} collective-permute-done((f32[4,256,2]{2,1,0:T(8,128)S(1)}, f32[4,256,2]{2,1,0:T(8,128)S(1)}, u32[]{:S(2)}, u32[]{:S(2)}) %collective-permute-start) | collective-permute-done | bytes 8224 | tf_op jit(solution)/shard_map/ppermute | solution.py:24
  28.4 0.7 collective-permute-done.1
  29.1 0.5 pad_maximum_fusion
  29.6 0.1 fusion.38
  29.6 5.4 %collective-permute-start.2 = (f32[2,256,132]{2,1,0:T(8,128)S(1)}, f32[2,256,132]{2,1,0:T(8,128)S(1)}, u32[]{:S(2)}, u32[]{:S(2)}) collective-permute-start(f32[2,256,132]{2,1,0:T(8,128)S(1)} %get-tuple-element.72), channel_id=1, source_target_pairs={{0,1},{1,2},{2,3},{3,4},{4,5},{5,6},{6,7},{7,8},{8,9},{9,10},{10,1... | collective-permute-start | bytes 811016 | tf_op jit(solution)/shard_map/ppermute | solution.py:24
  35.1 2.1 %collective-permute-start.3 = (f32[2,256,132]{2,1,0:T(8,128)S(1)}, f32[2,256,132]{2,1,0:T(8,128)S(1)}, u32[]{:S(2)}, u32[]{:S(2)}) collective-permute-start(f32[2,256,132]{2,1,0:T(8,128)S(1)} %get-tuple-element.73), channel_id=1, source_target_pairs={{1,0},{2,1},{3,2},{4,3},{5,4},{6,5},{7,6},{8,7},{9,8},{10,9},{11,1... | collective-permute-start | bytes 811016 | tf_op jit(solution)/shard_map/ppermute | solution.py:27
  37.2 1.1 maximum_bitcast_fusion
  38.3 0.1 pad.21
  38.4 1.1 maximum_bitcast_fusion.1
  39.5 0.1 pad.22
  39.6 0.4 pad_maximum_fusion.1
  40.0 3.7 %pack.1.vf_ref = f32[2,8,4,2,2,8,128]{6,5,4,3,2,1,0:T(8,128)S(1)} custom-call(f32[16,8,8,256]{3,2,1,0:T(8,128)S(1)} %get-tuple-element.86.force_ref, f32[16,8,8,256]{3,2,1,0:T(8,128)S(1)} %get-tuple-element.87.free_ref), custom_call_target="tpu_custom_call" | custom-call | tf_op jit(solution)/shard_map/pack/pallas_call | solution.py:743
  43.7 1.9 collective-permute-done.3
  45.6 0.5 select_maximum_fusion.4
  46.1 1.2 slice_add_fusion.1
  47.3 0.5 slice_add_fusion.3
  47.8 0.3 multiply_reduce_fusion
  48.1 0.1 copy.20
  48.2 5.6 %reduce_sum.14 = f32[64,4,64,2]{1,0,3,2:T(8,128)} reshape(f32[256,128]{0,1:T(8,128)S(1)} %copy.20) | data formatting | bytes 262144 | tf_op jit(solution)/shard_map/reduce_sum | solution.py:88
  53.9 2.8 %reduce_sum.18 = f32[64,64]{0,1:T(8,128)S(1)} reduce(f32[64,4,64,2]{1,0,3,2:T(8,128)} %reduce_sum.14, f32[]{:T(128)} %constant.25.clone.1), dimensions={1,3}, to_apply=%region_1.2 | reduce | flops 28672 | bytes 147460 | tf_op jit(solution)/shard_map/reduce_sum | solution.py:88
  56.8 0.1 pad_select_fusion
  56.9 12.9 %start_exchange.1 = (f32[2,4,2,8,128]{4,3,2,1,0:T(8,128)S(1)}, f32[2,8,2,8,128]{4,3,2,1,0:T(8,128)S(1)}, f32[2,8,128]{2,1,0:T(8,128)S(1)}, f32[16,8,128]{2,1,0:T(8,128)S(1)}) custom-call(f32[2,8,4,2,2,8,128]{6,5,4,3,2,1,0:T(8,128)S(1)} %pack.1.vf_ref, f32[16,8,128]{2,1,0:T(8,128)S(1)} %pad.23.dens_ref), custom_call_target="tpu_custom_call" | custom-call | tf_op jit(solution)/shard_map/start_exchange/pallas_call | solution.py:232
  69.9 3.8 %first_step.1 = (f32[9,5,2,2,8,128]{5,4,3,2,1,0:T(8,128)S(1)}, f32[9,5,2,2,8,128]{5,4,3,2,1,0:T(8,128)S(1)}, f32[9,5,2,2,8,128]{5,4,3,2,1,0:T(8,128)S(1)}, f32[8,128]{1,0:T(8,128)S(1)}) custom-call(f32[2,8,4,2,2,8,128]{6,5,4,3,2,1,0:T(8,128)S(1)} %pack.1.vf_ref, f32[2,4,2,8,128]{4,3,2,1,0:T(8,128)S(1)} %get-tuple-element.32.xhi, ...), custom_call_target="tpu_custom_call" | custom-call | tf_op jit(solution)/shard_map/first_step/pallas_call | solution.py:552
  73.7 18.5 %face_exchange.2 = (f32[5,2,8,128]{3,2,1,0:T(8,128)S(1)}, f32[5,2,8,128]{3,2,1,0:T(8,128)S(1)}, f32[9,2,8,128]{3,2,1,0:T(8,128)S(1)}, f32[9,2,8,128]{3,2,1,0:T(8...) custom-call(f32[9,5,2,2,8,128]{5,4,3,2,1,0:T(8,128)S(1)} %get-tuple-element.38.image_ref.image_in, ...), custom_call_target="tpu_custom_call" | custom-call | tf_op jit(solution)/shard_map/face_exchange/pallas_call | solution.py:323
  92.2 3.9 %second_step.1 = (f32[9,5,2,2,8,128]{5,4,3,2,1,0:T(8,128)S(1)}, f32[9,5,2,2,8,128]{5,4,3,2,1,0:T(8,128)S(1)}, f32[9,5,2,2,8,128]{5,4,3,2,1,0:T(8,128)S(1)}, f32[8,128]{1,0:T(8,128)S(1)}) custom-call(f32[9,5,2,2,8,128]{5,4,3,2,1,0:T(8,128)S(1)} %get-tuple-element.36.r_in.r0, f32[9,5,2,2,8,128]{5,4,3,2,1,0:T(8,128)S(1)} %get-tuple-element.37.free_ref, ...), custom_call_target="tpu_custom_call" | custom-call | tf_op jit(solution)/shard_map/second_step/pallas_call | solution.py:596
  96.2 15.4 %face_exchange.3 = (f32[5,2,8,128]{3,2,1,0:T(8,128)S(1)}, f32[5,2,8,128]{3,2,1,0:T(8,128)S(1)}, f32[9,2,8,128]{3,2,1,0:T(8,128)S(1)}, f32[9,2,8,128]{3,2,1,0:T(8...) custom-call(f32[9,5,2,2,8,128]{5,4,3,2,1,0:T(8,128)S(1)} %get-tuple-element.48.image_ref.image_in, ...), custom_call_target="tpu_custom_call" | custom-call | tf_op jit(solution)/shard_map/face_exchange/pallas_call | solution.py:323
  111.6 4.6 %third_step.1 = (f32[9,5,2,2,8,128]{5,4,3,2,1,0:T(8,128)S(1)}, f32[9,5,2,2,8,128]{5,4,3,2,1,0:T(8,128)S(1)}, f32[9,5,2,2,8,128]{5,4,3,2,1,0:T(8,128)S(1)}, f32[8,128]{1,0:T(8,128)S(1)}) custom-call(f32[9,5,2,2,8,128]{5,4,3,2,1,0:T(8,128)S(1)} %get-tuple-element.36.r_in.r0, f32[9,5,2,2,8,128]{5,4,3,2,1,0:T(8,128)S(1)} %get-tuple-element.46.r1, ...), custom_call_target="tpu_custom_call" | custom-call | tf_op jit(solution)/shard_map/third_step/pallas_call | solution.py:627
  116.3 12.6 %reduce_all.1.sum2 = f32[8,128]{1,0:T(8,128)S(1)} custom-call(f32[8,128]{1,0:T(8,128)S(1)} %get-tuple-element.59.tile_ref), custom_call_target="tpu_custom_call" | custom-call | tf_op jit(solution)/shard_map/reduce_all/pallas_call | solution.py:351
  128.9 8.4 %last_step.1 = (f32[8,8,128]{2,1,0:T(8,128)S(1)}, f32[16,8,8,256]{3,2,1,0:T(8,128)S(1)}) custom-call(f32[9,5,2,2,8,128]{5,4,3,2,1,0:T(8,128)S(1)} %get-tuple-element.56.p1, f32[9,5,2,2,8,128]{5,4,3,2,1,0:T(8,128)S(1)} %get-tuple-element.57.u1, f32[9,5,2,2,8,128]{5,4,3,2,1,0:T(8,128)S(1)} %get-tuple-element.58.r2, ...), custom_call_target="tpu_custom_call" | custom-call | tf_op jit(solution)/shard_map/last_step/pallas_call | solution.py:690
  137.3 9.1 %gradient_exchange.1 = f32[16,8,128]{2,1,0:T(8,128)S(1)} custom-call(f32[8,8,128]{2,1,0:T(8,128)S(1)} %get-tuple-element.60.grad_ref), custom_call_target="tpu_custom_call" | custom-call | tf_op jit(solution)/shard_map/gradient_exchange/pallas_call | solution.py:384
  146.6 0.1 slice_bitcast_fusion
  146.7 2.5 %broadcast_in_dim.2 = f32[64,4,64,2]{1,0,3,2:T(8,128)} broadcast(f32[64,64]{0,1:T(8,128)S(1)} %copy.22), dimensions={0,2} | broadcast | bytes 147456 | tf_op jit(solution)/shard_map/broadcast_in_dim | solution.py:93
  149.2 4.9 %mul.182 = f32[256,128]{0,1:T(8,128)S(1)} reshape(f32[64,4,64,2]{1,0,3,2:T(8,128)} %broadcast_in_dim.2) | data formatting | bytes 262144 | tf_op jit(solution)/shard_map/mul | solution.py:768
  154.1 0.1 copy.23
  154.2 0.2 multiply_divide_fusion
  154.5 0.2 fusion.40
  154.7 4.1 %collective-permute-start.6 = (f32[4,256,2]{2,1,0:T(8,128)S(1)}, f32[4,256,2]{2,1,0:T(8,128)S(1)}, u32[]{:S(2)}, u32[]{:S(2)}) collective-permute-start(f32[4,256,2]{2,1,0:T(8,128)S(1)} %get-tuple-element.76), channel_id=1, source_target_pairs={{0,64},{1,65},{2,66},{3,67},{4,68},{5,69},{6,70},{7,71},{8,72},{9,... | collective-permute-start | bytes 24584 | tf_op jit(solution)/shard_map/ppermute | solution.py:24
  158.8 1.3 collective-permute-start.7
  160.1 0.1 fusion.39
  160.3 3.7 %collective-permute-start.10 = (f32[3,16,8,128]{3,0,2,1:T(4,128)S(1)}, f32[3,16,8,128]{3,0,2,1:T(4,128)S(1)}, u32[]{:S(2)}, u32[]{:S(2)}) collective-permute-start(f32[3,16,8,128]{3,0,2,1:T(4,128)S(1)} %get-tuple-element.75), channel_id=1, source_target_pairs={{0,64},{64,0},{1,65},{65,1},{2,66},{66,2},{3,67},{67,3},{4,68},{68... | collective-permute-start | bytes 589832 | tf_op jit(solution)/shard_map/ppermute | solution.py:705
  163.9 5.7 %collective-permute-done.6 = f32[4,256,2]{2,1,0:T(8,128)S(1)} collective-permute-done((f32[4,256,2]{2,1,0:T(8,128)S(1)}, f32[4,256,2]{2,1,0:T(8,128)S(1)}, u32[]{:S(2)}, u32[]{:S(2)}) %collective-permute-start.6) | collective-permute-done | bytes 8224 | tf_op jit(solution)/shard_map/ppermute | solution.py:24
  169.7 5.3 %collective-permute-done.7 = f32[4,256,2]{2,1,0:T(8,128)S(1)} collective-permute-done((f32[4,256,2]{2,1,0:T(8,128)S(1)}, f32[4,256,2]{2,1,0:T(8,128)S(1)}, u32[]{:S(2)}, u32[]{:S(2)}) %collective-permute-start.7) | collective-permute-done | bytes 8224 | tf_op jit(solution)/shard_map/ppermute | solution.py:27
  175.0 0.5 pad_maximum_fusion.3
  175.5 0.1 fusion.37
  175.6 4.7 %collective-permute-start.8 = (f32[2,256,132]{2,1,0:T(8,128)S(1)}, f32[2,256,132]{2,1,0:T(8,128)S(1)}, u32[]{:S(2)}, u32[]{:S(2)}) collective-permute-start(f32[2,256,132]{2,1,0:T(8,128)S(1)} %get-tuple-element.70), channel_id=1, source_target_pairs={{0,1},{1,2},{2,3},{3,4},{4,5},{5,6},{6,7},{7,8},{8,9},{9,10},{10,1... | collective-permute-start | bytes 811016 | tf_op jit(solution)/shard_map/ppermute | solution.py:24
  180.3 1.9 collective-permute-start.9
  182.2 0.2 maximum_select_fusion
  182.5 0.8 copy.24
  183.2 3.2 %collective-permute-done.8 = f32[2,256,132]{2,1,0:T(8,128)S(1)} collective-permute-done((f32[2,256,132]{2,1,0:T(8,128)S(1)}, f32[2,256,132]{2,1,0:T(8,128)S(1)}, u32[]{:S(2)}, u32[]{:S(2)}) %collective-permute-start.8) | collective-permute-done | bytes 270368 | tf_op jit(solution)/shard_map/ppermute | solution.py:24
  186.4 4.4 %collective-permute-done.9 = f32[2,256,132]{2,1,0:T(8,128)S(1)} collective-permute-done((f32[2,256,132]{2,1,0:T(8,128)S(1)}, f32[2,256,132]{2,1,0:T(8,128)S(1)}, u32[]{:S(2)}, u32[]{:S(2)}) %collective-permute-start.9) | collective-permute-done | bytes 270368 | tf_op jit(solution)/shard_map/ppermute | solution.py:27
  190.8 0.5 select_maximum_fusion
  191.3 1.2 slice_add_fusion
  192.5 0.5 slice_add_fusion.2
  193.0 0.9 slice_add_fusion.4
  (22 shorter events, 0.4 us)
Async XLA Ops:
  0.6 14.5 %copy-start = (f32[81,81]{1,0:T(8,128)S(1)}, f32[81,81]{1,0:T(8,128)}, u32[]{:S(2)}) copy-start(f32[81,81]{1,0:T(8,128)} %param.8) | copy-start | bytes 78736
  0.6 8.0 %copy-start.2 = (f32[4,256,128]{2,1,0:T(8,128)S(1)}, f32[4,256,128]{2,1,0:T(8,128)}, u32[]{:S(2)}) copy-start(f32[4,256,128]{2,1,0:T(8,128)} %param.5) | copy-start | bytes 1572868
  2.1 13.1 %copy-start.3 = (f32[112,81]{1,0:T(8,128)S(1)}, f32[112,81]{1,0:T(8,128)}, u32[]{:S(2)}) copy-start(f32[112,81]{1,0:T(8,128)} %constant.47.clone) | copy-start | bytes 108868
  2.1 35.1 %collective-permute-start.4 = (f32[3,16,8,128]{3,0,2,1:T(4,128)S(1)}, f32[3,16,8,128]{3,0,2,1:T(4,128)}, u32[]{:S(2)}, u32[]{:S(2)}) collective-permute-start(f32[3,16,8,128]{3,0,2,1:T(4,128)S(1)} %get-tuple-element.83), channel_id=1, source_target_pairs={{0,64},{64,0},{1,65},{65,1},{2,66},{66,2},{3,67},{67,3},{4,68},{68... | collective-permute-start | bytes 589832 | tf_op jit(solution)/shard_map/ppermute | solution.py:705
  8.7 29.8 %collective-permute-start.5 = (f32[3,16,8,128]{3,0,2,1:T(4,128)}, f32[3,16,8,128]{3,0,2,1:T(4,128)}, u32[]{:S(2)}, u32[]{:S(2)}) collective-permute-start(f32[3,16,8,128]{3,0,2,1:T(4,128)} %get-tuple-element.79), channel_id=1, source_target_pairs={{0,64},{64,0},{1,65},{65,1},{2,66},{66,2},{3,67},{67,3},{4,68},{68... | collective-permute-start | bytes 589832 | tf_op jit(solution)/shard_map/ppermute | solution.py:705
  8.9 19.5 %collective-permute-start = (f32[4,256,2]{2,1,0:T(8,128)S(1)}, f32[4,256,2]{2,1,0:T(8,128)S(1)}, u32[]{:S(2)}, u32[]{:S(2)}) collective-permute-start(f32[4,256,2]{2,1,0:T(8,128)S(1)} %get-tuple-element.80), channel_id=1, source_target_pairs={{0,64},{1,65},{2,66},{3,67},{4,68},{5,69},{6,70},{7,71},{8,72},{9,... | collective-permute-start | bytes 24584 | tf_op jit(solution)/shard_map/ppermute | solution.py:24
  13.8 15.3 %collective-permute-start.1 = (f32[4,256,2]{2,1,0:T(8,128)S(1)}, f32[4,256,2]{2,1,0:T(8,128)S(1)}, u32[]{:S(2)}, u32[]{:S(2)}) collective-permute-start(f32[4,256,2]{2,1,0:T(8,128)S(1)} %get-tuple-element.81), channel_id=1, source_target_pairs={{64,0},{65,1},{66,2},{67,3},{68,4},{69,5},{70,6},{71,7},{72,8},{73... | collective-permute-start | bytes 24584 | tf_op jit(solution)/shard_map/ppermute | solution.py:27
  29.6 14.1 %collective-permute-start.2 = (f32[2,256,132]{2,1,0:T(8,128)S(1)}, f32[2,256,132]{2,1,0:T(8,128)S(1)}, u32[]{:S(2)}, u32[]{:S(2)}) collective-permute-start(f32[2,256,132]{2,1,0:T(8,128)S(1)} %get-tuple-element.72), channel_id=1, source_target_pairs={{0,1},{1,2},{2,3},{3,4},{4,5},{5,6},{6,7},{7,8},{8,9},{9,10},{10,1... | collective-permute-start | bytes 811016 | tf_op jit(solution)/shard_map/ppermute | solution.py:24
  35.1 10.5 %collective-permute-start.3 = (f32[2,256,132]{2,1,0:T(8,128)S(1)}, f32[2,256,132]{2,1,0:T(8,128)S(1)}, u32[]{:S(2)}, u32[]{:S(2)}) collective-permute-start(f32[2,256,132]{2,1,0:T(8,128)S(1)} %get-tuple-element.73), channel_id=1, source_target_pairs={{1,0},{2,1},{3,2},{4,3},{5,4},{6,5},{7,6},{8,7},{9,8},{10,9},{11,1... | collective-permute-start | bytes 811016 | tf_op jit(solution)/shard_map/ppermute | solution.py:27
  96.2 15.5 %copy-start.1 = (f32[9,5,2,2,8,128]{5,4,3,2,1,0:T(8,128)}, f32[9,5,2,2,8,128]{5,4,3,2,1,0:T(8,128)S(1)}, u32[]{:S(2)}) copy-start(f32[9,5,2,2,8,128]{5,4,3,2,1,0:T(8,128)S(1)} %get-tuple-element.48.image_ref.image_in) | copy-start | bytes 2211844
  154.7 15.0 %collective-permute-start.6 = (f32[4,256,2]{2,1,0:T(8,128)S(1)}, f32[4,256,2]{2,1,0:T(8,128)S(1)}, u32[]{:S(2)}, u32[]{:S(2)}) collective-permute-start(f32[4,256,2]{2,1,0:T(8,128)S(1)} %get-tuple-element.76), channel_id=1, source_target_pairs={{0,64},{1,65},{2,66},{3,67},{4,68},{5,69},{6,70},{7,71},{8,72},{9,... | collective-permute-start | bytes 24584 | tf_op jit(solution)/shard_map/ppermute | solution.py:24
  158.8 16.2 %collective-permute-start.7 = (f32[4,256,2]{2,1,0:T(8,128)S(1)}, f32[4,256,2]{2,1,0:T(8,128)S(1)}, u32[]{:S(2)}, u32[]{:S(2)}) collective-permute-start(f32[4,256,2]{2,1,0:T(8,128)S(1)} %get-tuple-element.77), channel_id=1, source_target_pairs={{64,0},{65,1},{66,2},{67,3},{68,4},{69,5},{70,6},{71,7},{72,8},{73... | collective-permute-start | bytes 24584 | tf_op jit(solution)/shard_map/ppermute | solution.py:27
  160.3 22.0 %collective-permute-start.10 = (f32[3,16,8,128]{3,0,2,1:T(4,128)S(1)}, f32[3,16,8,128]{3,0,2,1:T(4,128)S(1)}, u32[]{:S(2)}, u32[]{:S(2)}) collective-permute-start(f32[3,16,8,128]{3,0,2,1:T(4,128)S(1)} %get-tuple-element.75), channel_id=1, source_target_pairs={{0,64},{64,0},{1,65},{65,1},{2,66},{66,2},{3,67},{67,3},{4,68},{68... | collective-permute-start | bytes 589832 | tf_op jit(solution)/shard_map/ppermute | solution.py:705
  175.6 10.9 %collective-permute-start.8 = (f32[2,256,132]{2,1,0:T(8,128)S(1)}, f32[2,256,132]{2,1,0:T(8,128)S(1)}, u32[]{:S(2)}, u32[]{:S(2)}) collective-permute-start(f32[2,256,132]{2,1,0:T(8,128)S(1)} %get-tuple-element.70), channel_id=1, source_target_pairs={{0,1},{1,2},{2,3},{3,4},{4,5},{5,6},{6,7},{7,8},{8,9},{9,10},{10,1... | collective-permute-start | bytes 811016 | tf_op jit(solution)/shard_map/ppermute | solution.py:24
  180.3 10.5 %collective-permute-start.9 = (f32[2,256,132]{2,1,0:T(8,128)S(1)}, f32[2,256,132]{2,1,0:T(8,128)S(1)}, u32[]{:S(2)}, u32[]{:S(2)}) collective-permute-start(f32[2,256,132]{2,1,0:T(8,128)S(1)} %get-tuple-element.71), channel_id=1, source_target_pairs={{1,0},{2,1},{3,2},{4,3},{5,4},{6,5},{7,6},{8,7},{9,8},{10,9},{11,1... | collective-permute-start | bytes 811016 | tf_op jit(solution)/shard_map/ppermute | solution.py:27

commit v2 on v0

v2 whole, which is shorter than its diff:
```python
import functools
import math

import jax
import jax.numpy as jnp
import numpy as np
from jax import lax
from jax.experimental import pallas as pl
from jax.experimental.pallas import tpu as pltpu
from jax.sharding import PartitionSpec as P

sharpness = 4.0
threshold = 0.5
floor_stiff = 0.001
BEND = math.tanh(sharpness * threshold)
FULL = math.tanh(sharpness * threshold) + math.tanh(sharpness * (1.0 - threshold))
HAT = (1.0, 2.0, 3.0, 2.0, 1.0)

MESH = pl.DeviceIdType.MESH
F32 = jnp.float32
BF16 = jnp.bfloat16
I32 = jnp.int32
ROWS = 112
LANES = 128
GXN = 8
YN = 16
CHUNKS = (
    (0, 0, 0), (0, 0, 1), (0, 0, 2), (0, 0, 3), (0, 0, 4), (0, 0, 5),
    (1, 0, 0), (1, 0, 1), (1, 0, 4),
    (0, 1, 0), (0, 1, 2), (0, 1, 6),
    (1, 1, 0), (1, 1, 4),
)
PAIRS = {4: ((0, 0), (0, 1)), 5: ((1, 0), (1, 1)), 6: ((0, 0), (1, 0))}


def row_table():
    table = np.zeros((ROWS, 81), np.float32)
    seen = set()
    for place, (dx, dy, kind) in enumerate(CHUNKS):
        for half in range(2):
            if kind < 4:
                px, py, c = kind // 2, kind % 2, half
            else:
                (px, py), c = PAIRS[kind][half], 2
            if (dx and px) or (dy and py):
                continue
            a, b = px + 2 * dx, py + 2 * dy
            for q in range(3):
                index = ((c * 3 + b) * 3 + a) * 3 + q
                assert index not in seen
                seen.add(index)
                table[place * 8 + half * 4 + q, index] = 1.0
    assert len(seen) == 81
    return table


def place_of():
    role, gx, gy = lax.axis_index("role"), lax.axis_index("gx"), lax.axis_index("gy")
    return role, gx, gy, 2 * gy + role


def device_at(gx, row):
    gx = lax.rem(gx + GXN, GXN)
    row = lax.rem(row + YN, YN)
    return {"role": lax.rem(row, 2), "gx": gx, "gy": lax.div(row, 2)}


def remote(src, dst, send, recv, device):
    return pltpu.make_async_remote_copy(
        src_ref=src, dst_ref=dst, send_sem=send, recv_sem=recv, device_id=device, device_id_type=MESH
    )


def iota(shape, dim):
    return lax.broadcasted_iota(I32, shape, dim)


def pieces_of(values, count):
    parts = []
    for _ in range(count):
        part = values.astype(BF16)
        parts.append(part)
        values = values - part.astype(F32)
    return parts


def slab_of(shift):
    role, gx, gy, row = place_of()
    slab = lax.rem(gx * 8 + gy + shift + 64, 64)
    return lax.div(slab, 8), lax.rem(slab, 8)


def slab_device(shift, other):
    role = lax.axis_index("role")
    gx, gy = slab_of(shift)
    return {"role": (1 - role) if other else role, "gx": gx, "gy": gy}


def partner():
    return slab_device(0, True)


def reach(places, extent):
    total = jnp.zeros(places.shape, F32)
    for k, weight in enumerate(HAT):
        target = places + (k - 2)
        total = total + jnp.where(jnp.logical_and(target >= 0, target < extent), weight, 0.0)
    return jnp.maximum(total, 1.0)


def column_z(role, shape, dim):
    lane = iota(shape, dim)
    beyond = lane - LANES + jnp.where(role == 0, LANES, -2)
    return jnp.where(lane < LANES, lane, jnp.where(lane < LANES + 2, beyond, -4096))


def hat_of(distance):
    return jnp.maximum(3 - jnp.abs(distance), 0).astype(F32)


def at(field, e, f, kind):
    return field[e, kind // 2, 16 * f + 8 * (kind % 2) : 16 * f + 8 * (kind % 2) + 8]


def parity_matrix(role):
    rows, cols = iota((256, 256), 0), iota((256, 256), 1)
    half = jnp.where(rows < LANES, role, 1 - role)
    spot = half * LANES + lax.rem(rows, LANES)
    return (spot == 2 * lax.rem(cols, LANES) + lax.div(cols, LANES)).astype(F32).astype(BF16)


def parity_back(role):
    rows, cols = iota((256, 256), 0), iota((256, 256), 1)
    half = jnp.where(cols < LANES, role, 1 - role)
    spot = half * LANES + lax.rem(cols, LANES)
    return (spot == 2 * lax.rem(rows, LANES) + lax.div(rows, LANES)).astype(F32).astype(BF16)


def mul(left, right):
    return jnp.dot(left, right, preferred_element_type=F32)


def edge_stage(r):
    role = lax.axis_index("role")
    rows, cols = iota((16, LANES), 0), iota((16, LANES), 1)
    chosen = jnp.where(role == 0, 124 + rows, rows)
    chosen = jnp.logical_and(cols == chosen, rows < 4).astype(F32).astype(BF16)
    for x in range(4):
        total = None
        for part in pieces_of(r.design[x], 2):
            one = lax.dot_general(chosen, part, (((1,), (1,)), ((), ())), preferred_element_type=F32)
            total = one if total is None else total + one
        r.edge[:, 256 * x : 256 * x + 256] = total[:8]


def design_copies(r):
    return [
        remote(r.design, r.lo, r.dsend.at[0], r.drecv.at[0], slab_device(1, False)),
        remote(r.design, r.hi, r.dsend.at[1], r.drecv.at[1], slab_device(-1, False)),
        remote(r.edge, r.edges.at[1], r.dsend.at[2], r.drecv.at[2], slab_device(0, True)),
        remote(r.edge, r.edges.at[0], r.dsend.at[3], r.drecv.at[3], slab_device(1, True)),
        remote(r.edge, r.edges.at[2], r.dsend.at[4], r.drecv.at[4], slab_device(-1, True)),
    ]


def nodal_copies(r):
    role = lax.axis_index("role")
    spot = pl.ds(pl.multiple_of(8 * (1 - role), 8), 8)
    return [
        remote(r.force.at[:, :, spot], r.force_other, r.dsend.at[5], r.drecv.at[5], partner()),
        remote(r.mask.at[:, :, spot], r.mask_other, r.dsend.at[6], r.drecv.at[6], partner()),
    ]


def swap_stage(r):
    copies = design_copies(r)
    for copy in copies + nodal_copies(r):
        copy.start()
    for copy in copies:
        copy.wait()


def filter_stage(r):
    role, gx, gy, row = place_of()
    slab = gx * 8 + gy
    has_lo, has_hi = slab > 0, slab < 63

    @pl.when(jnp.logical_not(has_lo))
    def _():
        r.lo[...] = jnp.zeros_like(r.lo)
        r.edges[0] = jnp.zeros((8, 1024), F32)

    @pl.when(jnp.logical_not(has_hi))
    def _():
        r.hi[...] = jnp.zeros_like(r.hi)
        r.edges[2] = jnp.zeros((8, 1024), F32)

    band = hat_of(column_z(role, (LANES, 256), 1) - iota((LANES, 256), 0)).astype(BF16)
    bands = jnp.concatenate([band, band], axis=0)
    step = iota((16, 256), 0)
    far = lax.rem(step, 8)
    spot = jnp.where(role == 0, LANES + far, far - 4)
    rim = hat_of(column_z(role, (16, 256), 1) - spot)
    rim = jnp.where(far < 4, rim, 0.0).astype(BF16)

    def plane(p, rows):
        ref = (r.lo, r.design, r.hi)[p // 4]
        return ref[p % 4, rows]

    def mix(get):
        return 3.0 * get(2) + 2.0 * (get(1) + get(3)) + (get(0) + get(4))

    for i in range(8):
        beyond = mix(lambda k: r.edges[(i + k) // 4, :, 256 * ((i + k) % 4) : 256 * ((i + k) % 4) + 256])
        beyond = jnp.concatenate(pieces_of(beyond, 2), axis=0)
        beyond = lax.dot_general(beyond, rim, (((0,), (0,)), ((), ())), preferred_element_type=F32)
        for b in range(4):
            rows = slice(64 * b, 64 * b + 64)
            wide = mix(lambda k: plane(i + k, rows))
            out = mul(jnp.concatenate(pieces_of(wide, 2), axis=1), bands)
            r.zc[i, 8 + 64 * b : 72 + 64 * b] = out + beyond[rows]
        r.zc[i, 0:8] = jnp.zeros((8, 256), F32)
        r.zc[i, 264:272] = jnp.zeros((8, 256), F32)

    z_places = column_z(role, (1, 256), 1) + role * LANES
    by_z = 1.0 / reach(z_places, 256)
    r.psum[...] = jnp.zeros_like(r.psum)

    def body(i, _):
        x = 4 * slab + i - 2
        inside = jnp.logical_and(x >= 0, x < 256)
        own = jnp.logical_and(i >= 2, i < 6)
        by_x = 1.0 / reach(jnp.full((1, 256), x, I32), 256)
        by_xz = by_z * by_x
        for b in range(8):
            first = 32 * b
            by = by_xz / reach(iota((32, 256), 0) + first, 256)
            total = (
                3.0 * r.zc[i, 8 + first : 40 + first]
                + 2.0 * (r.zc[i, 7 + first : 39 + first] + r.zc[i, 9 + first : 41 + first])
                + (r.zc[i, 6 + first : 38 + first] + r.zc[i, 10 + first : 42 + first])
            )
            bent = jnp.tanh(sharpness * (total * by - threshold))
            r.m[i, first : first + 32] = jnp.where(inside, (1.0 - bent * bent) * (by * (sharpness / FULL)), 0.0)
            shown = (BEND + bent[:, :LANES]) * (1.0 / FULL)
            r.psum[first : first + 32] += jnp.where(own, shown, 0.0)
        return 0

    lax.fori_loop(0, 8, body, 0)
    rows, cols = iota((LANES, 256), 0), iota((LANES, 256), 1)
    gather = jnp.logical_and(
        lax.div(cols, 16) == lax.div(rows, 8), lax.div(lax.rem(cols, 16), 4) == lax.rem(rows, 8)
    ).astype(F32).astype(BF16)
    parts = pieces_of(r.psum[...], 3)
    by_rows = mul(gather, parts[0]) + mul(gather, parts[1]) + mul(gather, parts[2])
    rows, cols = iota((LANES, LANES), 0), iota((LANES, LANES), 1)
    merge = (cols == 64 * role + lax.div(rows, 2)).astype(F32).astype(BF16)
    parts = pieces_of(by_rows, 3)
    density = (mul(parts[0], merge) + mul(parts[1], merge) + mul(parts[2], merge)) * (1.0 / 32.0)
    for k in range(YN):
        r.dens[k] = density[8 * k : 8 * k + 8]


def pack_stage(r):
    for copy in nodal_copies(r):
        copy.wait()
    role = lax.axis_index("role")
    matrix = parity_matrix(role)
    spot = pl.ds(pl.multiple_of(8 * role, 8), 8)
    r.vf[...] = jnp.zeros_like(r.vf)
    for q in range(3):
        own = r.force[q, :, spot].reshape(LANES, LANES)
        wide = jnp.concatenate([own, r.force_other[q].reshape(LANES, LANES)], axis=1)
        force = None
        for part in pieces_of(wide, 3):
            one = mul(part, matrix)
            force = one if force is None else force + one
        own = r.mask[q, :, spot].reshape(LANES, LANES)
        wide = jnp.concatenate([own, r.mask_other[q].reshape(LANES, LANES)], axis=1)
        free = mul((1 - wide).astype(F32).astype(BF16), matrix)
        force = force * free
        for x in range(16):
            for half in range(2):
                for kind, values in ((0, force), (1, free)):
                    r.vf[kind, x // 2, x % 2, pl.ds(4 * half + q, 8, stride=8)] = values[
                        8 * x : 8 * x + 8, LANES * half : LANES * half + LANES
                    ]


def spread_stage(r):
    role, gx, gy, row = place_of()
    copies = []
    for k in range(1, YN):
        target = lax.rem(row + k, YN)
        copies.append(
            remote(r.dens.at[target], r.dall.at[row], r.nsend.at[k], r.nrecv.at[k], device_at(gx, row + k))
        )
    copies.append(remote(r.vf.at[:, 0, 0], r.nxhi, r.nsend.at[16], r.nrecv.at[16], device_at(gx - 1, row)))
    copies.append(
        remote(r.vf.at[:, :, :, 0:8], r.nyhi, r.nsend.at[17], r.nrecv.at[17], device_at(gx, row - 1))
    )
    copies.append(
        remote(r.vf.at[:, 0, 0, 0:8], r.ncorner, r.nsend.at[18], r.nrecv.at[18], device_at(gx - 1, row - 1))
    )
    for copy in copies:
        copy.start()
    r.dall[row] = r.dens[row]
    for copy in copies:
        copy.wait()


def frame_stage(r):
    role, gx, gy, row = place_of()
    has_x, has_y = gx < GXN - 1, row < YN - 1
    has_both = jnp.logical_and(has_x, has_y)
    for kind, ref in ((0, r.r0), (1, r.free)):
        for e in range(8):
            for px in range(2):
                ref[e, px, 0:64] = r.vf[kind, e, px]
                ref[e, px, 64:72] = jnp.where(has_y, r.nyhi[kind, e, px], 0.0)
                ref[e, px, 72:80] = jnp.zeros((8, LANES), F32)
        ref[8, 0, 0:64] = jnp.where(has_x, r.nxhi[kind], 0.0)
        ref[8, 0, 64:72] = jnp.where(has_both, r.ncorner[kind], 0.0)
        ref[8, 0, 72:80] = jnp.zeros((8, LANES), F32)
        ref[8, 1] = jnp.zeros((80, LANES), F32)
    for e in range(8):
        r.rho[e] = r.dall[2 * e] + r.dall[2 * e + 1]
    whole = r.table[...]
    high, low = pieces_of(whole, 2)
    r.stiff[...] = jnp.concatenate(
        [
            jnp.concatenate([high, high], axis=1),
            jnp.concatenate([low, jnp.zeros_like(low)], axis=1),
        ],
        axis=0,
    )


def build_store(field, store):
    sub = iota((8, LANES), 0) < 4
    inside = iota((8, LANES), 1) < LANES - 1

    def body(e, _):
        for f in range(5):
            held = [at(field, e, f, k) for k in range(4)]
            shifted = [jnp.where(inside, pltpu.roll(v, LANES - 1, 1), 0.0) for v in held]
            turned = [None] + [pltpu.roll(v, 4, 0) for v in shifted[1:]]
            for k in range(4):
                store[e, f, k] = held[k]
            store[e, f, 4] = jnp.where(sub, shifted[0], turned[1])
            store[e, f, 5] = jnp.where(sub, shifted[2], turned[3])
            store[e, f, 6] = jnp.where(sub, shifted[0], turned[2])
        return 0

    lax.fori_loop(0, 9, body, 0)


def element_product(store, stiff, e):
    columns = []
    for f in range(4):
        columns.append(jnp.concatenate([store[e + dx, f + dy, kind] for dx, dy, kind in CHUNKS], axis=0))
    wide = jnp.concatenate(columns, axis=1)
    out = mul(stiff, jnp.concatenate(pieces_of(wide, 2), axis=0))
    product = out[:ROWS] + out[ROWS:]
    return columns, [product[:, f * LANES : (f + 1) * LANES] for f in range(4)]


def chunk_sum(left, right):
    both = left * right
    total = both[:8]
    for k in range(1, len(CHUNKS)):
        total = total + both[8 * k : 8 * k + 8]
    return total


def factor_of(rho):
    return floor_stiff + (1.0 - floor_stiff) * (rho * rho * rho)


def apply_operator(r, image):
    store, acc = r.store, r.acc
    acc[...] = jnp.zeros_like(acc)
    stiff = r.stiff[...]

    def body(e, energy):
        columns, products = element_product(store, stiff, e)
        factor = factor_of(r.rho[e])
        for f in range(4):
            scaled = products[f] * factor[f : f + 1, :]
            energy = energy + chunk_sum(columns[f], scaled)
            for place, (dx, dy, kind) in enumerate(CHUNKS):
                acc[e + dx, f + dy, kind] += scaled[8 * place : 8 * place + 8]
        return energy

    energy = lax.fori_loop(0, 8, body, jnp.zeros((8, LANES), F32))
    keep = jnp.logical_and(iota((8, LANES), 0) < 4, iota((8, LANES), 1) > 0)

    def fold(e, _):
        for f in range(5):
            z0, z1, z2 = acc[e, f, 4], acc[e, f, 5], acc[e, f, 6]
            t0, t1, t2 = (pltpu.roll(v, 4, 0) for v in (z0, z1, z2))
            for k, extra in enumerate((z0 + z2, t0, z1 + t2, t1)):
                extra = jnp.where(keep, pltpu.roll(extra, 1, 1), 0.0)
                first = 16 * f + 8 * (k % 2)
                image[e, k // 2, first : first + 8] = acc[e, f, k] + extra
        return 0

    lax.fori_loop(0, 9, fold, 0)
    return energy


def element_energy(r):
    stiff = r.stiff[...]

    def body(e, energy):
        columns, products = element_product(r.store, stiff, e)
        factor = factor_of(r.rho[e])
        for f in range(4):
            energy = energy + chunk_sum(columns[f], products[f] * factor[f : f + 1, :])
        return energy

    return lax.fori_loop(0, 8, body, jnp.zeros((8, LANES), F32))


def square_sum(field):
    def body(e, total):
        for f in range(4):
            for k in range(4):
                held = at(field, e, f, k)
                total = total + held * held
        return total

    return lax.fori_loop(0, 8, body, jnp.zeros((8, LANES), F32))


def sums_tile(gamma, delta):
    rows = iota((8, LANES), 0)
    gamma = jnp.sum(gamma, axis=0, keepdims=True)
    delta = jnp.sum(delta, axis=0, keepdims=True)
    return jnp.where(rows == 0, gamma, jnp.where(rows == 1, delta, 0.0))


def read_sums(sum_ref):
    return (
        jnp.sum(sum_ref[0:1, :], axis=1, keepdims=True),
        jnp.sum(sum_ref[1:2, :], axis=1, keepdims=True),
    )


def over_nodes(body):
    def step(e, _):
        body(e)
        return 0

    lax.fori_loop(0, 9, step, 0)


def reduce_parts(r, n):
    role, gx, gy, row = place_of()
    tile, slots, second, half = r["tile", n], r["slots", n], r["second", n], r["half", n]
    send, recv = r["rsend", n], r["rrecv", n]
    slots[row] = tile[...]
    copies = []
    for k in range(1, YN):
        copies.append(remote(tile, slots.at[row], send.at[k], recv.at[k], device_at(gx, row + k)))
    for copy in copies:
        copy.start()
    for copy in copies:
        copy.wait()
    part = slots[0]
    for k in range(1, YN):
        part = part + slots[k]
    half[...] = part
    second[gx] = part
    copies = []
    for k in range(1, GXN):
        copies.append(remote(half, second.at[gx], send.at[YN + k], recv.at[YN + k], device_at(gx + k, row)))
    for copy in copies:
        copy.start()
    for copy in copies:
        copy.wait()
    part = second[0]
    for k in range(1, GXN):
        part = part + second[k]
    r["sum", n][...] = part


FACE_MOVES = ((1, 0), (-1, 0), (0, 1), (0, -1), (1, 1), (1, -1), (-1, 1), (-1, -1))


def face_stage(r, n):
    role, gx, gy, row = place_of()
    image, corners = r["image", n], r["corners", n]
    ends = (
        (image.at[8, 0], r["xlo", n]),
        (image.at[0, 0], r["xhi", n]),
        (image.at[:, :, 64:72], r["ylo", n]),
        (image.at[:, :, 0:8], r["yhi", n]),
        (image.at[8, 0, 64:72], corners.at[0]),
        (image.at[8, 0, 0:8], corners.at[1]),
        (image.at[0, 0, 64:72], corners.at[2]),
        (image.at[0, 0, 0:8], corners.at[3]),
    )
    send, recv = r["fsend", n], r["frecv", n]
    copies = []
    for k, ((dx, dy), (src, dst)) in enumerate(zip(FACE_MOVES, ends)):
        copies.append(remote(src, dst, send.at[k], recv.at[k], device_at(gx + dx, row + dy)))
    for copy in copies:
        copy.start()
    reduce_parts(r, n)
    for copy in copies:
        copy.wait()


def add_faces(r, n, work):
    role, gx, gy, row = place_of()
    low_x, low_y = gx > 0, row > 0
    image, corners = r["image", n], r["corners", n]
    xlo, xhi, ylo, yhi = (r[name, n] for name in ("xlo", "xhi", "ylo", "yhi"))
    work[...] = image[...]
    work[0, 0] += jnp.where(low_x, xlo[...], 0.0)
    work[8, 0] += xhi[...]
    for e in range(9):
        for p in range(2):
            work[e, p, 0:8] += jnp.where(low_y, ylo[e, p], 0.0)
            work[e, p, 64:72] += yhi[e, p]
    work[0, 0, 0:8] += jnp.where(jnp.logical_and(low_x, low_y), corners[0], 0.0)
    work[0, 0, 64:72] += jnp.where(low_x, corners[1], 0.0)
    work[8, 0, 0:8] += jnp.where(low_y, corners[2], 0.0)
    work[8, 0, 64:72] += corners[3]
    work[...] = work[...] * r.free[...]


def spare(value):
    return value.reshape(1, 1, 1)


def first_stage(r):
    build_store(r.r0, r.store)
    delta = apply_operator(r, r["image", 0])
    r["tile", 0][...] = sums_tile(square_sum(r.r0), delta)


def second_stage(r):
    add_faces(r, 0, r.s0)
    gamma, delta = read_sums(r["sum", 0])
    alpha = spare(gamma / delta)

    def update(e):
        r.r1[e] = r.r0[e] - alpha * r.s0[e]

    over_nodes(update)
    build_store(r.r1, r.store)
    delta = apply_operator(r, r["image", 1])
    r["tile", 1][...] = sums_tile(square_sum(r.r1), delta)


def third_stage(r):
    add_faces(r, 1, r.work)
    gamma0, delta0 = read_sums(r["sum", 0])
    gamma1, delta1 = read_sums(r["sum", 1])
    alpha0 = gamma0 / delta0
    beta1 = gamma1 / gamma0
    alpha1 = gamma1 / (delta1 - beta1 * gamma1 / alpha0)
    alpha0, alpha1, beta1 = spare(alpha0), spare(alpha1), spare(beta1)

    def update(e):
        p = r.r1[e] + beta1 * r.r0[e]
        r.p1[e] = p
        r.u1[e] = alpha0 * r.r0[e] + alpha1 * p
        r.r2[e] = r.r1[e] - alpha1 * (r.work[e] + beta1 * r.s0[e])

    over_nodes(update)
    build_store(r.r2, r.store)
    delta = element_energy(r)
    r["tile", 2][...] = sums_tile(square_sum(r.r2), delta)


def reduce_stage(r):
    reduce_parts(r, 2)


def last_stage(r):
    gamma0, delta0 = read_sums(r["sum", 0])
    gamma1, delta1 = read_sums(r["sum", 1])
    gamma2, delta2 = read_sums(r["sum", 2])
    alpha0 = gamma0 / delta0
    beta1 = gamma1 / gamma0
    alpha1 = gamma1 / (delta1 - beta1 * gamma1 / alpha0)
    beta2 = gamma2 / gamma1
    alpha2 = spare(gamma2 / (delta2 - beta2 * gamma2 / alpha1))
    beta2 = spare(beta2)

    def update(e):
        r.u[e] = r.u1[e] + alpha2 * (r.r2[e] + beta2 * r.p1[e])

    over_nodes(update)
    build_store(r.u, r.store)
    stiff = r.stiff[...]
    rows = iota((8, LANES), 0)
    r.grad[0] = jnp.zeros((8, LANES), F32)
    r.grad[9] = jnp.zeros((8, LANES), F32)

    def body(e, _):
        columns, products = element_product(r.store, stiff, e)
        rho = r.rho[e]
        energy = jnp.zeros((8, LANES), F32)
        for f in range(4):
            one = jnp.sum(chunk_sum(columns[f], products[f]), axis=0, keepdims=True)
            energy = jnp.where(rows == f, one, energy)
        r.grad[e + 1] = (-3.0 * (1.0 - floor_stiff) / 32.0) * (rho * rho) * energy
        return 0

    lax.fori_loop(0, 8, body, 0)


def edge_targets():
    role, gx, gy, row = place_of()
    up, down = lax.rem(gx + 1, GXN), lax.rem(gx + GXN - 1, GXN)
    return [
        {"role": 0, "gx": up, "gy": 0},
        {"role": 1, "gx": up, "gy": 0},
        {"role": 0, "gx": down, "gy": 7},
        {"role": 1, "gx": down, "gy": 7},
    ]


def gradient_copies(r):
    role, gx, gy, row = place_of()
    copies = []
    for k in range(1, YN):
        target = lax.div(lax.rem(row + k, YN), 2)
        copies.append(
            remote(r.grad.at[pl.ds(target, 3)], r.gall.at[row], r.gsend.at[k], r.grecv.at[k], device_at(gx, row + k))
        )
    return copies


def rim_copies(r):
    role, gx, gy, row = place_of()
    copies = []
    for k, device in enumerate(edge_targets()):
        layer = 8 if k < 2 else 1
        copies.append(remote(r.grad.at[layer], r.grim.at[row], r.esend.at[k], r.erecv.at[row], device))
    return copies


def gradient_stage(r):
    role, gx, gy, row = place_of()
    copies, rims = gradient_copies(r), rim_copies(r)
    for copy in copies + rims:
        copy.start()
    r.gall[row] = r.grad[pl.ds(gy, 3)]
    for copy in copies:
        copy.wait()
    for copy in rims:
        copy.wait_send()

    @pl.when(jnp.logical_or(gy == 0, gy == 7))
    def _():
        for k in range(YN):
            remote(r.grad.at[1], r.grim.at[k], r.esend.at[0], r.erecv.at[k], partner()).wait_recv()


def unpack_stage(r):
    role = lax.axis_index("role")
    back = parity_back(role)
    spot = pl.ds(pl.multiple_of(8 * role, 8), 8)
    for q in range(3):
        even = [r.u[x // 2, x % 2, pl.ds(q, 8, stride=8)] for x in range(16)]
        odd = [r.u[x // 2, x % 2, pl.ds(4 + q, 8, stride=8)] for x in range(16)]
        wide = jnp.concatenate([jnp.concatenate(even, axis=0), jnp.concatenate(odd, axis=0)], axis=1)
        total = None
        for part in pieces_of(wide, 3):
            one = mul(part, back)
            total = one if total is None else total + one
        r.disp[q, :, spot] = total[:, :LANES].reshape(16, 8, LANES)
        r.give[q] = total[:, LANES:].reshape(16, 8, LANES)


def give_copy(r):
    role = lax.axis_index("role")
    spot = pl.ds(pl.multiple_of(8 * role, 8), 8)
    return remote(r.give, r.disp.at[:, :, spot], r.osend.at[0], r.orecv.at[0], partner())


def give_stage(r):
    give_copy(r).start()


def given_stage(r):
    give_copy(r).wait()


def final_stage(r):
    role, gx, gy, row = place_of()
    for k in range(YN):
        r.layers[0, 8 * k : 8 * k + 8] = r.gall[k, 0]
        r.layers[1, 8 * k : 8 * k + 8] = r.gall[k, 1]
        r.layers[2, 8 * k : 8 * k + 8] = r.gall[k, 2]

    @pl.when(gy == 0)
    def _():
        for k in range(YN):
            r.layers[0, 8 * k : 8 * k + 8] = r.grim[k]

    @pl.when(gy == 7)
    def _():
        for k in range(YN):
            r.layers[2, 8 * k : 8 * k + 8] = r.grim[k]

    rows = iota((LANES, 256), 0)
    z = column_z(role, (LANES, 256), 1) + role * LANES
    widen = jnp.logical_and(z >= 0, rows == lax.div(jnp.maximum(z, 0), 2)).astype(F32).astype(BF16)
    widen = jnp.concatenate([widen, widen], axis=0)
    rows, cols = iota((256, LANES), 0), iota((256, LANES), 1)
    repeat = (cols == 8 * lax.div(rows, 16) + lax.div(lax.rem(rows, 16), 4)).astype(F32).astype(BF16)
    repeat = jnp.concatenate([repeat, repeat], axis=1)
    for k in range(3):
        wide = mul(jnp.concatenate(pieces_of(r.layers[k], 2), axis=1), widen)
        r.wide[k] = mul(repeat, jnp.concatenate(pieces_of(wide, 2), axis=0))
    band = hat_of(iota((256, LANES), 1) - column_z(role, (256, LANES), 0)).astype(BF16)
    bands = jnp.concatenate([band, band], axis=0)
    for o in range(4):
        r.zc[o, 0:8] = jnp.zeros((8, 256), F32)
        r.zc[o, 264:272] = jnp.zeros((8, 256), F32)
        for b in range(8):
            spot = slice(32 * b, 32 * b + 32)
            total = None
            for layer, planes in ((0, (0, 1)), (1, (2, 3, 4, 5)), (2, (6, 7))):
                part = None
                for i in planes:
                    if o <= i <= o + 4:
                        one = HAT[i - o] * r.m[i, spot]
                        part = one if part is None else part + one
                if part is not None:
                    part = part * r.wide[layer, spot]
                    total = part if total is None else total + part
            r.zc[o, 8 + 32 * b : 40 + 32 * b] = total
        for b in range(8):
            first = 32 * b
            total = (
                3.0 * r.zc[o, 8 + first : 40 + first]
                + 2.0 * (r.zc[o, 7 + first : 39 + first] + r.zc[o, 9 + first : 41 + first])
                + (r.zc[o, 6 + first : 38 + first] + r.zc[o, 10 + first : 42 + first])
            )
            r.sens[o, first : first + 32] = mul(jnp.concatenate(pieces_of(total, 2), axis=1), bands)


FIELD = (9, 2, 80, LANES)
TILE = (8, LANES)


class Refs(dict):
    def __getattr__(self, name):
        return self[name]


def buffers():
    shapes = {
        "edge": (8, 1024), "lo": (4, 256, LANES), "hi": (4, 256, LANES), "edges": (3, 8, 1024),
        "force_other": (3, 16, 8, LANES), "m": (8, 256, 256), "zc": (8, 272, 256), "psum": (256, LANES),
        "dens": (YN, 8, LANES), "vf": (2, 8, 2, 64, LANES), "nxhi": (2, 64, LANES), "nyhi": (2, 8, 2, 8, LANES),
        "ncorner": (2, 8, LANES), "dall": (YN, 8, LANES), "rho": (8, 8, LANES), "store": (9, 5, 7, 8, LANES),
        "acc": (9, 5, 7, 8, LANES), "grad": (10, 8, LANES), "gall": (YN, 3, 8, LANES), "grim": (YN, 8, LANES),
        "give": (3, 16, 8, LANES), "layers": (3, LANES, LANES), "wide": (3, 256, 256),
    }
    for name in ("r0", "free", "s0", "r1", "p1", "u1", "r2", "u", "work"):
        shapes[name] = FIELD
    for n in range(3):
        shapes["tile", n] = shapes["sum", n] = shapes["half", n] = TILE
        shapes["slots", n] = (YN, 8, LANES)
        shapes["second", n] = (GXN, 8, LANES)
    for n in range(2):
        shapes["image", n] = FIELD
        shapes["xlo", n] = shapes["xhi", n] = (80, LANES)
        shapes["ylo", n] = shapes["yhi", n] = (9, 2, 8, LANES)
        shapes["corners", n] = (4, 8, LANES)
    scratch = {name: pltpu.VMEM(shape, F32) for name, shape in shapes.items()}
    scratch["mask_other"] = pltpu.VMEM((3, 16, 8, LANES), I32)
    scratch["stiff"] = pltpu.VMEM((2 * ROWS, 2 * ROWS), BF16)
    counts = {"dsend": 7, "drecv": 7, "nsend": 19, "nrecv": 19, "gsend": 16, "grecv": 16, "esend": 4, "erecv": 16,
              "osend": 1, "orecv": 1}
    for n in range(3):
        counts["rsend", n] = counts["rrecv", n] = 24
        counts["fsend", n] = counts["frecv", n] = 8
    for name, count in counts.items():
        scratch[name] = pltpu.SemaphoreType.DMA((count,))
    return scratch


def greet_all():
    role, gx, gy, row = place_of()
    barrier = pltpu.get_barrier_semaphore()
    devices = [device_at(gx, row + k) for k in range(1, YN)]
    devices += [device_at(gx + k, row) for k in range(1, GXN)]
    devices += [device_at(gx + dx, row + dy) for dx, dy in FACE_MOVES[4:]]
    devices += [slab_device(shift, other) for shift, other in ((1, 0), (-1, 0), (1, 1), (-1, 1))]
    for device in devices:
        pl.semaphore_signal(barrier, inc=1, device_id=device, device_id_type=MESH)

    @pl.when(gy == 0)
    def _():
        for k in range(YN):
            pl.semaphore_signal(barrier, inc=1, device_id=device_at(gx - 1, row * 0 + k), device_id_type=MESH)

    @pl.when(gy == 7)
    def _():
        for k in range(YN):
            pl.semaphore_signal(barrier, inc=1, device_id=device_at(gx + 1, row * 0 + k), device_id_type=MESH)

    return len(devices) + 4


def whole_kernel(names, *refs):
    r = Refs(zip(names, refs))
    count = greet_all()
    edge_stage(r)
    pl.semaphore_wait(pltpu.get_barrier_semaphore(), count)
    swap_stage(r)
    filter_stage(r)
    pack_stage(r)
    spread_stage(r)
    frame_stage(r)
    first_stage(r)
    face_stage(r, 0)
    second_stage(r)
    face_stage(r, 1)
    third_stage(r)
    reduce_stage(r)
    last_stage(r)
    gradient_stage(r)
    unpack_stage(r)
    give_stage(r)
    final_stage(r)
    given_stage(r)


def on_device(design, force, clamped_dof_mask, stiffness):
    chosen = jnp.asarray(row_table())
    table = jnp.dot(
        jnp.dot(chosen, stiffness, precision=lax.Precision.HIGHEST), chosen.T, precision=lax.Precision.HIGHEST
    )
    scratch = buffers()
    names = ["design", "force", "mask", "table", "sens", "disp"] + list(scratch)
    vmem = pl.BlockSpec(memory_space=pltpu.VMEM)
    return pl.pallas_call(
        functools.partial(whole_kernel, names),
        out_shape=(
            jax.ShapeDtypeStruct((4, 256, LANES), F32),
            jax.ShapeDtypeStruct((3, 16, 16, LANES), F32),
        ),
        in_specs=[vmem] * 4,
        out_specs=(vmem, vmem),
        scratch_shapes=list(scratch.values()),
        compiler_params=pltpu.CompilerParams(
            collective_id=0, has_side_effects=True, vmem_limit_bytes=56 * 1024 * 1024
        ),
        name="compliance",
    )(design, force, clamped_dof_mask, table)


def solution(mesh):
    fine = P(("gx", "gy"), None, "role")
    nodes = P(None, "gx", "gy", "role")
    return jax.shard_map(
        on_device, mesh=mesh, in_specs=(fine, nodes, nodes, P()), out_specs=(fine, nodes), check_vma=False
    )
```

time: 581 us -> 104 us (0.18); the launches traced: 571 us -> 103 us
  blocking collectives: 176 us -> 0 us
  local copies, waits for them, and re-layouts: 131 us -> 3.45 us
  Pallas kernels: 0 us -> 97 us
  starting transfers between devices: 93.2 us -> 0 us
  waiting for transfers between devices: 68.7 us -> 0 us
  other arithmetic: 52.8 us -> 0 us
  matrix products: 40.7 us -> 1.87 us
  between operations: 8.97 us -> 0.68 us
    psum x25 -> x0, blocking collectives: 169 us -> none  [over_axes(): shard = lax.psum(shard, axis)]
    pallas_call x0 -> x1, Pallas kernels: none -> 97 us  [on_device(): pl.pallas_call(functools.partial(whole_kernel, names), out_shape=(jax.Sha...]
    ppermute x32 -> x0, starting transfers between devices: 88 us -> none  [the longest x16 62.8 us: with_halo(): lax.ppermute(lax.slice_in_dim(block, block.shape[dim] - width, None, axis...]
    ppermute x32 -> x0, waiting for transfers between devices: 68.7 us -> none  [the longest x16 56.8 us: with_halo(): lax.ppermute(lax.slice_in_dim(block, 0, width, axis=dim), axis, backward)]
    slice x40 -> x0, local copies, waits for them, and re-layouts: 62 us -> none  [the longest x12 47.5 us: split_axis(): lax.slice_in_dim(values, corner, corner + 2 * half_len - 1, stride=2, axi...]
    dot_general x15 -> x2, matrix products: 40.7 us -> 1.87 us  [the longest x1 1.01 us: on_device(): jnp.dot(chosen, stiffness, precision=lax.Precision.HIGHEST)]
    reshape x11 -> x0, local copies, waits for them, and re-layouts: 19.8 us -> none  [the longest x4 10.5 us: split_nodes(): return stacked.reshape(81, -1)]
    concatenate x16 -> x0, other arithmetic: 10.9 us -> none  [the longest x8 8.27 us: with_halo(): block = jnp.concatenate([low, block, high], axis=dim)]
  transfers between devices with their start and end apart: 33 -> 0, of which waited for: 18 -> 0; matrix products, arithmetic and copies ran while one was open for 9% -> 0% of each run, Pallas kernels for 0% -> 0%
where the time goes in v2:
time: 104 us; the launch traced here: 103 us
  Pallas kernels  97 us (93%)
  local copies, waits for them, and re-layouts  3.45 us (3%)
  matrix products  1.87 us (2%)
    pallas_call x1, Pallas kernels, on_device(): pl.pallas_call(functools.partial(whole_kernel, names), out_shape=(jax.Sha...  97 us
    unnamed x8, local copies, waits for them, and re-layouts  3.45 us

profile of v2, /device:TPU:1, one launch (start us, length us, event | category | flops | bytes accessed | tf_op | source)
XLA Modules:
  0.0 103.0 jit_solution(17327125748496271313)
XLA Ops:
  0.6 0.0 copy-start
  0.6 0.0 copy-start.2
  0.7 0.8 copy-done
  1.4 1.0 fusion
  2.4 0.0 copy-done.2
  2.5 0.9 fusion.1.refs_3_
  3.3 97.0 %compliance.1 = (f32[4,256,128]{2,1,0:T(8,128)}, f32[3,16,16,128]{3,2,1,0:T(8,128)}) custom-call(f32[4,256,128]{2,1,0:T(8,128)} %refs_0_.1, f32[3,16,16,128]{3,2,1,0:T(8,128)} %refs_1_.1, s32[3,16,16,128]{3,2,1,0:T(8,128)} %refs_2_.1, f32[112,112]{1,0:T(8,128)} %fusion.1.refs_3_), custom_call_target="tpu_custom_call" | custom-call | tf_op jit(solution)/shard_map/compliance/pallas_call | solution.py:847
  100.3 0.0 copy-start.1
  100.3 1.9 %copy.9 = f32[4,256,128]{2,1,0:T(8,128)} copy(f32[4,256,128]{2,1,0:T(8,128)} %get-tuple-element.4) | data formatting | bytes 1048576
  102.2 0.0 copy-done.1
  102.2 0.7 copy.10
Async XLA Ops:
  0.6 0.8 copy-start
  0.6 1.8 %copy-start.2 = (f32[112,81]{1,0:T(8,128)S(1)}, f32[112,81]{1,0:T(8,128)}, u32[]{:S(2)}) copy-start(f32[112,81]{1,0:T(8,128)} %constant.2.clone) | copy-start | bytes 108868
  100.3 1.9 %copy-start.1 = (f32[3,16,16,128]{3,2,1,0:T(8,128)S(1)}, f32[3,16,16,128]{3,2,1,0:T(8,128)}, u32[]{:S(2)}) copy-start(f32[3,16,16,128]{3,2,1,0:T(8,128)} %get-tuple-element.5) | copy-start | bytes 1179652

commit v3 on v2

--- a/solution.py
+++ b/solution.py
@@ -23,6 +23,7 @@
 ROWS = 112
 LANES = 128
 GXN = 8
+UPWARD = False
 YN = 16
 CHUNKS = (
     (0, 0, 0), (0, 0, 1), (0, 0, 2), (0, 0, 3), (0, 0, 4), (0, 0, 5),
@@ -153,52 +154,96 @@
         r.edge[:, 256 * x : 256 * x + 256] = total[:8]
 
 
-def design_copies(r):
+def near_copies(r):
     return [
-        remote(r.design, r.lo, r.dsend.at[0], r.drecv.at[0], slab_device(1, False)),
-        remote(r.design, r.hi, r.dsend.at[1], r.drecv.at[1], slab_device(-1, False)),
+        remote(r.design.at[2:4], r.lo.at[2:4], r.dsend.at[0], r.drecv.at[0], slab_device(1, False)),
+        remote(r.design.at[0:2], r.hi.at[0:2], r.dsend.at[1], r.drecv.at[1], slab_device(-1, False)),
         remote(r.edge, r.edges.at[1], r.dsend.at[2], r.drecv.at[2], slab_device(0, True)),
         remote(r.edge, r.edges.at[0], r.dsend.at[3], r.drecv.at[3], slab_device(1, True)),
         remote(r.edge, r.edges.at[2], r.dsend.at[4], r.drecv.at[4], slab_device(-1, True)),
     ]
 
 
-def nodal_copies(r):
+def far_copies(r):
+    return [
+        remote(r.design.at[0:2], r.lo.at[0:2], r.dsend.at[5], r.drecv.at[5], slab_device(1, False)),
+        remote(r.design.at[2:4], r.hi.at[2:4], r.dsend.at[6], r.drecv.at[6], slab_device(-1, False)),
+    ]
+
+
+def z_neighbour(upward):
+    role, gx, gy, row = place_of()
+    low = lax.rem(gx, 2)
+    same = (low == 0) if upward else (low == 1)
+    return {
+        "role": jnp.where(same, role, 1 - role), "gx": gx + 1 - 2 * low, "gy": gy,
+    }
+
+
+def force_copy(r):
+    spot = pl.ds(pl.multiple_of(8 * (1 - lax.axis_index("role")), 8), 8)
+    return remote(r.force.at[:, :, spot], r.force_other, r.dsend.at[7], r.drecv.at[7], partner())
+
+
+def mask_hop(r, q):
+    spot = pl.ds(pl.multiple_of(8 * (1 - lax.axis_index("role")), 8), 8)
+    return remote(
+        r.mask.at[q, :, spot], r.relay.at[q], r.dsend.at[8 + q], r.drecv.at[8 + q], z_neighbour(UPWARD)
+    )
+
+
+def mask_copy(r, q):
+    return remote(
+        r.relay.at[q], r.mask_other.at[q], r.dsend.at[11 + q], r.drecv.at[11 + q], z_neighbour(UPWARD)
+    )
+
+
+def swap_stage(r):
+    near = near_copies(r)
+    for copy in near:
+        copy.start()
+    for q in range(3):
+        mask_hop(r, q).start()
+    force_copy(r).start()
+    for copy in far_copies(r):
+        copy.start()
+    table_stage(r)
+    for q in range(3):
+        mask_hop(r, q).wait()
+        mask_copy(r, q).start()
+    for copy in near:
+        copy.wait()
+
+
+def table_stage(r):
+    chosen = r.chosen[...].astype(BF16)
+    table = None
+    for part in pieces_of(r.stiffness[...], 3):
+        one = mul(chosen, part)
+        table = one if table is None else table + one
+    whole = None
+    for part in pieces_of(table, 3):
+        one = lax.dot_general(part, chosen, (((1,), (1,)), ((), ())), preferred_element_type=F32)
+        whole = one if whole is None else whole + one
+    high, low = pieces_of(whole, 2)
+    r.stiff[...] = jnp.concatenate(
+        [
+            jnp.concatenate([high, high], axis=1),
+            jnp.concatenate([low, jnp.zeros_like(low)], axis=1),
+        ],
+        axis=0,
+    )
+
+
+def mix(get):
+    return 3.0 * get(2) + 2.0 * (get(1) + get(3)) + (get(0) + get(4))
+
+
+def taps_stage(r, planes):
     role = lax.axis_index("role")
-    spot = pl.ds(pl.multiple_of(8 * (1 - role), 8), 8)
-    return [
-        remote(r.force.at[:, :, spot], r.force_other, r.dsend.at[5], r.drecv.at[5], partner()),
-        remote(r.mask.at[:, :, spot], r.mask_other, r.dsend.at[6], r.drecv.at[6], partner()),
-    ]
-
-
-def swap_stage(r):
-    copies = design_copies(r)
-    for copy in copies + nodal_copies(r):
-        copy.start()
-    for copy in copies:
-        copy.wait()
-
-
-def filter_stage(r):
-    role, gx, gy, row = place_of()
-    slab = gx * 8 + gy
-    has_lo, has_hi = slab > 0, slab < 63
-
-    @pl.when(jnp.logical_not(has_lo))
-    def _():
-        r.lo[...] = jnp.zeros_like(r.lo)
-        r.edges[0] = jnp.zeros((8, 1024), F32)
-
-    @pl.when(jnp.logical_not(has_hi))
-    def _():
-        r.hi[...] = jnp.zeros_like(r.hi)
-        r.edges[2] = jnp.zeros((8, 1024), F32)
-
     band = hat_of(column_z(role, (LANES, 256), 1) - iota((LANES, 256), 0)).astype(BF16)
     bands = jnp.concatenate([band, band], axis=0)
-    step = iota((16, 256), 0)
-    far = lax.rem(step, 8)
+    far = lax.rem(iota((16, 256), 0), 8)
     spot = jnp.where(role == 0, LANES + far, far - 4)
     rim = hat_of(column_z(role, (16, 256), 1) - spot)
     rim = jnp.where(far < 4, rim, 0.0).astype(BF16)
@@ -207,10 +252,7 @@
         ref = (r.lo, r.design, r.hi)[p // 4]
         return ref[p % 4, rows]
 
-    def mix(get):
-        return 3.0 * get(2) + 2.0 * (get(1) + get(3)) + (get(0) + get(4))
-
-    for i in range(8):
+    for i in planes:
         beyond = mix(lambda k: r.edges[(i + k) // 4, :, 256 * ((i + k) % 4) : 256 * ((i + k) % 4) + 256])
         beyond = jnp.concatenate(pieces_of(beyond, 2), axis=0)
         beyond = lax.dot_general(beyond, rim, (((0,), (0,)), ((), ())), preferred_element_type=F32)
@@ -222,31 +264,72 @@
         r.zc[i, 0:8] = jnp.zeros((8, 256), F32)
         r.zc[i, 264:272] = jnp.zeros((8, 256), F32)
 
+
+def bend_stage(r, count, plane_of, shown):
+    role, gx, gy, row = place_of()
+    slab = gx * 8 + gy
     z_places = column_z(role, (1, 256), 1) + role * LANES
     by_z = 1.0 / reach(z_places, 256)
-    r.psum[...] = jnp.zeros_like(r.psum)
-
-    def body(i, _):
+
+    def body(step, _):
+        i = plane_of(step)
         x = 4 * slab + i - 2
         inside = jnp.logical_and(x >= 0, x < 256)
-        own = jnp.logical_and(i >= 2, i < 6)
         by_x = 1.0 / reach(jnp.full((1, 256), x, I32), 256)
         by_xz = by_z * by_x
         for b in range(8):
             first = 32 * b
             by = by_xz / reach(iota((32, 256), 0) + first, 256)
-            total = (
-                3.0 * r.zc[i, 8 + first : 40 + first]
-                + 2.0 * (r.zc[i, 7 + first : 39 + first] + r.zc[i, 9 + first : 41 + first])
-                + (r.zc[i, 6 + first : 38 + first] + r.zc[i, 10 + first : 42 + first])
-            )
+            total = mix(lambda k: r.zc[i, 6 + k + first : 38 + k + first])
             bent = jnp.tanh(sharpness * (total * by - threshold))
             r.m[i, first : first + 32] = jnp.where(inside, (1.0 - bent * bent) * (by * (sharpness / FULL)), 0.0)
-            shown = (BEND + bent[:, :LANES]) * (1.0 / FULL)
-            r.psum[first : first + 32] += jnp.where(own, shown, 0.0)
+            if shown:
+                r.psum[first : first + 32] += (BEND + bent[:, :LANES]) * (1.0 / FULL)
         return 0
 
-    lax.fori_loop(0, 8, body, 0)
+    lax.fori_loop(0, count, body, 0)
+
+
+def inner_stage(r):
+    role, gx, gy, row = place_of()
+    slab = gx * 8 + gy
+
+    @pl.when(slab == 0)
+    def _():
+        r.lo[2:4] = jnp.zeros((2, 256, LANES), F32)
+        r.edges[0] = jnp.zeros((8, 1024), F32)
+
+    @pl.when(slab == 63)
+    def _():
+        r.hi[0:2] = jnp.zeros((2, 256, LANES), F32)
+        r.edges[2] = jnp.zeros((8, 1024), F32)
+
+    taps_stage(r, (2, 3, 4, 5))
+    r.psum[...] = jnp.zeros_like(r.psum)
+    bend_stage(r, 4, lambda step: step + 2, True)
+    density_stage(r)
+
+
+def outer_stage(r):
+    role, gx, gy, row = place_of()
+    slab = gx * 8 + gy
+    for copy in far_copies(r):
+        copy.wait()
+
+    @pl.when(slab == 0)
+    def _():
+        r.lo[0:2] = jnp.zeros((2, 256, LANES), F32)
+
+    @pl.when(slab == 63)
+    def _():
+        r.hi[2:4] = jnp.zeros((2, 256, LANES), F32)
+
+    taps_stage(r, (0, 1, 6, 7))
+    bend_stage(r, 4, lambda step: jnp.where(step < 2, step, step + 4), False)
+
+
+def density_stage(r):
+    role = lax.axis_index("role")
     rows, cols = iota((LANES, 256), 0), iota((LANES, 256), 1)
     gather = jnp.logical_and(
         lax.div(cols, 16) == lax.div(rows, 8), lax.div(lax.rem(cols, 16), 4) == lax.rem(rows, 8)
@@ -262,8 +345,9 @@
 
 
 def pack_stage(r):
-    for copy in nodal_copies(r):
-        copy.wait()
+    force_copy(r).wait()
+    for q in range(3):
+        mask_copy(r, q).wait()
     role = lax.axis_index("role")
     matrix = parity_matrix(role)
     spot = pl.ds(pl.multiple_of(8 * role, 8), 8)
@@ -287,7 +371,7 @@
                     ]
 
 
-def spread_stage(r):
+def density_copies(r):
     role, gx, gy, row = place_of()
     copies = []
     for k in range(1, YN):
@@ -295,21 +379,33 @@
         copies.append(
             remote(r.dens.at[target], r.dall.at[row], r.nsend.at[k], r.nrecv.at[k], device_at(gx, row + k))
         )
-    copies.append(remote(r.vf.at[:, 0, 0], r.nxhi, r.nsend.at[16], r.nrecv.at[16], device_at(gx - 1, row)))
-    copies.append(
-        remote(r.vf.at[:, :, :, 0:8], r.nyhi, r.nsend.at[17], r.nrecv.at[17], device_at(gx, row - 1))
-    )
-    copies.append(
-        remote(r.vf.at[:, 0, 0, 0:8], r.ncorner, r.nsend.at[18], r.nrecv.at[18], device_at(gx - 1, row - 1))
-    )
-    for copy in copies:
+    return copies
+
+
+def upper_copies(r):
+    role, gx, gy, row = place_of()
+    return [
+        remote(r.vf.at[:, 0, 0], r.nxhi, r.nsend.at[16], r.nrecv.at[16], device_at(gx - 1, row)),
+        remote(r.vf.at[:, :, :, 0:8], r.nyhi, r.nsend.at[17], r.nrecv.at[17], device_at(gx, row - 1)),
+        remote(r.vf.at[:, 0, 0, 0:8], r.ncorner, r.nsend.at[18], r.nrecv.at[18], device_at(gx - 1, row - 1)),
+    ]
+
+
+def spread_stage(r):
+    role, gx, gy, row = place_of()
+    for copy in density_copies(r):
         copy.start()
     r.dall[row] = r.dens[row]
-    for copy in copies:
+
+
+def upper_stage(r):
+    for copy in upper_copies(r):
+        copy.start()
+
+
+def frame_stage(r):
+    for copy in density_copies(r) + upper_copies(r):
         copy.wait()
-
-
-def frame_stage(r):
     role, gx, gy, row = place_of()
     has_x, has_y = gx < GXN - 1, row < YN - 1
     has_both = jnp.logical_and(has_x, has_y)
@@ -325,15 +421,6 @@
         ref[8, 1] = jnp.zeros((80, LANES), F32)
     for e in range(8):
         r.rho[e] = r.dall[2 * e] + r.dall[2 * e + 1]
-    whole = r.table[...]
-    high, low = pieces_of(whole, 2)
-    r.stiff[...] = jnp.concatenate(
-        [
-            jnp.concatenate([high, high], axis=1),
-            jnp.concatenate([low, jnp.zeros_like(low)], axis=1),
-        ],
-        axis=0,
-    )
 
 
 def build_store(field, store):
@@ -434,16 +521,17 @@
 
 
 def sums_tile(gamma, delta):
-    rows = iota((8, LANES), 0)
     gamma = jnp.sum(gamma, axis=0, keepdims=True)
     delta = jnp.sum(delta, axis=0, keepdims=True)
-    return jnp.where(rows == 0, gamma, jnp.where(rows == 1, delta, 0.0))
+    gamma, delta = gamma + pltpu.roll(gamma, 64, 1), delta + pltpu.roll(delta, 64, 1)
+    return jnp.where(iota((1, LANES), 1) < 64, gamma, delta)
 
 
 def read_sums(sum_ref):
+    held, low = sum_ref[...], iota((1, LANES), 1) < 64
     return (
-        jnp.sum(sum_ref[0:1, :], axis=1, keepdims=True),
-        jnp.sum(sum_ref[1:2, :], axis=1, keepdims=True),
+        jnp.sum(jnp.where(low, held, 0.0), axis=1, keepdims=True),
+        jnp.sum(jnp.where(low, 0.0, held), axis=1, keepdims=True),
     )
 
 
@@ -455,34 +543,32 @@
     lax.fori_loop(0, 9, step, 0)
 
 
+def gy_device(shift):
+    role, gx, gy, row = place_of()
+    return {"role": role, "gx": gx, "gy": lax.rem(gy + shift, 8)}
+
+
+def cross_device(shift):
+    role, gx, gy, row = place_of()
+    target = lax.rem(2 * gx + role + shift, 16)
+    return {"role": lax.rem(target, 2), "gx": lax.div(target, 2), "gy": gy}
+
+
 def reduce_parts(r, n):
     role, gx, gy, row = place_of()
-    tile, slots, second, half = r["tile", n], r["slots", n], r["second", n], r["half", n]
-    send, recv = r["rsend", n], r["rrecv", n]
-    slots[row] = tile[...]
-    copies = []
-    for k in range(1, YN):
-        copies.append(remote(tile, slots.at[row], send.at[k], recv.at[k], device_at(gx, row + k)))
-    for copy in copies:
-        copy.start()
-    for copy in copies:
-        copy.wait()
-    part = slots[0]
-    for k in range(1, YN):
-        part = part + slots[k]
+    mine, slots, half, send, recv = r["tile", n], r["slots", n], r["half", n], r["rsend", n], r["rrecv", n]
+    slots[gy] = mine[...]
+    for k in range(1, 8):
+        remote(mine, slots.at[gy], send.at[0], recv.at[0], gy_device(k)).start()
+    remote(slots.at[0:7], slots.at[0:7], send.at[0], recv.at[0], partner()).wait()
+    part = jnp.sum(slots[0:8], axis=0)
     half[...] = part
-    second[gx] = part
-    copies = []
-    for k in range(1, GXN):
-        copies.append(remote(half, second.at[gx], send.at[YN + k], recv.at[YN + k], device_at(gx + k, row)))
-    for copy in copies:
-        copy.start()
-    for copy in copies:
-        copy.wait()
-    part = second[0]
-    for k in range(1, GXN):
-        part = part + second[k]
-    r["sum", n][...] = part
+    place = 8 + 2 * gx + role
+    slots[place] = part
+    for k in range(1, 16):
+        remote(half, slots.at[place], send.at[1], recv.at[1], cross_device(k)).start()
+    remote(slots.at[8:23], slots.at[8:23], send.at[1], recv.at[1], partner()).wait()
+    r["sum", n][...] = jnp.sum(slots[8:24], axis=0)
 
 
 FACE_MOVES = ((1, 0), (-1, 0), (0, 1), (0, -1), (1, 1), (1, -1), (-1, 1), (-1, -1))
@@ -598,20 +684,19 @@
     build_store(r.u, r.store)
     stiff = r.stiff[...]
     rows = iota((8, LANES), 0)
-    r.grad[0] = jnp.zeros((8, LANES), F32)
-    r.grad[9] = jnp.zeros((8, LANES), F32)
-
-    def body(e, _):
+
+    def body(e, before):
         columns, products = element_product(r.store, stiff, e)
         rho = r.rho[e]
         energy = jnp.zeros((8, LANES), F32)
         for f in range(4):
             one = jnp.sum(chunk_sum(columns[f], products[f]), axis=0, keepdims=True)
             energy = jnp.where(rows == f, one, energy)
-        r.grad[e + 1] = (-3.0 * (1.0 - floor_stiff) / 32.0) * (rho * rho) * energy
-        return 0
-
-    lax.fori_loop(0, 8, body, 0)
+        layer = (-3.0 * (1.0 - floor_stiff) / 32.0) * (rho * rho) * energy
+        r.grad[e] = before + pltpu.roll(layer, 4, 0)
+        return layer
+
+    r.grad[8] = lax.fori_loop(0, 8, body, jnp.zeros((8, LANES), F32))
 
 
 def edge_targets():
@@ -631,7 +716,7 @@
     for k in range(1, YN):
         target = lax.div(lax.rem(row + k, YN), 2)
         copies.append(
-            remote(r.grad.at[pl.ds(target, 3)], r.gall.at[row], r.gsend.at[k], r.grecv.at[k], device_at(gx, row + k))
+            remote(r.grad.at[pl.ds(target, 2)], r.gall.at[row], r.gsend.at[k], r.grecv.at[k], device_at(gx, row + k))
         )
     return copies
 
@@ -640,7 +725,7 @@
     role, gx, gy, row = place_of()
     copies = []
     for k, device in enumerate(edge_targets()):
-        layer = 8 if k < 2 else 1
+        layer = 8 if k < 2 else 0
         copies.append(remote(r.grad.at[layer], r.grim.at[row], r.esend.at[k], r.erecv.at[row], device))
     return copies
 
@@ -650,7 +735,7 @@
     copies, rims = gradient_copies(r), rim_copies(r)
     for copy in copies + rims:
         copy.start()
-    r.gall[row] = r.grad[pl.ds(gy, 3)]
+    r.gall[row] = r.grad[pl.ds(gy, 2)]
     for copy in copies:
         copy.wait()
     for copy in rims:
@@ -696,8 +781,8 @@
     role, gx, gy, row = place_of()
     for k in range(YN):
         r.layers[0, 8 * k : 8 * k + 8] = r.gall[k, 0]
-        r.layers[1, 8 * k : 8 * k + 8] = r.gall[k, 1]
-        r.layers[2, 8 * k : 8 * k + 8] = r.gall[k, 2]
+        r.layers[1, 8 * k : 8 * k + 8] = r.gall[k, 0]
+        r.layers[2, 8 * k : 8 * k + 8] = r.gall[k, 1]
 
     @pl.when(gy == 0)
     def _():
@@ -714,9 +799,10 @@
     widen = jnp.logical_and(z >= 0, rows == lax.div(jnp.maximum(z, 0), 2)).astype(F32).astype(BF16)
     widen = jnp.concatenate([widen, widen], axis=0)
     rows, cols = iota((256, LANES), 0), iota((256, LANES), 1)
-    repeat = (cols == 8 * lax.div(rows, 16) + lax.div(lax.rem(rows, 16), 4)).astype(F32).astype(BF16)
-    repeat = jnp.concatenate([repeat, repeat], axis=1)
+    cols = cols - 8 * lax.div(rows, 16) - lax.div(lax.rem(rows, 16), 4)
     for k in range(3):
+        repeat = (cols == (4 if k else 0)).astype(F32).astype(BF16)
+        repeat = jnp.concatenate([repeat, repeat], axis=1)
         wide = mul(jnp.concatenate(pieces_of(r.layers[k], 2), axis=1), widen)
         r.wide[k] = mul(repeat, jnp.concatenate(pieces_of(wide, 2), axis=0))
     band = hat_of(iota((256, LANES), 1) - column_z(role, (256, LANES), 0)).astype(BF16)
@@ -748,7 +834,7 @@
 
 
 FIELD = (9, 2, 80, LANES)
-TILE = (8, LANES)
+TILE = (1, LANES)
 
 
 class Refs(dict):
@@ -762,27 +848,27 @@
         "force_other": (3, 16, 8, LANES), "m": (8, 256, 256), "zc": (8, 272, 256), "psum": (256, LANES),
         "dens": (YN, 8, LANES), "vf": (2, 8, 2, 64, LANES), "nxhi": (2, 64, LANES), "nyhi": (2, 8, 2, 8, LANES),
         "ncorner": (2, 8, LANES), "dall": (YN, 8, LANES), "rho": (8, 8, LANES), "store": (9, 5, 7, 8, LANES),
-        "acc": (9, 5, 7, 8, LANES), "grad": (10, 8, LANES), "gall": (YN, 3, 8, LANES), "grim": (YN, 8, LANES),
+        "acc": (9, 5, 7, 8, LANES), "grad": (9, 8, LANES), "gall": (YN, 2, 8, LANES), "grim": (YN, 8, LANES),
         "give": (3, 16, 8, LANES), "layers": (3, LANES, LANES), "wide": (3, 256, 256),
     }
     for name in ("r0", "free", "s0", "r1", "p1", "u1", "r2", "u", "work"):
         shapes[name] = FIELD
     for n in range(3):
         shapes["tile", n] = shapes["sum", n] = shapes["half", n] = TILE
-        shapes["slots", n] = (YN, 8, LANES)
-        shapes["second", n] = (GXN, 8, LANES)
+        shapes["slots", n] = (24, 1, LANES)
     for n in range(2):
         shapes["image", n] = FIELD
         shapes["xlo", n] = shapes["xhi", n] = (80, LANES)
         shapes["ylo", n] = shapes["yhi", n] = (9, 2, 8, LANES)
         shapes["corners", n] = (4, 8, LANES)
     scratch = {name: pltpu.VMEM(shape, F32) for name, shape in shapes.items()}
+    scratch["relay"] = pltpu.VMEM((3, 16, 8, LANES), I32)
     scratch["mask_other"] = pltpu.VMEM((3, 16, 8, LANES), I32)
     scratch["stiff"] = pltpu.VMEM((2 * ROWS, 2 * ROWS), BF16)
-    counts = {"dsend": 7, "drecv": 7, "nsend": 19, "nrecv": 19, "gsend": 16, "grecv": 16, "esend": 4, "erecv": 16,
+    counts = {"dsend": 14, "drecv": 14, "nsend": 19, "nrecv": 19, "gsend": 16, "grecv": 16, "esend": 4, "erecv": 16,
               "osend": 1, "orecv": 1}
     for n in range(3):
-        counts["rsend", n] = counts["rrecv", n] = 24
+        counts["rsend", n] = counts["rrecv", n] = 2
         counts["fsend", n] = counts["frecv", n] = 8
     for name, count in counts.items():
         scratch[name] = pltpu.SemaphoreType.DMA((count,))
@@ -793,9 +879,10 @@
     role, gx, gy, row = place_of()
     barrier = pltpu.get_barrier_semaphore()
     devices = [device_at(gx, row + k) for k in range(1, YN)]
-    devices += [device_at(gx + k, row) for k in range(1, GXN)]
+    devices += [cross_device(k) for k in range(1, 16)]
     devices += [device_at(gx + dx, row + dy) for dx, dy in FACE_MOVES[4:]]
-    devices += [slab_device(shift, other) for shift, other in ((1, 0), (-1, 0), (1, 1), (-1, 1))]
+    devices += [slab_device(shift, other) for shift, other in ((1, False), (-1, False), (1, True), (-1, True))]
+    devices += [z_neighbour(True), z_neighbour(False), device_at(gx + 1, row), device_at(gx - 1, row)]
     for device in devices:
         pl.semaphore_signal(barrier, inc=1, device_id=device, device_id_type=MESH)
 
@@ -818,9 +905,11 @@
     edge_stage(r)
     pl.semaphore_wait(pltpu.get_barrier_semaphore(), count)
     swap_stage(r)
-    filter_stage(r)
+    inner_stage(r)
+    spread_stage(r)
     pack_stage(r)
-    spread_stage(r)
+    upper_stage(r)
+    outer_stage(r)
     frame_stage(r)
     first_stage(r)
     face_stage(r, 0)
@@ -838,11 +927,8 @@
 
 def on_device(design, force, clamped_dof_mask, stiffness):
     chosen = jnp.asarray(row_table())
-    table = jnp.dot(
-        jnp.dot(chosen, stiffness, precision=lax.Precision.HIGHEST), chosen.T, precision=lax.Precision.HIGHEST
-    )
     scratch = buffers()
-    names = ["design", "force", "mask", "table", "sens", "disp"] + list(scratch)
+    names = ["design", "force", "mask", "stiffness", "chosen", "sens", "disp"] + list(scratch)
     vmem = pl.BlockSpec(memory_space=pltpu.VMEM)
     return pl.pallas_call(
         functools.partial(whole_kernel, names),
@@ -850,14 +936,14 @@
             jax.ShapeDtypeStruct((4, 256, LANES), F32),
             jax.ShapeDtypeStruct((3, 16, 16, LANES), F32),
         ),
-        in_specs=[vmem] * 4,
+        in_specs=[vmem] * 5,
         out_specs=(vmem, vmem),
         scratch_shapes=list(scratch.values()),
         compiler_params=pltpu.CompilerParams(
-            collective_id=0, has_side_effects=True, vmem_limit_bytes=56 * 1024 * 1024
+            collective_id=0, has_side_effects=True, vmem_limit_bytes=36 * 1024 * 1024
         ),
         name="compliance",
-    )(design, force, clamped_dof_mask, table)
+    )(design, force, clamped_dof_mask, stiffness, chosen)
 
 
 def solution(mesh):

time: 104 us -> 97.7 us (0.939)
  Pallas kernels: 97 us -> 90.4 us
  local copies, waits for them, and re-layouts: 3.45 us -> 6.17 us
  matrix products: 1.87 us -> 0 us
    pallas_call x1, Pallas kernels: 97 us -> 90.4 us  [on_device(): pl.pallas_call(functools.partial(whole_kernel, names), out_shape=(jax.Sha...]
    unnamed x8 -> x12, local copies, waits for them, and re-layouts: 3.45 us -> 6.17 us
    dot_general x2 -> x0, matrix products: 1.87 us -> none  [the longest x1 1.01 us: on_device(): jnp.dot(chosen, stiffness, precision=lax.Precision.HIGHEST)]
where the time goes in v3:
time: 97.7 us; the launch traced here: 97.2 us
  Pallas kernels  90.4 us (93%)
  local copies, waits for them, and re-layouts  6.17 us (6%)
    pallas_call x1, Pallas kernels, on_device(): pl.pallas_call(functools.partial(whole_kernel, names), out_shape=(jax.Sha...  90.4 us
    unnamed x12, local copies, waits for them, and re-layouts  6.17 us

profile of v3, /device:TPU:1, one launch (start us, length us, event | category | flops | bytes accessed | tf_op | source)
XLA Modules:
  0.0 97.2 jit_solution(3978483872311514925)
XLA Ops:
  0.6 0.0 copy-start
  0.6 1.0 %copy-done = f32[4,256,128]{2,1,0:T(8,128)S(1)} copy-done((f32[4,256,128]{2,1,0:T(8,128)S(1)}, f32[4,256,128]{2,1,0:T(8,128)}, u32[]{:S(2)}) %copy-start) | copy-done | bytes 524312
  1.7 0.0 copy-start.1
  1.7 1.0 %copy-done.1 = f32[3,16,16,128]{3,2,1,0:T(8,128)S(1)} copy-done((f32[3,16,16,128]{3,2,1,0:T(8,128)S(1)}, f32[3,16,16,128]{3,2,1,0:T(8,128)}, u32[]{:S(2)}) %copy-start.1) | copy-done | bytes 393240
  2.7 0.0 copy-start.2
  2.7 1.0 %copy-done.2 = s32[3,16,16,128]{3,2,1,0:T(8,128)S(1)} copy-done((s32[3,16,16,128]{3,2,1,0:T(8,128)S(1)}, s32[3,16,16,128]{3,2,1,0:T(8,128)}, u32[]{:S(2)}) %copy-start.2) | copy-done | bytes 393240
  3.7 0.0 copy-start.3
  3.7 0.8 copy-done.3
  4.5 0.0 copy-start.4
  4.5 0.8 copy-done.4
  5.3 90.4 %compliance.1 = (f32[4,256,128]{2,1,0:T(8,128)S(1)}, f32[3,16,16,128]{3,2,1,0:T(8,128)S(1)}) custom-call(f32[4,256,128]{2,1,0:T(8,128)S(1)} %copy-done, f32[3,16,16,128]{3,2,1,0:T(8,128)S(1)} %copy-done.1, s32[3,16,16,128]{3,2,1,0:T(8,128)S(1)} %copy-done.2, f32[81,81]{1,0:T(8,128)S(1)} %copy-done.4, f32[112,81]{1,0:T(8,128)S(1)} %copy-done.3), custom_call_target="tpu_custom_call" | custom-call | tf_op jit(solution)/shard_map/compliance/pallas_call | solution.py:933
  95.7 0.8 copy.9
  96.5 0.7 copy.10
Async XLA Ops:
  0.6 1.0 %copy-start = (f32[4,256,128]{2,1,0:T(8,128)S(1)}, f32[4,256,128]{2,1,0:T(8,128)}, u32[]{:S(2)}) copy-start(f32[4,256,128]{2,1,0:T(8,128)} %refs_0_.1) | copy-start | bytes 1572868
  1.7 1.0 %copy-start.1 = (f32[3,16,16,128]{3,2,1,0:T(8,128)S(1)}, f32[3,16,16,128]{3,2,1,0:T(8,128)}, u32[]{:S(2)}) copy-start(f32[3,16,16,128]{3,2,1,0:T(8,128)} %refs_1_.1) | copy-start | bytes 1179652
  2.7 1.0 %copy-start.2 = (s32[3,16,16,128]{3,2,1,0:T(8,128)S(1)}, s32[3,16,16,128]{3,2,1,0:T(8,128)}, u32[]{:S(2)}) copy-start(s32[3,16,16,128]{3,2,1,0:T(8,128)} %refs_2_.1) | copy-start | bytes 1179652
  3.7 0.8 copy-start.3
  4.5 0.8 copy-start.4

commit v4 on v3

--- a/solution.py
+++ b/solution.py
@@ -23,8 +23,8 @@
 ROWS = 112
 LANES = 128
 GXN = 8
-UPWARD = False
-YN = 16
+GYN = 8
+LAST = 9
 CHUNKS = (
     (0, 0, 0), (0, 0, 1), (0, 0, 2), (0, 0, 3), (0, 0, 4), (0, 0, 5),
     (1, 0, 0), (1, 0, 1), (1, 0, 4),
@@ -56,14 +56,16 @@
 
 
 def place_of():
-    role, gx, gy = lax.axis_index("role"), lax.axis_index("gx"), lax.axis_index("gy")
-    return role, gx, gy, 2 * gy + role
-
-
-def device_at(gx, row):
-    gx = lax.rem(gx + GXN, GXN)
-    row = lax.rem(row + YN, YN)
-    return {"role": lax.rem(row, 2), "gx": gx, "gy": lax.div(row, 2)}
+    return lax.axis_index("role"), lax.axis_index("gx"), lax.axis_index("gy")
+
+
+def device_at(dx, dy, other=False):
+    role, gx, gy = place_of()
+    return {
+        "role": (1 - role) if other else role,
+        "gx": lax.rem(gx + dx + GXN, GXN),
+        "gy": lax.rem(gy + dy + GYN, GYN),
+    }
 
 
 def remote(src, dst, send, recv, device):
@@ -86,7 +88,7 @@
 
 
 def slab_of(shift):
-    role, gx, gy, row = place_of()
+    role, gx, gy = place_of()
     slab = lax.rem(gx * 8 + gy + shift + 64, 64)
     return lax.div(slab, 8), lax.rem(slab, 8)
 
@@ -95,10 +97,6 @@
     role = lax.axis_index("role")
     gx, gy = slab_of(shift)
     return {"role": (1 - role) if other else role, "gx": gx, "gy": gy}
-
-
-def partner():
-    return slab_device(0, True)
 
 
 def reach(places, extent):
@@ -123,18 +121,14 @@
     return field[e, kind // 2, 16 * f + 8 * (kind % 2) : 16 * f + 8 * (kind % 2) + 8]
 
 
-def parity_matrix(role):
+def parity_matrix():
     rows, cols = iota((256, 256), 0), iota((256, 256), 1)
-    half = jnp.where(rows < LANES, role, 1 - role)
-    spot = half * LANES + lax.rem(rows, LANES)
-    return (spot == 2 * lax.rem(cols, LANES) + lax.div(cols, LANES)).astype(F32).astype(BF16)
-
-
-def parity_back(role):
+    return (rows == 2 * lax.rem(cols, LANES) + lax.div(cols, LANES)).astype(F32).astype(BF16)
+
+
+def parity_back():
     rows, cols = iota((256, 256), 0), iota((256, 256), 1)
-    half = jnp.where(cols < LANES, role, 1 - role)
-    spot = half * LANES + lax.rem(cols, LANES)
-    return (spot == 2 * lax.rem(rows, LANES) + lax.div(rows, LANES)).astype(F32).astype(BF16)
+    return (cols == 2 * lax.rem(rows, LANES) + lax.div(rows, LANES)).astype(F32).astype(BF16)
 
 
 def mul(left, right):
@@ -171,47 +165,15 @@
     ]
 
 
-def z_neighbour(upward):
-    role, gx, gy, row = place_of()
-    low = lax.rem(gx, 2)
-    same = (low == 0) if upward else (low == 1)
-    return {
-        "role": jnp.where(same, role, 1 - role), "gx": gx + 1 - 2 * low, "gy": gy,
-    }
-
-
-def force_copy(r):
-    spot = pl.ds(pl.multiple_of(8 * (1 - lax.axis_index("role")), 8), 8)
-    return remote(r.force.at[:, :, spot], r.force_other, r.dsend.at[7], r.drecv.at[7], partner())
-
-
-def mask_hop(r, q):
-    spot = pl.ds(pl.multiple_of(8 * (1 - lax.axis_index("role")), 8), 8)
-    return remote(
-        r.mask.at[q, :, spot], r.relay.at[q], r.dsend.at[8 + q], r.drecv.at[8 + q], z_neighbour(UPWARD)
-    )
-
-
-def mask_copy(r, q):
-    return remote(
-        r.relay.at[q], r.mask_other.at[q], r.dsend.at[11 + q], r.drecv.at[11 + q], z_neighbour(UPWARD)
-    )
-
-
 def swap_stage(r):
-    near = near_copies(r)
-    for copy in near:
-        copy.start()
-    for q in range(3):
-        mask_hop(r, q).start()
-    force_copy(r).start()
-    for copy in far_copies(r):
+    for copy in near_copies(r) + upper_copies(r) + far_copies(r):
         copy.start()
     table_stage(r)
-    for q in range(3):
-        mask_hop(r, q).wait()
-        mask_copy(r, q).start()
-    for copy in near:
+    for copy in upper_copies(r):
+        copy.wait()
+    frame_stage(r)
+    bottom_copy(r).start()
+    for copy in near_copies(r):
         copy.wait()
 
 
@@ -266,7 +228,7 @@
 
 
 def bend_stage(r, count, plane_of, shown):
-    role, gx, gy, row = place_of()
+    role, gx, gy = place_of()
     slab = gx * 8 + gy
     z_places = column_z(role, (1, 256), 1) + role * LANES
     by_z = 1.0 / reach(z_places, 256)
@@ -291,7 +253,7 @@
 
 
 def inner_stage(r):
-    role, gx, gy, row = place_of()
+    role, gx, gy = place_of()
     slab = gx * 8 + gy
 
     @pl.when(slab == 0)
@@ -311,7 +273,7 @@
 
 
 def outer_stage(r):
-    role, gx, gy, row = place_of()
+    role, gx, gy = place_of()
     slab = gx * 8 + gy
     for copy in far_copies(r):
         copy.wait()
@@ -329,38 +291,35 @@
 
 
 def density_stage(r):
-    role = lax.axis_index("role")
     rows, cols = iota((LANES, 256), 0), iota((LANES, 256), 1)
-    gather = jnp.logical_and(
-        lax.div(cols, 16) == lax.div(rows, 8), lax.div(lax.rem(cols, 16), 4) == lax.rem(rows, 8)
-    ).astype(F32).astype(BF16)
+    sub = lax.rem(rows, 8)
+    wanted = 8 * lax.div(lax.rem(rows, 64), 8) + 4 * lax.div(rows, 64) + sub
+    gather = jnp.logical_and(sub < 4, lax.div(cols, 4) == wanted).astype(F32).astype(BF16)
     parts = pieces_of(r.psum[...], 3)
     by_rows = mul(gather, parts[0]) + mul(gather, parts[1]) + mul(gather, parts[2])
-    rows, cols = iota((LANES, LANES), 0), iota((LANES, LANES), 1)
-    merge = (cols == 64 * role + lax.div(rows, 2)).astype(F32).astype(BF16)
+    by_rows = jnp.concatenate([by_rows[:64], by_rows[64:]], axis=1)
+    rows, cols = iota((256, LANES), 0), iota((256, LANES), 1)
+    merge = (cols == 64 * lax.div(rows, LANES) + lax.div(lax.rem(rows, LANES), 2)).astype(F32).astype(BF16)
     parts = pieces_of(by_rows, 3)
     density = (mul(parts[0], merge) + mul(parts[1], merge) + mul(parts[2], merge)) * (1.0 / 32.0)
-    for k in range(YN):
+    for k in range(GYN):
         r.dens[k] = density[8 * k : 8 * k + 8]
 
 
 def pack_stage(r):
-    force_copy(r).wait()
-    for q in range(3):
-        mask_copy(r, q).wait()
-    role = lax.axis_index("role")
-    matrix = parity_matrix(role)
-    spot = pl.ds(pl.multiple_of(8 * role, 8), 8)
+    matrix = parity_matrix()
     r.vf[...] = jnp.zeros_like(r.vf)
     for q in range(3):
-        own = r.force[q, :, spot].reshape(LANES, LANES)
-        wide = jnp.concatenate([own, r.force_other[q].reshape(LANES, LANES)], axis=1)
+        wide = jnp.concatenate(
+            [r.force[q, :, 8 * h : 8 * h + 8].reshape(LANES, LANES) for h in range(2)], axis=1
+        )
         force = None
         for part in pieces_of(wide, 3):
             one = mul(part, matrix)
             force = one if force is None else force + one
-        own = r.mask[q, :, spot].reshape(LANES, LANES)
-        wide = jnp.concatenate([own, r.mask_other[q].reshape(LANES, LANES)], axis=1)
+        wide = jnp.concatenate(
+            [r.mask[q, :, 8 * h : 8 * h + 8].reshape(LANES, LANES) for h in range(2)], axis=1
+        )
         free = mul((1 - wide).astype(F32).astype(BF16), matrix)
         force = force * free
         for x in range(16):
@@ -372,65 +331,111 @@
 
 
 def density_copies(r):
-    role, gx, gy, row = place_of()
+    role, gx, gy = place_of()
     copies = []
-    for k in range(1, YN):
-        target = lax.rem(row + k, YN)
-        copies.append(
-            remote(r.dens.at[target], r.dall.at[row], r.nsend.at[k], r.nrecv.at[k], device_at(gx, row + k))
-        )
+    for k in range(1, GYN):
+        target = lax.rem(gy + k, GYN)
+        copies.append(remote(r.dens.at[target], r.dall.at[gy], r.nsend.at[k], r.nrecv.at[k], device_at(0, k)))
     return copies
 
 
 def upper_copies(r):
-    role, gx, gy, row = place_of()
     return [
-        remote(r.vf.at[:, 0, 0], r.nxhi, r.nsend.at[16], r.nrecv.at[16], device_at(gx - 1, row)),
-        remote(r.vf.at[:, :, :, 0:8], r.nyhi, r.nsend.at[17], r.nrecv.at[17], device_at(gx, row - 1)),
-        remote(r.vf.at[:, 0, 0, 0:8], r.ncorner, r.nsend.at[18], r.nrecv.at[18], device_at(gx - 1, row - 1)),
+        remote(r.vf.at[:, 0, 0], r.nxhi, r.nsend.at[8], r.nrecv.at[8], device_at(-1, 0)),
+        remote(r.vf.at[:, :, :, 0:8], r.nyhi, r.nsend.at[9], r.nrecv.at[9], device_at(0, -1)),
+        remote(r.vf.at[:, 0, 0, 0:8], r.ncorner, r.nsend.at[10], r.nrecv.at[10], device_at(-1, -1)),
     ]
 
 
+def bottom_copy(r):
+    return remote(r.bottom, r.nbottom, r.nsend.at[11], r.nrecv.at[11], device_at(0, 0, True))
+
+
 def spread_stage(r):
-    role, gx, gy, row = place_of()
+    gy = lax.axis_index("gy")
     for copy in density_copies(r):
         copy.start()
-    r.dall[row] = r.dens[row]
-
-
-def upper_stage(r):
-    for copy in upper_copies(r):
-        copy.start()
+    r.dall[gy] = r.dens[gy]
+
+
+def low_lanes():
+    return iota((8, LANES), 1) < 64
 
 
 def frame_stage(r):
-    for copy in density_copies(r) + upper_copies(r):
-        copy.wait()
-    role, gx, gy, row = place_of()
-    has_x, has_y = gx < GXN - 1, row < YN - 1
+    role, gx, gy = place_of()
+    has_x, has_y = gx < GXN - 1, gy < GYN - 1
     has_both = jnp.logical_and(has_x, has_y)
+    low = low_lanes()
+
+    def upper(beyond, own):
+        return pltpu.roll(jnp.where(low, beyond, own), 64, 1)
+
     for kind, ref in ((0, r.r0), (1, r.free)):
         for e in range(8):
             for px in range(2):
                 ref[e, px, 0:64] = r.vf[kind, e, px]
-                ref[e, px, 64:72] = jnp.where(has_y, r.nyhi[kind, e, px], 0.0)
+                ref[e, px, 64:72] = upper(jnp.where(has_y, r.nyhi[kind, e, px], 0.0), r.vf[kind, e, px, 0:8])
                 ref[e, px, 72:80] = jnp.zeros((8, LANES), F32)
-        ref[8, 0, 0:64] = jnp.where(has_x, r.nxhi[kind], 0.0)
-        ref[8, 0, 64:72] = jnp.where(has_both, r.ncorner[kind], 0.0)
+        beside = jnp.where(has_x, r.nxhi[kind], 0.0)
+        ref[8, 0, 0:64] = beside
+        ref[8, 0, 64:72] = upper(jnp.where(has_both, r.ncorner[kind], 0.0), beside[0:8])
         ref[8, 0, 72:80] = jnp.zeros((8, LANES), F32)
         ref[8, 1] = jnp.zeros((80, LANES), F32)
-    for e in range(8):
-        r.rho[e] = r.dall[2 * e] + r.dall[2 * e + 1]
-
-
-def build_store(field, store):
+        pack_bottom(ref, r.bottom.at[kind])
+
+
+def pack_bottom(field, out):
+    sub, lane = iota((8, LANES), 0) < 4, lax.rem(iota((8, LANES), 1), 64)
+
+    def body(e, _):
+        for px in range(2):
+            tile = jnp.zeros((8, LANES), F32)
+            for j in range(LAST):
+                held = field[e, px, 8 * j : 8 * j + 8]
+                held = pltpu.roll(held, j, 1) if j else held
+                tile = jnp.where(lane == j, held, tile)
+            out[2 * e + px] = jnp.where(sub, tile, 0.0)
+        return 0
+
+    lax.fori_loop(0, 9, body, 0)
+
+
+def add_bottom(field, tiles):
+    keep = jnp.logical_and(iota((8, LANES), 0) < 4, lax.rem(iota((8, LANES), 1), 64) == 0)
+
+    def body(e, _):
+        for px in range(2):
+            tile = tiles[2 * e + px]
+            for j in range(LAST):
+                moved = pltpu.roll(tile, LANES - j, 1) if j else tile
+                field[e, px, 8 * j : 8 * j + 8] += jnp.where(keep, moved, 0.0)
+        return 0
+
+    lax.fori_loop(0, 9, body, 0)
+
+
+def top_stage(r):
+    role = lax.axis_index("role")
+    bottom_copy(r).wait()
+    for kind, ref in ((0, r.r0t), (1, r.freet)):
+        ref[...] = jnp.where(role == 0, r.nbottom[kind], 0.0)
+    for copy in density_copies(r):
+        copy.wait()
+
+
+def build_store(field, top, store):
     sub = iota((8, LANES), 0) < 4
-    inside = iota((8, LANES), 1) < LANES - 1
+    inside = lax.rem(iota((8, LANES), 1), 64) < 63
 
     def body(e, _):
+        tops = [top[2 * e], top[2 * e + 1]]
         for f in range(5):
             held = [at(field, e, f, k) for k in range(4)]
-            shifted = [jnp.where(inside, pltpu.roll(v, LANES - 1, 1), 0.0) for v in held]
+            shifted = []
+            for k in range(4):
+                above = pltpu.roll(tops[k // 2], 63 - 2 * f - k % 2, 1)
+                shifted.append(jnp.where(inside, pltpu.roll(held[k], LANES - 1, 1), above))
             turned = [None] + [pltpu.roll(v, 4, 0) for v in shifted[1:]]
             for k in range(4):
                 store[e, f, k] = held[k]
@@ -464,7 +469,7 @@
     return floor_stiff + (1.0 - floor_stiff) * (rho * rho * rho)
 
 
-def apply_operator(r, image):
+def apply_operator(r, image, top):
     store, acc = r.store, r.acc
     acc[...] = jnp.zeros_like(acc)
     stiff = r.stiff[...]
@@ -480,16 +485,22 @@
         return energy
 
     energy = lax.fori_loop(0, 8, body, jnp.zeros((8, LANES), F32))
-    keep = jnp.logical_and(iota((8, LANES), 0) < 4, iota((8, LANES), 1) > 0)
+    sub, lane = iota((8, LANES), 0) < 4, lax.rem(iota((8, LANES), 1), 64)
+    keep = jnp.logical_and(sub, lane > 0)
 
     def fold(e, _):
+        tops = [jnp.zeros((8, LANES), F32), jnp.zeros((8, LANES), F32)]
         for f in range(5):
             z0, z1, z2 = acc[e, f, 4], acc[e, f, 5], acc[e, f, 6]
             t0, t1, t2 = (pltpu.roll(v, 4, 0) for v in (z0, z1, z2))
             for k, extra in enumerate((z0 + z2, t0, z1 + t2, t1)):
-                extra = jnp.where(keep, pltpu.roll(extra, 1, 1), 0.0)
                 first = 16 * f + 8 * (k % 2)
-                image[e, k // 2, first : first + 8] = acc[e, f, k] + extra
+                image[e, k // 2, first : first + 8] = acc[e, f, k] + jnp.where(keep, pltpu.roll(extra, 1, 1), 0.0)
+                j = 2 * f + k % 2
+                if j < LAST:
+                    tops[k // 2] = jnp.where(lane == j, pltpu.roll(extra, 65 + j, 1), tops[k // 2])
+        for px in range(2):
+            top[2 * e + px] = jnp.where(sub, tops[px], 0.0)
         return 0
 
     lax.fori_loop(0, 9, fold, 0)
@@ -543,40 +554,43 @@
     lax.fori_loop(0, 9, step, 0)
 
 
-def gy_device(shift):
-    role, gx, gy, row = place_of()
-    return {"role": role, "gx": gx, "gy": lax.rem(gy + shift, 8)}
-
-
 def cross_device(shift):
-    role, gx, gy, row = place_of()
+    role, gx, gy = place_of()
     target = lax.rem(2 * gx + role + shift, 16)
     return {"role": lax.rem(target, 2), "gx": lax.div(target, 2), "gy": gy}
 
 
-def reduce_parts(r, n):
-    role, gx, gy, row = place_of()
-    mine, slots, half, send, recv = r["tile", n], r["slots", n], r["half", n], r["rsend", n], r["rrecv", n]
+def reduce_start(r, n):
+    gy = lax.axis_index("gy")
+    mine, slots, send, recv = r["tile", n], r["slots", n], r["rsend", n], r["rrecv", n]
     slots[gy] = mine[...]
-    for k in range(1, 8):
-        remote(mine, slots.at[gy], send.at[0], recv.at[0], gy_device(k)).start()
-    remote(slots.at[0:7], slots.at[0:7], send.at[0], recv.at[0], partner()).wait()
+    for k in range(1, GYN):
+        remote(mine, slots.at[gy], send.at[0], recv.at[0], device_at(0, k)).start()
+
+
+def reduce_middle(r, n):
+    role, gx, gy = place_of()
+    slots, half, send, recv = r["slots", n], r["half", n], r["rsend", n], r["rrecv", n]
+    remote(slots.at[0:7], slots.at[0:7], send.at[0], recv.at[0], device_at(0, 0, True)).wait()
     part = jnp.sum(slots[0:8], axis=0)
     half[...] = part
     place = 8 + 2 * gx + role
     slots[place] = part
     for k in range(1, 16):
         remote(half, slots.at[place], send.at[1], recv.at[1], cross_device(k)).start()
-    remote(slots.at[8:23], slots.at[8:23], send.at[1], recv.at[1], partner()).wait()
+
+
+def reduce_end(r, n):
+    slots, send, recv = r["slots", n], r["rsend", n], r["rrecv", n]
+    remote(slots.at[8:23], slots.at[8:23], send.at[1], recv.at[1], device_at(0, 0, True)).wait()
     r["sum", n][...] = jnp.sum(slots[8:24], axis=0)
 
 
 FACE_MOVES = ((1, 0), (-1, 0), (0, 1), (0, -1), (1, 1), (1, -1), (-1, 1), (-1, -1))
 
 
-def face_stage(r, n):
-    role, gx, gy, row = place_of()
-    image, corners = r["image", n], r["corners", n]
+def face_copies(r, n):
+    image, corners, top, rows = r["image", n], r["corners", n], r["imaget", n], r["trow", n]
     ends = (
         (image.at[8, 0], r["xlo", n]),
         (image.at[0, 0], r["xhi", n]),
@@ -587,34 +601,102 @@
         (image.at[0, 0, 64:72], corners.at[2]),
         (image.at[0, 0, 0:8], corners.at[3]),
     )
+    tops = (top.at[16], top.at[0], rows.at[1], rows.at[0], rows.at[1], rows.at[0], rows.at[1], rows.at[0])
     send, recv = r["fsend", n], r["frecv", n]
     copies = []
     for k, ((dx, dy), (src, dst)) in enumerate(zip(FACE_MOVES, ends)):
-        copies.append(remote(src, dst, send.at[k], recv.at[k], device_at(gx + dx, row + dy)))
+        copies.append(remote(src, dst, send.at[k], recv.at[k], device_at(dx, dy)))
+        copies.append(remote(tops[k], r["tface", n].at[k], send.at[8 + k], recv.at[8 + k], device_at(dx, dy)))
+    return copies
+
+
+def face_stage(r, n):
+    role = lax.axis_index("role")
+    image, top, lift = r["image", n], r["imaget", n], r["lift", n]
+    reduce_start(r, n)
+
+    @pl.when(role == 0)
+    def _():
+        lift[...] = top[...]
+
+    @pl.when(role == 1)
+    def _():
+        pack_bottom(image, lift)
+
+    across = remote(lift, r["lifted", n], r["zsend", n].at[0], r["zrecv", n].at[0], device_at(0, 0, True))
+    across.start()
+    reduce_middle(r, n)
+    across.wait()
+
+    @pl.when(role == 0)
+    def _():
+        top[...] += r["lifted", n][...]
+
+    @pl.when(role == 1)
+    def _():
+        add_bottom(image, r["lifted", n])
+
+    lane = iota((8, LANES), 1)
+    below, above = jnp.zeros((8, LANES), F32), jnp.zeros((8, LANES), F32)
+    for x in range(17):
+        tile = top[x]
+        below = jnp.where(lane == x, pltpu.roll(tile, x, 1) if x else tile, below)
+        above = jnp.where(lane == x, pltpu.roll(tile, 56 + x, 1), above)
+    r["trow", n][0] = below
+    r["trow", n][1] = above
+    copies = face_copies(r, n)
     for copy in copies:
         copy.start()
-    reduce_parts(r, n)
+    reduce_end(r, n)
     for copy in copies:
         copy.wait()
 
 
-def add_faces(r, n, work):
-    role, gx, gy, row = place_of()
-    low_x, low_y = gx > 0, row > 0
-    image, corners = r["image", n], r["corners", n]
+def add_faces(r, n, work, workt):
+    role, gx, gy = place_of()
+    low_x, low_y = gx > 0, gy > 0
+    image, corners, top, tface = r["image", n], r["corners", n], r["imaget", n], r["tface", n]
     xlo, xhi, ylo, yhi = (r[name, n] for name in ("xlo", "xhi", "ylo", "yhi"))
+    low = low_lanes()
+
+    def join(e, p, below, above):
+        f0, f4 = work[e, p, 0:8], work[e, p, 64:72]
+        below = jnp.where(low_y, below, 0.0)
+        work[e, p, 0:8] = f0 + pltpu.roll(jnp.where(low, f4, below), 64, 1)
+        work[e, p, 64:72] = f4 + pltpu.roll(jnp.where(low, above, f0), 64, 1)
+
     work[...] = image[...]
     work[0, 0] += jnp.where(low_x, xlo[...], 0.0)
     work[8, 0] += xhi[...]
-    for e in range(9):
+    join(0, 0, ylo[0, 0] + jnp.where(low_x, corners[0], 0.0), yhi[0, 0] + jnp.where(low_x, corners[1], 0.0))
+    join(8, 0, ylo[8, 0] + corners[2], yhi[8, 0] + corners[3])
+    for e in range(8):
         for p in range(2):
-            work[e, p, 0:8] += jnp.where(low_y, ylo[e, p], 0.0)
-            work[e, p, 64:72] += yhi[e, p]
-    work[0, 0, 0:8] += jnp.where(jnp.logical_and(low_x, low_y), corners[0], 0.0)
-    work[0, 0, 64:72] += jnp.where(low_x, corners[1], 0.0)
-    work[8, 0, 0:8] += jnp.where(low_y, corners[2], 0.0)
-    work[8, 0, 64:72] += corners[3]
+            if e or p:
+                join(e, p, ylo[e, p], yhi[e, p])
     work[...] = work[...] * r.free[...]
+
+    lane = iota((8, LANES), 1)
+
+    def row_of(face, first, last):
+        first = jnp.where(low_x, first, 0.0)
+        face = face + jnp.where(lane == 0, pltpu.roll(first, LANES - 16, 1), 0.0)
+        return face + jnp.where(lane == 16, pltpu.roll(last, 16, 1), 0.0)
+
+    below = jnp.where(low_y, row_of(tface[2], tface[4], tface[6]), 0.0)
+    above = row_of(tface[3], tface[5], tface[7])
+    for x in range(17):
+        tile = top[x]
+        if x == 0:
+            tile = tile + jnp.where(low_x, tface[0], 0.0)
+        if x == 16:
+            tile = tile + tface[1]
+        total = tile + jnp.where(lane == 64, pltpu.roll(tile, 56, 1), 0.0)
+        total = total + jnp.where(lane == 8, pltpu.roll(tile, 72, 1), 0.0)
+        total = total + jnp.where(lane == 0, pltpu.roll(below, LANES - x, 1) if x else below, 0.0)
+        total = total + jnp.where(lane == 72, pltpu.roll(above, 72 - x, 1), 0.0)
+        workt[x] = total * r.freet[x]
+    workt[17] = jnp.zeros((8, LANES), F32)
 
 
 def spare(value):
@@ -622,13 +704,15 @@
 
 
 def first_stage(r):
-    build_store(r.r0, r.store)
-    delta = apply_operator(r, r["image", 0])
+    for e in range(8):
+        r.rho[e] = r.dall[e]
+    build_store(r.r0, r.r0t, r.store)
+    delta = apply_operator(r, r["image", 0], r["imaget", 0])
     r["tile", 0][...] = sums_tile(square_sum(r.r0), delta)
 
 
 def second_stage(r):
-    add_faces(r, 0, r.s0)
+    add_faces(r, 0, r.s0, r.s0t)
     gamma, delta = read_sums(r["sum", 0])
     alpha = spare(gamma / delta)
 
@@ -636,13 +720,14 @@
         r.r1[e] = r.r0[e] - alpha * r.s0[e]
 
     over_nodes(update)
-    build_store(r.r1, r.store)
-    delta = apply_operator(r, r["image", 1])
+    r.r1t[...] = r.r0t[...] - alpha * r.s0t[...]
+    build_store(r.r1, r.r1t, r.store)
+    delta = apply_operator(r, r["image", 1], r["imaget", 1])
     r["tile", 1][...] = sums_tile(square_sum(r.r1), delta)
 
 
 def third_stage(r):
-    add_faces(r, 1, r.work)
+    add_faces(r, 1, r.work, r.workt)
     gamma0, delta0 = read_sums(r["sum", 0])
     gamma1, delta1 = read_sums(r["sum", 1])
     alpha0 = gamma0 / delta0
@@ -657,13 +742,19 @@
         r.r2[e] = r.r1[e] - alpha1 * (r.work[e] + beta1 * r.s0[e])
 
     over_nodes(update)
-    build_store(r.r2, r.store)
+    p = r.r1t[...] + beta1 * r.r0t[...]
+    r.p1t[...] = p
+    r.u1t[...] = alpha0 * r.r0t[...] + alpha1 * p
+    r.r2t[...] = r.r1t[...] - alpha1 * (r.workt[...] + beta1 * r.s0t[...])
+    build_store(r.r2, r.r2t, r.store)
     delta = element_energy(r)
     r["tile", 2][...] = sums_tile(square_sum(r.r2), delta)
 
 
 def reduce_stage(r):
-    reduce_parts(r, 2)
+    reduce_start(r, 2)
+    reduce_middle(r, 2)
+    reduce_end(r, 2)
 
 
 def last_stage(r):
@@ -681,7 +772,8 @@
         r.u[e] = r.u1[e] + alpha2 * (r.r2[e] + beta2 * r.p1[e])
 
     over_nodes(update)
-    build_store(r.u, r.store)
+    r.ut[...] = r.u1t[...] + alpha2 * (r.r2t[...] + beta2 * r.p1t[...])
+    build_store(r.u, r.ut, r.store)
     stiff = r.stiff[...]
     rows = iota((8, LANES), 0)
 
@@ -697,60 +789,75 @@
         return layer
 
     r.grad[8] = lax.fori_loop(0, 8, body, jnp.zeros((8, LANES), F32))
+    role, lane = lax.axis_index("role"), lax.rem(iota((8, LANES), 1), 64)
+    rim = jnp.zeros((8, LANES), F32)
+    for k in range(9):
+        held = r.grad[k]
+        held = jnp.where(role == 0, pltpu.roll(held, k + 65, 1), pltpu.roll(held, k, 1) if k else held)
+        rim = jnp.where(lane == k, held, rim)
+    r.zgrad[...] = rim
 
 
 def edge_targets():
-    role, gx, gy, row = place_of()
+    role, gx, gy = place_of()
     up, down = lax.rem(gx + 1, GXN), lax.rem(gx + GXN - 1, GXN)
     return [
-        {"role": 0, "gx": up, "gy": 0},
-        {"role": 1, "gx": up, "gy": 0},
-        {"role": 0, "gx": down, "gy": 7},
-        {"role": 1, "gx": down, "gy": 7},
+        {"role": role, "gx": up, "gy": 0},
+        {"role": role, "gx": down, "gy": 7},
+        {"role": 1 - role, "gx": up, "gy": 0},
+        {"role": 1 - role, "gx": down, "gy": 7},
     ]
 
 
 def gradient_copies(r):
-    role, gx, gy, row = place_of()
+    gy = lax.axis_index("gy")
     copies = []
-    for k in range(1, YN):
-        target = lax.div(lax.rem(row + k, YN), 2)
+    for k in range(GYN):
+        target = lax.rem(gy + k, GYN)
+        if k:
+            copies.append(
+                remote(r.grad.at[pl.ds(target, 2)], r.gall.at[gy], r.gsend.at[k], r.grecv.at[k], device_at(0, k))
+            )
         copies.append(
-            remote(r.grad.at[pl.ds(target, 2)], r.gall.at[row], r.gsend.at[k], r.grecv.at[k], device_at(gx, row + k))
+            remote(r.zgrad, r.zall.at[gy], r.gsend.at[8 + k], r.grecv.at[8 + k], device_at(0, k, True))
         )
     return copies
 
 
 def rim_copies(r):
-    role, gx, gy, row = place_of()
-    copies = []
-    for k, device in enumerate(edge_targets()):
-        layer = 8 if k < 2 else 0
-        copies.append(remote(r.grad.at[layer], r.grim.at[row], r.esend.at[k], r.erecv.at[row], device))
-    return copies
+    gy = lax.axis_index("gy")
+    up, down, up_z, down_z = edge_targets()
+    return [
+        remote(r.grad.at[8], r.grim.at[gy], r.esend.at[0], r.erecv.at[gy], up),
+        remote(r.grad.at[0], r.grim.at[gy], r.esend.at[1], r.erecv.at[gy], down),
+        remote(r.zgrad, r.zrim.at[gy], r.esend.at[2], r.erecv.at[8 + gy], up_z),
+        remote(r.zgrad, r.zrim.at[gy], r.esend.at[3], r.erecv.at[8 + gy], down_z),
+    ]
 
 
 def gradient_stage(r):
-    role, gx, gy, row = place_of()
-    copies, rims = gradient_copies(r), rim_copies(r)
-    for copy in copies + rims:
+    gy = lax.axis_index("gy")
+    for copy in gradient_copies(r) + rim_copies(r):
         copy.start()
-    r.gall[row] = r.grad[pl.ds(gy, 2)]
-    for copy in copies:
+    r.gall[gy] = r.grad[pl.ds(gy, 2)]
+
+
+def gradient_end(r):
+    gy = lax.axis_index("gy")
+    for copy in gradient_copies(r):
         copy.wait()
-    for copy in rims:
+    for copy in rim_copies(r):
         copy.wait_send()
 
     @pl.when(jnp.logical_or(gy == 0, gy == 7))
     def _():
-        for k in range(YN):
-            remote(r.grad.at[1], r.grim.at[k], r.esend.at[0], r.erecv.at[k], partner()).wait_recv()
+        for k in range(GYN):
+            remote(r.zgrad, r.grim.at[k], r.esend.at[0], r.erecv.at[k], device_at(0, 0, True)).wait_recv()
+            remote(r.zgrad, r.zrim.at[k], r.esend.at[0], r.erecv.at[8 + k], device_at(0, 0, True)).wait_recv()
 
 
 def unpack_stage(r):
-    role = lax.axis_index("role")
-    back = parity_back(role)
-    spot = pl.ds(pl.multiple_of(8 * role, 8), 8)
+    back = parity_back()
     for q in range(3):
         even = [r.u[x // 2, x % 2, pl.ds(q, 8, stride=8)] for x in range(16)]
         odd = [r.u[x // 2, x % 2, pl.ds(4 + q, 8, stride=8)] for x in range(16)]
@@ -759,51 +866,56 @@
         for part in pieces_of(wide, 3):
             one = mul(part, back)
             total = one if total is None else total + one
-        r.disp[q, :, spot] = total[:, :LANES].reshape(16, 8, LANES)
-        r.give[q] = total[:, LANES:].reshape(16, 8, LANES)
-
-
-def give_copy(r):
-    role = lax.axis_index("role")
-    spot = pl.ds(pl.multiple_of(8 * role, 8), 8)
-    return remote(r.give, r.disp.at[:, :, spot], r.osend.at[0], r.orecv.at[0], partner())
-
-
-def give_stage(r):
-    give_copy(r).start()
-
-
-def given_stage(r):
-    give_copy(r).wait()
+        r.disp[q, :, 0:8] = total[:, :LANES].reshape(16, 8, LANES)
+        r.disp[q, :, 8:16] = total[:, LANES:].reshape(16, 8, LANES)
 
 
 def final_stage(r):
-    role, gx, gy, row = place_of()
-    for k in range(YN):
-        r.layers[0, 8 * k : 8 * k + 8] = r.gall[k, 0]
-        r.layers[1, 8 * k : 8 * k + 8] = r.gall[k, 0]
-        r.layers[2, 8 * k : 8 * k + 8] = r.gall[k, 1]
+    role, gx, gy = place_of()
+    for k in range(GYN):
+        rows = slice(8 * k, 8 * k + 8)
+        r.layers[0, rows] = r.gall[k, 0]
+        r.layers[1, rows] = r.gall[k, 0]
+        r.layers[2, rows] = r.gall[k, 1]
+        for layer in range(3):
+            r.zlayers[layer, rows] = r.zall[k]
 
     @pl.when(gy == 0)
     def _():
-        for k in range(YN):
+        for k in range(GYN):
             r.layers[0, 8 * k : 8 * k + 8] = r.grim[k]
+            r.zlayers[0, 8 * k : 8 * k + 8] = r.zrim[k]
 
     @pl.when(gy == 7)
     def _():
-        for k in range(YN):
+        for k in range(GYN):
             r.layers[2, 8 * k : 8 * k + 8] = r.grim[k]
-
-    rows = iota((LANES, 256), 0)
-    z = column_z(role, (LANES, 256), 1) + role * LANES
-    widen = jnp.logical_and(z >= 0, rows == lax.div(jnp.maximum(z, 0), 2)).astype(F32).astype(BF16)
-    widen = jnp.concatenate([widen, widen], axis=0)
-    rows, cols = iota((256, LANES), 0), iota((256, LANES), 1)
-    cols = cols - 8 * lax.div(rows, 16) - lax.div(lax.rem(rows, 16), 4)
+            r.zlayers[2, 8 * k : 8 * k + 8] = r.zrim[k]
+
+    pairs = (jnp.where(gy == 0, 8, gy), gy, jnp.where(gy == 7, 0, gy + 1))
+    rows, cols = iota((LANES, 256), 0), iota((LANES, 256), 1)
+    fine, beyond = cols < LANES, jnp.logical_and(cols >= LANES, cols < LANES + 2)
+
+    def twice(chosen):
+        chosen = chosen.astype(F32).astype(BF16)
+        return jnp.concatenate([chosen, chosen], axis=0)
+
+    widen = [twice(jnp.logical_and(fine, rows == 64 * h + lax.div(cols, 2))) for h in range(2)]
+    rows_y, cols_y = iota((256, LANES), 0), iota((256, LANES), 1)
+    wanted = lax.div(rows_y, 4) - 8 * lax.div(lax.rem(cols_y, 64), 8) - 4 * lax.div(cols_y, 64)
+    spot = lax.rem(cols_y, 8)
     for k in range(3):
-        repeat = (cols == (4 if k else 0)).astype(F32).astype(BF16)
+        wide = []
+        main = jnp.concatenate(pieces_of(r.layers[k], 2), axis=1)
+        side = jnp.concatenate(pieces_of(r.zlayers[k], 2), axis=1)
+        for h in range(2):
+            reach_out = twice(jnp.logical_and(beyond, rows == 64 * h + pairs[k]))
+            wide.append(mul(main, widen[h]) + mul(side, reach_out))
+        wide = jnp.concatenate(wide, axis=0)
+        first = 4 if k else 0
+        inside = jnp.logical_and(spot >= first, spot < first + 4)
+        repeat = jnp.logical_and(inside, wanted == spot - first).astype(F32).astype(BF16)
         repeat = jnp.concatenate([repeat, repeat], axis=1)
-        wide = mul(jnp.concatenate(pieces_of(r.layers[k], 2), axis=1), widen)
         r.wide[k] = mul(repeat, jnp.concatenate(pieces_of(wide, 2), axis=0))
     band = hat_of(iota((256, LANES), 1) - column_z(role, (256, LANES), 0)).astype(BF16)
     bands = jnp.concatenate([band, band], axis=0)
@@ -835,6 +947,7 @@
 
 FIELD = (9, 2, 80, LANES)
 TILE = (1, LANES)
+TOP = (18, 8, LANES)
 
 
 class Refs(dict):
@@ -845,56 +958,58 @@
 def buffers():
     shapes = {
         "edge": (8, 1024), "lo": (4, 256, LANES), "hi": (4, 256, LANES), "edges": (3, 8, 1024),
-        "force_other": (3, 16, 8, LANES), "m": (8, 256, 256), "zc": (8, 272, 256), "psum": (256, LANES),
-        "dens": (YN, 8, LANES), "vf": (2, 8, 2, 64, LANES), "nxhi": (2, 64, LANES), "nyhi": (2, 8, 2, 8, LANES),
-        "ncorner": (2, 8, LANES), "dall": (YN, 8, LANES), "rho": (8, 8, LANES), "store": (9, 5, 7, 8, LANES),
-        "acc": (9, 5, 7, 8, LANES), "grad": (9, 8, LANES), "gall": (YN, 2, 8, LANES), "grim": (YN, 8, LANES),
-        "give": (3, 16, 8, LANES), "layers": (3, LANES, LANES), "wide": (3, 256, 256),
+        "m": (8, 256, 256), "zc": (8, 272, 256), "psum": (256, LANES),
+        "dens": (GYN, 8, LANES), "vf": (2, 8, 2, 64, LANES), "nxhi": (2, 64, LANES), "nyhi": (2, 8, 2, 8, LANES),
+        "ncorner": (2, 8, LANES), "bottom": (2,) + TOP, "nbottom": (2,) + TOP, "dall": (GYN, 8, LANES),
+        "rho": (8, 8, LANES), "store": (9, 5, 7, 8, LANES), "acc": (9, 5, 7, 8, LANES), "grad": (9, 8, LANES),
+        "zgrad": (8, LANES), "gall": (GYN, 2, 8, LANES), "grim": (GYN, 8, LANES), "zall": (GYN, 8, LANES),
+        "zrim": (GYN, 8, LANES), "layers": (3, 64, LANES), "zlayers": (3, 64, LANES), "wide": (3, 256, 256),
     }
     for name in ("r0", "free", "s0", "r1", "p1", "u1", "r2", "u", "work"):
         shapes[name] = FIELD
+        shapes[name + "t"] = TOP
     for n in range(3):
         shapes["tile", n] = shapes["sum", n] = shapes["half", n] = TILE
         shapes["slots", n] = (24, 1, LANES)
     for n in range(2):
         shapes["image", n] = FIELD
+        shapes["imaget", n] = shapes["lift", n] = shapes["lifted", n] = TOP
+        shapes["trow", n] = (2, 8, LANES)
+        shapes["tface", n] = (8, 8, LANES)
         shapes["xlo", n] = shapes["xhi", n] = (80, LANES)
         shapes["ylo", n] = shapes["yhi", n] = (9, 2, 8, LANES)
         shapes["corners", n] = (4, 8, LANES)
     scratch = {name: pltpu.VMEM(shape, F32) for name, shape in shapes.items()}
-    scratch["relay"] = pltpu.VMEM((3, 16, 8, LANES), I32)
-    scratch["mask_other"] = pltpu.VMEM((3, 16, 8, LANES), I32)
     scratch["stiff"] = pltpu.VMEM((2 * ROWS, 2 * ROWS), BF16)
-    counts = {"dsend": 14, "drecv": 14, "nsend": 19, "nrecv": 19, "gsend": 16, "grecv": 16, "esend": 4, "erecv": 16,
-              "osend": 1, "orecv": 1}
+    counts = {"dsend": 7, "drecv": 7, "nsend": 12, "nrecv": 12, "gsend": 16, "grecv": 16, "esend": 4, "erecv": 16}
     for n in range(3):
         counts["rsend", n] = counts["rrecv", n] = 2
-        counts["fsend", n] = counts["frecv", n] = 8
+        counts["fsend", n] = counts["frecv", n] = 16
+        counts["zsend", n] = counts["zrecv", n] = 1
     for name, count in counts.items():
         scratch[name] = pltpu.SemaphoreType.DMA((count,))
     return scratch
 
 
 def greet_all():
-    role, gx, gy, row = place_of()
+    gx, gy = lax.axis_index("gx"), lax.axis_index("gy")
     barrier = pltpu.get_barrier_semaphore()
-    devices = [device_at(gx, row + k) for k in range(1, YN)]
+    devices = [device_at(0, k) for k in range(1, GYN)]
+    devices += [device_at(0, k, True) for k in range(1, GYN)]
     devices += [cross_device(k) for k in range(1, 16)]
-    devices += [device_at(gx + dx, row + dy) for dx, dy in FACE_MOVES[4:]]
+    devices += [device_at(dx, dy) for dx, dy in FACE_MOVES[4:]]
     devices += [slab_device(shift, other) for shift, other in ((1, False), (-1, False), (1, True), (-1, True))]
-    devices += [z_neighbour(True), z_neighbour(False), device_at(gx + 1, row), device_at(gx - 1, row)]
     for device in devices:
         pl.semaphore_signal(barrier, inc=1, device_id=device, device_id_type=MESH)
 
-    @pl.when(gy == 0)
-    def _():
-        for k in range(YN):
-            pl.semaphore_signal(barrier, inc=1, device_id=device_at(gx - 1, row * 0 + k), device_id_type=MESH)
-
-    @pl.when(gy == 7)
-    def _():
-        for k in range(YN):
-            pl.semaphore_signal(barrier, inc=1, device_id=device_at(gx + 1, row * 0 + k), device_id_type=MESH)
+    for last, dx in ((0, -1), (7, 1)):
+
+        @pl.when(gy == last)
+        def _():
+            for k in range(GYN):
+                for other in (False, True):
+                    device = dict(device_at(dx, 0, other), gy=k)
+                    pl.semaphore_signal(barrier, inc=1, device_id=device, device_id_type=MESH)
 
     return len(devices) + 4
 
@@ -903,14 +1018,13 @@
     r = Refs(zip(names, refs))
     count = greet_all()
     edge_stage(r)
+    pack_stage(r)
     pl.semaphore_wait(pltpu.get_barrier_semaphore(), count)
     swap_stage(r)
     inner_stage(r)
     spread_stage(r)
-    pack_stage(r)
-    upper_stage(r)
     outer_stage(r)
-    frame_stage(r)
+    top_stage(r)
     first_stage(r)
     face_stage(r, 0)
     second_stage(r)
@@ -920,9 +1034,8 @@
     last_stage(r)
     gradient_stage(r)
     unpack_stage(r)
-    give_stage(r)
+    gradient_end(r)
     final_stage(r)
-    given_stage(r)
 
 
 def on_device(design, force, clamped_dof_mask, stiffness):

time: 97.7 us -> 85 us (0.87)
  Pallas kernels: 90.4 us -> 77.9 us
    pallas_call x1, Pallas kernels: 90.4 us -> 77.9 us  [on_device(): pl.pallas_call(functools.partial(whole_kernel, names), out_shape=(jax.Sha...]
where the time goes in v4:
time: 85 us; the launch traced here: 84.7 us
  Pallas kernels  77.9 us (92%)
  local copies, waits for them, and re-layouts  6.17 us (7%)
    pallas_call x1, Pallas kernels, on_device(): pl.pallas_call(functools.partial(whole_kernel, names), out_shape=(jax.Sha...  77.9 us
    unnamed x12, local copies, waits for them, and re-layouts  6.17 us

profile of v4, /device:TPU:1, one launch (start us, length us, event | category | flops | bytes accessed | tf_op | source)
XLA Modules:
  0.0 84.7 jit_solution(8258920236836217414)
XLA Ops:
  0.6 0.0 copy-start
  0.6 1.0 %copy-done = f32[4,256,128]{2,1,0:T(8,128)S(1)} copy-done((f32[4,256,128]{2,1,0:T(8,128)S(1)}, f32[4,256,128]{2,1,0:T(8,128)}, u32[]{:S(2)}) %copy-start) | copy-done | bytes 524312
  1.7 0.0 copy-start.1
  1.7 1.0 %copy-done.1 = f32[3,16,16,128]{3,2,1,0:T(8,128)S(1)} copy-done((f32[3,16,16,128]{3,2,1,0:T(8,128)S(1)}, f32[3,16,16,128]{3,2,1,0:T(8,128)}, u32[]{:S(2)}) %copy-start.1) | copy-done | bytes 393240
  2.7 0.0 copy-start.2
  2.7 1.0 %copy-done.2 = s32[3,16,16,128]{3,2,1,0:T(8,128)S(1)} copy-done((s32[3,16,16,128]{3,2,1,0:T(8,128)S(1)}, s32[3,16,16,128]{3,2,1,0:T(8,128)}, u32[]{:S(2)}) %copy-start.2) | copy-done | bytes 393240
  3.7 0.0 copy-start.3
  3.7 0.8 copy-done.3
  4.5 0.0 copy-start.4
  4.5 0.8 copy-done.4
  5.3 77.9 %compliance.1 = (f32[4,256,128]{2,1,0:T(8,128)S(1)}, f32[3,16,16,128]{3,2,1,0:T(8,128)S(1)}) custom-call(f32[4,256,128]{2,1,0:T(8,128)S(1)} %copy-done, f32[3,16,16,128]{3,2,1,0:T(8,128)S(1)} %copy-done.1, s32[3,16,16,128]{3,2,1,0:T(8,128)S(1)} %copy-done.2, f32[81,81]{1,0:T(8,128)S(1)} %copy-done.4, f32[112,81]{1,0:T(8,128)S(1)} %copy-done.3), custom_call_target="tpu_custom_call" | custom-call | tf_op jit(solution)/shard_map/compliance/pallas_call | solution.py:1046
  83.1 0.8 copy.9
  83.9 0.7 copy.10
Async XLA Ops:
  0.6 1.0 %copy-start = (f32[4,256,128]{2,1,0:T(8,128)S(1)}, f32[4,256,128]{2,1,0:T(8,128)}, u32[]{:S(2)}) copy-start(f32[4,256,128]{2,1,0:T(8,128)} %refs_0_.1) | copy-start | bytes 1572868
  1.7 1.0 %copy-start.1 = (f32[3,16,16,128]{3,2,1,0:T(8,128)S(1)}, f32[3,16,16,128]{3,2,1,0:T(8,128)}, u32[]{:S(2)}) copy-start(f32[3,16,16,128]{3,2,1,0:T(8,128)} %refs_1_.1) | copy-start | bytes 1179652
  2.7 1.0 %copy-start.2 = (s32[3,16,16,128]{3,2,1,0:T(8,128)S(1)}, s32[3,16,16,128]{3,2,1,0:T(8,128)}, u32[]{:S(2)}) copy-start(s32[3,16,16,128]{3,2,1,0:T(8,128)} %refs_2_.1) | copy-start | bytes 1179652
  3.7 0.8 copy-start.3
  4.5 0.8 copy-start.4

commit v5 on v4

--- a/solution.py
+++ b/solution.py
@@ -138,13 +138,15 @@
 def edge_stage(r):
     role = lax.axis_index("role")
     rows, cols = iota((16, LANES), 0), iota((16, LANES), 1)
-    chosen = jnp.where(role == 0, 124 + rows, rows)
-    chosen = jnp.logical_and(cols == chosen, rows < 4).astype(F32).astype(BF16)
-    for x in range(4):
+    first = jnp.where(role == 0, 124, 0)
+    for x in range(2):
         total = None
-        for part in pieces_of(r.design[x], 2):
-            one = lax.dot_general(chosen, part, (((1,), (1,)), ((), ())), preferred_element_type=F32)
-            total = one if total is None else total + one
+        for k in range(2):
+            inside = jnp.logical_and(rows >= 4 * k, rows < 4 * k + 4)
+            chosen = jnp.logical_and(cols == first + rows - 4 * k, inside).astype(F32).astype(BF16)
+            for part in pieces_of(r.design[x + 2 * k], 2):
+                one = lax.dot_general(chosen, part, (((1,), (1,)), ((), ())), preferred_element_type=F32)
+                total = one if total is None else total + one
         r.edge[:, 256 * x : 256 * x + 256] = total[:8]
 
 
@@ -166,7 +168,7 @@
 
 
 def swap_stage(r):
-    for copy in near_copies(r) + upper_copies(r) + far_copies(r):
+    for copy in near_copies(r) + upper_copies(r):
         copy.start()
     table_stage(r)
     for copy in upper_copies(r):
@@ -214,8 +216,12 @@
         ref = (r.lo, r.design, r.hi)[p // 4]
         return ref[p % 4, rows]
 
+    def edge_plane(p):
+        held = r.edges[p // 4, :, 256 * (p % 2) : 256 * (p % 2) + 256]
+        return pltpu.roll(held, 4, 0) if p % 4 > 1 else held
+
     for i in planes:
-        beyond = mix(lambda k: r.edges[(i + k) // 4, :, 256 * ((i + k) % 4) : 256 * ((i + k) % 4) + 256])
+        beyond = mix(lambda k: edge_plane(i + k))
         beyond = jnp.concatenate(pieces_of(beyond, 2), axis=0)
         beyond = lax.dot_general(beyond, rim, (((0,), (0,)), ((), ())), preferred_element_type=F32)
         for b in range(4):
@@ -259,12 +265,12 @@
     @pl.when(slab == 0)
     def _():
         r.lo[2:4] = jnp.zeros((2, 256, LANES), F32)
-        r.edges[0] = jnp.zeros((8, 1024), F32)
+        r.edges[0] = jnp.zeros((8, 512), F32)
 
     @pl.when(slab == 63)
     def _():
         r.hi[0:2] = jnp.zeros((2, 256, LANES), F32)
-        r.edges[2] = jnp.zeros((8, 1024), F32)
+        r.edges[2] = jnp.zeros((8, 512), F32)
 
     taps_stage(r, (2, 3, 4, 5))
     r.psum[...] = jnp.zeros_like(r.psum)
@@ -348,12 +354,14 @@
 
 
 def bottom_copy(r):
-    return remote(r.bottom, r.nbottom, r.nsend.at[11], r.nrecv.at[11], device_at(0, 0, True))
+    return remote(r.packed, r.npacked, r.nsend.at[11], r.nrecv.at[11], device_at(0, 0, True))
 
 
 def spread_stage(r):
     gy = lax.axis_index("gy")
     for copy in density_copies(r):
+        copy.start()
+    for copy in far_copies(r):
         copy.start()
     r.dall[gy] = r.dens[gy]
 
@@ -383,6 +391,7 @@
         ref[8, 0, 72:80] = jnp.zeros((8, LANES), F32)
         ref[8, 1] = jnp.zeros((80, LANES), F32)
         pack_bottom(ref, r.bottom.at[kind])
+    compress(lambda x: r.bottom[0, x] + pltpu.roll(r.bottom[1, x], 4, 0), r.packed)
 
 
 def pack_bottom(field, out):
@@ -401,6 +410,24 @@
     lax.fori_loop(0, 9, body, 0)
 
 
+def compress(tiles, out):
+    lane = lax.div(lax.rem(iota((8, LANES), 1), 64), 9)
+    for group in range(3):
+        total = jnp.zeros((8, LANES), F32)
+        for m in range(7):
+            x = 7 * group + m
+            if x < 17:
+                held = tiles(x)
+                total = jnp.where(lane == m, pltpu.roll(held, 9 * m, 1) if m else held, total)
+        out[group] = total
+
+
+def expand(packed, x):
+    held, m = packed[x // 7], x % 7
+    held = pltpu.roll(held, LANES - 9 * m, 1) if m else held
+    return jnp.where(lax.rem(iota((8, LANES), 1), 64) < 9, held, 0.0)
+
+
 def add_bottom(field, tiles):
     keep = jnp.logical_and(iota((8, LANES), 0) < 4, lax.rem(iota((8, LANES), 1), 64) == 0)
 
@@ -418,8 +445,13 @@
 def top_stage(r):
     role = lax.axis_index("role")
     bottom_copy(r).wait()
-    for kind, ref in ((0, r.r0t), (1, r.freet)):
-        ref[...] = jnp.where(role == 0, r.nbottom[kind], 0.0)
+    keep = jnp.logical_and(iota((8, LANES), 0) < 4, role == 0)
+    for x in range(17):
+        held = expand(r.npacked, x)
+        r.r0t[x] = jnp.where(keep, held, 0.0)
+        r.freet[x] = jnp.where(keep, pltpu.roll(held, 4, 0), 0.0)
+    r.r0t[17] = jnp.zeros((8, LANES), F32)
+    r.freet[17] = jnp.zeros((8, LANES), F32)
     for copy in density_copies(r):
         copy.wait()
 
@@ -469,7 +501,8 @@
     return floor_stiff + (1.0 - floor_stiff) * (rho * rho * rho)
 
 
-def apply_operator(r, image, top):
+def apply_operator(r, n, gamma):
+    image, top = r["image", n], r["imaget", n]
     store, acc = r.store, r.acc
     acc[...] = jnp.zeros_like(acc)
     stiff = r.stiff[...]
@@ -485,6 +518,8 @@
         return energy
 
     energy = lax.fori_loop(0, 8, body, jnp.zeros((8, LANES), F32))
+    r["tile", n][...] = sums_tile(gamma, energy)
+    reduce_start(r, n)
     sub, lane = iota((8, LANES), 0) < 4, lax.rem(iota((8, LANES), 1), 64)
     keep = jnp.logical_and(sub, lane > 0)
 
@@ -504,7 +539,6 @@
         return 0
 
     lax.fori_loop(0, 9, fold, 0)
-    return energy
 
 
 def element_energy(r):
@@ -613,7 +647,6 @@
 def face_stage(r, n):
     role = lax.axis_index("role")
     image, top, lift = r["image", n], r["imaget", n], r["lift", n]
-    reduce_start(r, n)
 
     @pl.when(role == 0)
     def _():
@@ -623,18 +656,23 @@
     def _():
         pack_bottom(image, lift)
 
-    across = remote(lift, r["lifted", n], r["zsend", n].at[0], r["zrecv", n].at[0], device_at(0, 0, True))
+    compress(lambda x: lift[x], r["packed", n])
+    across = remote(r["packed", n], r["lifted", n], r["zsend", n].at[0], r["zrecv", n].at[0], device_at(0, 0, True))
     across.start()
     reduce_middle(r, n)
     across.wait()
 
+    for x in range(17):
+        lift[x] = expand(r["lifted", n], x)
+    lift[17] = jnp.zeros((8, LANES), F32)
+
     @pl.when(role == 0)
     def _():
-        top[...] += r["lifted", n][...]
+        top[...] += lift[...]
 
     @pl.when(role == 1)
     def _():
-        add_bottom(image, r["lifted", n])
+        add_bottom(image, lift)
 
     lane = iota((8, LANES), 1)
     below, above = jnp.zeros((8, LANES), F32), jnp.zeros((8, LANES), F32)
@@ -647,6 +685,8 @@
     copies = face_copies(r, n)
     for copy in copies:
         copy.start()
+    if n == 0:
+        outer_stage(r)
     reduce_end(r, n)
     for copy in copies:
         copy.wait()
@@ -707,8 +747,7 @@
     for e in range(8):
         r.rho[e] = r.dall[e]
     build_store(r.r0, r.r0t, r.store)
-    delta = apply_operator(r, r["image", 0], r["imaget", 0])
-    r["tile", 0][...] = sums_tile(square_sum(r.r0), delta)
+    apply_operator(r, 0, square_sum(r.r0))
 
 
 def second_stage(r):
@@ -722,8 +761,7 @@
     over_nodes(update)
     r.r1t[...] = r.r0t[...] - alpha * r.s0t[...]
     build_store(r.r1, r.r1t, r.store)
-    delta = apply_operator(r, r["image", 1], r["imaget", 1])
-    r["tile", 1][...] = sums_tile(square_sum(r.r1), delta)
+    apply_operator(r, 1, square_sum(r.r1))
 
 
 def third_stage(r):
@@ -957,10 +995,10 @@
 
 def buffers():
     shapes = {
-        "edge": (8, 1024), "lo": (4, 256, LANES), "hi": (4, 256, LANES), "edges": (3, 8, 1024),
+        "edge": (8, 512), "lo": (4, 256, LANES), "hi": (4, 256, LANES), "edges": (3, 8, 512),
         "m": (8, 256, 256), "zc": (8, 272, 256), "psum": (256, LANES),
         "dens": (GYN, 8, LANES), "vf": (2, 8, 2, 64, LANES), "nxhi": (2, 64, LANES), "nyhi": (2, 8, 2, 8, LANES),
-        "ncorner": (2, 8, LANES), "bottom": (2,) + TOP, "nbottom": (2,) + TOP, "dall": (GYN, 8, LANES),
+        "ncorner": (2, 8, LANES), "bottom": (2,) + TOP, "packed": (3, 8, LANES), "npacked": (3, 8, LANES), "dall": (GYN, 8, LANES),
         "rho": (8, 8, LANES), "store": (9, 5, 7, 8, LANES), "acc": (9, 5, 7, 8, LANES), "grad": (9, 8, LANES),
         "zgrad": (8, LANES), "gall": (GYN, 2, 8, LANES), "grim": (GYN, 8, LANES), "zall": (GYN, 8, LANES),
         "zrim": (GYN, 8, LANES), "layers": (3, 64, LANES), "zlayers": (3, 64, LANES), "wide": (3, 256, 256),
@@ -973,7 +1011,8 @@
         shapes["slots", n] = (24, 1, LANES)
     for n in range(2):
         shapes["image", n] = FIELD
-        shapes["imaget", n] = shapes["lift", n] = shapes["lifted", n] = TOP
+        shapes["imaget", n] = shapes["lift", n] = TOP
+        shapes["packed", n] = shapes["lifted", n] = (3, 8, LANES)
         shapes["trow", n] = (2, 8, LANES)
         shapes["tface", n] = (8, 8, LANES)
         shapes["xlo", n] = shapes["xhi", n] = (80, LANES)
@@ -992,26 +1031,15 @@
 
 
 def greet_all():
-    gx, gy = lax.axis_index("gx"), lax.axis_index("gy")
     barrier = pltpu.get_barrier_semaphore()
     devices = [device_at(0, k) for k in range(1, GYN)]
-    devices += [device_at(0, k, True) for k in range(1, GYN)]
     devices += [cross_device(k) for k in range(1, 16)]
     devices += [device_at(dx, dy) for dx, dy in FACE_MOVES[4:]]
     devices += [slab_device(shift, other) for shift, other in ((1, False), (-1, False), (1, True), (-1, True))]
     for device in devices:
         pl.semaphore_signal(barrier, inc=1, device_id=device, device_id_type=MESH)
 
-    for last, dx in ((0, -1), (7, 1)):
-
-        @pl.when(gy == last)
-        def _():
-            for k in range(GYN):
-                for other in (False, True):
-                    device = dict(device_at(dx, 0, other), gy=k)
-                    pl.semaphore_signal(barrier, inc=1, device_id=device, device_id_type=MESH)
-
-    return len(devices) + 4
+    return len(devices)
 
 
 def whole_kernel(names, *refs):
@@ -1023,7 +1051,6 @@
     swap_stage(r)
     inner_stage(r)
     spread_stage(r)
-    outer_stage(r)
     top_stage(r)
     first_stage(r)
     face_stage(r, 0)

time: 85 us -> 82.9 us (0.975)
  Pallas kernels: 77.9 us -> 75.8 us
    pallas_call x1, Pallas kernels: 77.9 us -> 75.8 us  [on_device(): pl.pallas_call(functools.partial(whole_kernel, names), out_shape=(jax.Sha...]
where the time goes in v5:
time: 82.9 us; the launch traced here: 82.6 us
  Pallas kernels  75.8 us (91%)
  local copies, waits for them, and re-layouts  6.17 us (7%)
    pallas_call x1, Pallas kernels, on_device(): pl.pallas_call(functools.partial(whole_kernel, names), out_shape=(jax.Sha...  75.8 us
    unnamed x12, local copies, waits for them, and re-layouts  6.17 us

profile of v5, /device:TPU:1, one launch (start us, length us, event | category | flops | bytes accessed | tf_op | source)
XLA Modules:
  0.0 82.6 jit_solution(5153883296691129234)
XLA Ops:
  0.6 0.0 copy-start
  0.6 1.0 %copy-done = f32[4,256,128]{2,1,0:T(8,128)S(1)} copy-done((f32[4,256,128]{2,1,0:T(8,128)S(1)}, f32[4,256,128]{2,1,0:T(8,128)}, u32[]{:S(2)}) %copy-start) | copy-done | bytes 524312
  1.7 0.0 copy-start.1
  1.7 1.0 %copy-done.1 = f32[3,16,16,128]{3,2,1,0:T(8,128)S(1)} copy-done((f32[3,16,16,128]{3,2,1,0:T(8,128)S(1)}, f32[3,16,16,128]{3,2,1,0:T(8,128)}, u32[]{:S(2)}) %copy-start.1) | copy-done | bytes 393240
  2.7 0.0 copy-start.2
  2.7 1.0 %copy-done.2 = s32[3,16,16,128]{3,2,1,0:T(8,128)S(1)} copy-done((s32[3,16,16,128]{3,2,1,0:T(8,128)S(1)}, s32[3,16,16,128]{3,2,1,0:T(8,128)}, u32[]{:S(2)}) %copy-start.2) | copy-done | bytes 393240
  3.7 0.0 copy-start.3
  3.7 0.8 copy-done.3
  4.5 0.0 copy-start.4
  4.5 0.8 copy-done.4
  5.3 75.8 %compliance.1 = (f32[4,256,128]{2,1,0:T(8,128)S(1)}, f32[3,16,16,128]{3,2,1,0:T(8,128)S(1)}) custom-call(f32[4,256,128]{2,1,0:T(8,128)S(1)} %copy-done, f32[3,16,16,128]{3,2,1,0:T(8,128)S(1)} %copy-done.1, s32[3,16,16,128]{3,2,1,0:T(8,128)S(1)} %copy-done.2, f32[81,81]{1,0:T(8,128)S(1)} %copy-done.4, f32[112,81]{1,0:T(8,128)S(1)} %copy-done.3), custom_call_target="tpu_custom_call" | custom-call | tf_op jit(solution)/shard_map/compliance/pallas_call | solution.py:1073
  81.1 0.8 copy.9
  81.8 0.7 copy.10
Async XLA Ops:
  0.6 1.0 %copy-start = (f32[4,256,128]{2,1,0:T(8,128)S(1)}, f32[4,256,128]{2,1,0:T(8,128)}, u32[]{:S(2)}) copy-start(f32[4,256,128]{2,1,0:T(8,128)} %refs_0_.1) | copy-start | bytes 1572868
  1.7 1.0 %copy-start.1 = (f32[3,16,16,128]{3,2,1,0:T(8,128)S(1)}, f32[3,16,16,128]{3,2,1,0:T(8,128)}, u32[]{:S(2)}) copy-start(f32[3,16,16,128]{3,2,1,0:T(8,128)} %refs_1_.1) | copy-start | bytes 1179652
  2.7 1.0 %copy-start.2 = (s32[3,16,16,128]{3,2,1,0:T(8,128)S(1)}, s32[3,16,16,128]{3,2,1,0:T(8,128)}, u32[]{:S(2)}) copy-start(s32[3,16,16,128]{3,2,1,0:T(8,128)} %refs_2_.1) | copy-start | bytes 1179652
  3.7 0.8 copy-start.3
  4.5 0.8 copy-start.4

commit v6 on v5

--- a/solution.py
+++ b/solution.py
@@ -428,7 +428,7 @@
     return jnp.where(lax.rem(iota((8, LANES), 1), 64) < 9, held, 0.0)
 
 
-def add_bottom(field, tiles):
+def set_bottom(field, tiles):
     keep = jnp.logical_and(iota((8, LANES), 0) < 4, lax.rem(iota((8, LANES), 1), 64) == 0)
 
     def body(e, _):
@@ -436,7 +436,8 @@
             tile = tiles[2 * e + px]
             for j in range(LAST):
                 moved = pltpu.roll(tile, LANES - j, 1) if j else tile
-                field[e, px, 8 * j : 8 * j + 8] += jnp.where(keep, moved, 0.0)
+                spot = slice(8 * j, 8 * j + 8)
+                field[e, px, spot] = jnp.where(keep, moved, field[e, px, spot])
         return 0
 
     lax.fori_loop(0, 9, body, 0)
@@ -624,7 +625,7 @@
 
 
 def face_copies(r, n):
-    image, corners, top, rows = r["image", n], r["corners", n], r["imaget", n], r["trow", n]
+    image, corners = r["image", n], r["corners", n]
     ends = (
         (image.at[8, 0], r["xlo", n]),
         (image.at[0, 0], r["xhi", n]),
@@ -635,18 +636,32 @@
         (image.at[0, 0, 64:72], corners.at[2]),
         (image.at[0, 0, 0:8], corners.at[3]),
     )
-    tops = (top.at[16], top.at[0], rows.at[1], rows.at[0], rows.at[1], rows.at[0], rows.at[1], rows.at[0])
     send, recv = r["fsend", n], r["frecv", n]
-    copies = []
-    for k, ((dx, dy), (src, dst)) in enumerate(zip(FACE_MOVES, ends)):
-        copies.append(remote(src, dst, send.at[k], recv.at[k], device_at(dx, dy)))
-        copies.append(remote(tops[k], r["tface", n].at[k], send.at[8 + k], recv.at[8 + k], device_at(dx, dy)))
+    return [
+        remote(src, dst, send.at[k], recv.at[k], device_at(dx, dy))
+        for k, ((dx, dy), (src, dst)) in enumerate(zip(FACE_MOVES, ends))
+    ]
+
+
+def plane_copies(r, n):
+    lift, rows, send, recv = r["lift", n], r["trow", n], r["zsend", n], r["zrecv", n]
+    tiles = (lift.at[16], lift.at[0], rows.at[1], rows.at[0], rows.at[1], rows.at[0], rows.at[1], rows.at[0])
+    copies = [remote(r["packed", n], r["lifted", n], send.at[16], recv.at[16], device_at(0, 0, True))]
+    for k, (dx, dy) in enumerate(FACE_MOVES):
+        for other in range(2):
+            m = 2 * k + other
+            copies.append(
+                remote(tiles[k], r["tface", n].at[m], send.at[m], recv.at[m], device_at(dx, dy, other == 1))
+            )
     return copies
 
 
 def face_stage(r, n):
     role = lax.axis_index("role")
     image, top, lift = r["image", n], r["imaget", n], r["lift", n]
+    faces = face_copies(r, n)
+    for copy in faces:
+        copy.start()
 
     @pl.when(role == 0)
     def _():
@@ -657,45 +672,31 @@
         pack_bottom(image, lift)
 
     compress(lambda x: lift[x], r["packed", n])
-    across = remote(r["packed", n], r["lifted", n], r["zsend", n].at[0], r["zrecv", n].at[0], device_at(0, 0, True))
-    across.start()
-    reduce_middle(r, n)
-    across.wait()
-
-    for x in range(17):
-        lift[x] = expand(r["lifted", n], x)
-    lift[17] = jnp.zeros((8, LANES), F32)
-
-    @pl.when(role == 0)
-    def _():
-        top[...] += lift[...]
-
-    @pl.when(role == 1)
-    def _():
-        add_bottom(image, lift)
-
     lane = iota((8, LANES), 1)
     below, above = jnp.zeros((8, LANES), F32), jnp.zeros((8, LANES), F32)
     for x in range(17):
-        tile = top[x]
+        tile = lift[x]
         below = jnp.where(lane == x, pltpu.roll(tile, x, 1) if x else tile, below)
         above = jnp.where(lane == x, pltpu.roll(tile, 56 + x, 1), above)
     r["trow", n][0] = below
     r["trow", n][1] = above
-    copies = face_copies(r, n)
-    for copy in copies:
+    planes = plane_copies(r, n)
+    for copy in planes:
         copy.start()
+    reduce_middle(r, n)
     if n == 0:
         outer_stage(r)
     reduce_end(r, n)
-    for copy in copies:
+    for copy in faces + planes:
         copy.wait()
 
 
 def add_faces(r, n, work, workt):
     role, gx, gy = place_of()
     low_x, low_y = gx > 0, gy > 0
-    image, corners, top, tface = r["image", n], r["corners", n], r["imaget", n], r["tface", n]
+    image, corners = r["image", n], r["corners", n]
+    lift, lifted, edges = r["lift", n], r["lifted", n], r["tface", n]
+    tface = [edges[2 * k] + edges[2 * k + 1] for k in range(8)]
     xlo, xhi, ylo, yhi = (r[name, n] for name in ("xlo", "xhi", "ylo", "yhi"))
     low = low_lanes()
 
@@ -714,7 +715,6 @@
         for p in range(2):
             if e or p:
                 join(e, p, ylo[e, p], yhi[e, p])
-    work[...] = work[...] * r.free[...]
 
     lane = iota((8, LANES), 1)
 
@@ -726,7 +726,7 @@
     below = jnp.where(low_y, row_of(tface[2], tface[4], tface[6]), 0.0)
     above = row_of(tface[3], tface[5], tface[7])
     for x in range(17):
-        tile = top[x]
+        tile = lift[x] + expand(lifted, x)
         if x == 0:
             tile = tile + jnp.where(low_x, tface[0], 0.0)
         if x == 16:
@@ -735,8 +735,15 @@
         total = total + jnp.where(lane == 8, pltpu.roll(tile, 72, 1), 0.0)
         total = total + jnp.where(lane == 0, pltpu.roll(below, LANES - x, 1) if x else below, 0.0)
         total = total + jnp.where(lane == 72, pltpu.roll(above, 72 - x, 1), 0.0)
-        workt[x] = total * r.freet[x]
+        workt[x] = total
     workt[17] = jnp.zeros((8, LANES), F32)
+
+    @pl.when(role == 1)
+    def _():
+        set_bottom(work, workt)
+
+    work[...] = work[...] * r.free[...]
+    workt[...] = workt[...] * r.freet[...]
 
 
 def spare(value):
@@ -1014,7 +1021,7 @@
         shapes["imaget", n] = shapes["lift", n] = TOP
         shapes["packed", n] = shapes["lifted", n] = (3, 8, LANES)
         shapes["trow", n] = (2, 8, LANES)
-        shapes["tface", n] = (8, 8, LANES)
+        shapes["tface", n] = (16, 8, LANES)
         shapes["xlo", n] = shapes["xhi", n] = (80, LANES)
         shapes["ylo", n] = shapes["yhi", n] = (9, 2, 8, LANES)
         shapes["corners", n] = (4, 8, LANES)
@@ -1023,8 +1030,8 @@
     counts = {"dsend": 7, "drecv": 7, "nsend": 12, "nrecv": 12, "gsend": 16, "grecv": 16, "esend": 4, "erecv": 16}
     for n in range(3):
         counts["rsend", n] = counts["rrecv", n] = 2
-        counts["fsend", n] = counts["frecv", n] = 16
-        counts["zsend", n] = counts["zrecv", n] = 1
+        counts["fsend", n] = counts["frecv", n] = 8
+        counts["zsend", n] = counts["zrecv", n] = 17
     for name, count in counts.items():
         scratch[name] = pltpu.SemaphoreType.DMA((count,))
     return scratch

time: 82.9 us -> 79.1 us (0.954)
  Pallas kernels: 75.8 us -> 72 us
    pallas_call x1, Pallas kernels: 75.8 us -> 72 us  [on_device(): pl.pallas_call(functools.partial(whole_kernel, names), out_shape=(jax.Sha...]
where the time goes in v6:
time: 79.1 us; the launch traced here: 78.8 us
  Pallas kernels  72 us (91%)
  local copies, waits for them, and re-layouts  6.17 us (8%)
    pallas_call x1, Pallas kernels, on_device(): pl.pallas_call(functools.partial(whole_kernel, names), out_shape=(jax.Sha...  72 us
    unnamed x12, local copies, waits for them, and re-layouts  6.17 us

profile of v6, /device:TPU:1, one launch (start us, length us, event | category | flops | bytes accessed | tf_op | source)
XLA Modules:
  0.0 78.8 jit_solution(3728559489250061362)
XLA Ops:
  0.6 0.0 copy-start
  0.6 1.0 %copy-done = f32[4,256,128]{2,1,0:T(8,128)S(1)} copy-done((f32[4,256,128]{2,1,0:T(8,128)S(1)}, f32[4,256,128]{2,1,0:T(8,128)}, u32[]{:S(2)}) %copy-start) | copy-done | bytes 524312
  1.7 0.0 copy-start.1
  1.7 1.0 %copy-done.1 = f32[3,16,16,128]{3,2,1,0:T(8,128)S(1)} copy-done((f32[3,16,16,128]{3,2,1,0:T(8,128)S(1)}, f32[3,16,16,128]{3,2,1,0:T(8,128)}, u32[]{:S(2)}) %copy-start.1) | copy-done | bytes 393240
  2.7 0.0 copy-start.2
  2.7 1.0 %copy-done.2 = s32[3,16,16,128]{3,2,1,0:T(8,128)S(1)} copy-done((s32[3,16,16,128]{3,2,1,0:T(8,128)S(1)}, s32[3,16,16,128]{3,2,1,0:T(8,128)}, u32[]{:S(2)}) %copy-start.2) | copy-done | bytes 393240
  3.7 0.0 copy-start.3
  3.7 0.8 %copy-done.3 = f32[112,81]{1,0:T(8,128)S(1)} copy-done((f32[112,81]{1,0:T(8,128)S(1)}, f32[112,81]{1,0:T(8,128)}, u32[]{:S(2)}) %copy-start.3) | copy-done | bytes 36312
  4.5 0.0 copy-start.4
  4.5 0.8 copy-done.4
  5.3 72.0 %compliance.1 = (f32[4,256,128]{2,1,0:T(8,128)S(1)}, f32[3,16,16,128]{3,2,1,0:T(8,128)S(1)}) custom-call(f32[4,256,128]{2,1,0:T(8,128)S(1)} %copy-done, f32[3,16,16,128]{3,2,1,0:T(8,128)S(1)} %copy-done.1, s32[3,16,16,128]{3,2,1,0:T(8,128)S(1)} %copy-done.2, f32[81,81]{1,0:T(8,128)S(1)} %copy-done.4, f32[112,81]{1,0:T(8,128)S(1)} %copy-done.3), custom_call_target="tpu_custom_call" | custom-call | tf_op jit(solution)/shard_map/compliance/pallas_call | solution.py:1080
  77.3 0.8 %copy.9 = f32[4,256,128]{2,1,0:T(8,128)} copy(f32[4,256,128]{2,1,0:T(8,128)S(1)} %get-tuple-element.4) | data formatting | bytes 1048576
  78.1 0.7 copy.10
Async XLA Ops:
  0.6 1.0 %copy-start = (f32[4,256,128]{2,1,0:T(8,128)S(1)}, f32[4,256,128]{2,1,0:T(8,128)}, u32[]{:S(2)}) copy-start(f32[4,256,128]{2,1,0:T(8,128)} %refs_0_.1) | copy-start | bytes 1572868
  1.7 1.0 %copy-start.1 = (f32[3,16,16,128]{3,2,1,0:T(8,128)S(1)}, f32[3,16,16,128]{3,2,1,0:T(8,128)}, u32[]{:S(2)}) copy-start(f32[3,16,16,128]{3,2,1,0:T(8,128)} %refs_1_.1) | copy-start | bytes 1179652
  2.7 1.0 %copy-start.2 = (s32[3,16,16,128]{3,2,1,0:T(8,128)S(1)}, s32[3,16,16,128]{3,2,1,0:T(8,128)}, u32[]{:S(2)}) copy-start(s32[3,16,16,128]{3,2,1,0:T(8,128)} %refs_2_.1) | copy-start | bytes 1179652
  3.7 0.8 %copy-start.3 = (f32[112,81]{1,0:T(8,128)S(1)}, f32[112,81]{1,0:T(8,128)}, u32[]{:S(2)}) copy-start(f32[112,81]{1,0:T(8,128)} %constant.2.clone.refs_4_) | copy-start | bytes 108868
  4.5 0.8 %copy-start.4 = (f32[81,81]{1,0:T(8,128)S(1)}, f32[81,81]{1,0:T(8,128)}, u32[]{:S(2)}) copy-start(f32[81,81]{1,0:T(8,128)} %refs_3_.1) | copy-start | bytes 78736

commit v7 on v6

--- a/solution.py
+++ b/solution.py
@@ -255,7 +255,7 @@
                 r.psum[first : first + 32] += (BEND + bent[:, :LANES]) * (1.0 / FULL)
         return 0
 
-    lax.fori_loop(0, count, body, 0)
+    lax.fori_loop(0, count, body, 0, unroll=2)
 
 
 def inner_stage(r):
@@ -407,7 +407,7 @@
             out[2 * e + px] = jnp.where(sub, tile, 0.0)
         return 0
 
-    lax.fori_loop(0, 9, body, 0)
+    lax.fori_loop(0, 9, body, 0, unroll=9)
 
 
 def compress(tiles, out):
@@ -440,7 +440,7 @@
                 field[e, px, spot] = jnp.where(keep, moved, field[e, px, spot])
         return 0
 
-    lax.fori_loop(0, 9, body, 0)
+    lax.fori_loop(0, 9, body, 0, unroll=9)
 
 
 def top_stage(r):
@@ -477,7 +477,7 @@
             store[e, f, 6] = jnp.where(sub, shifted[0], turned[2])
         return 0
 
-    lax.fori_loop(0, 9, body, 0)
+    lax.fori_loop(0, 9, body, 0, unroll=9)
 
 
 def element_product(store, stiff, e):
@@ -518,7 +518,7 @@
                 acc[e + dx, f + dy, kind] += scaled[8 * place : 8 * place + 8]
         return energy
 
-    energy = lax.fori_loop(0, 8, body, jnp.zeros((8, LANES), F32))
+    energy = lax.fori_loop(0, 8, body, jnp.zeros((8, LANES), F32), unroll=8)
     r["tile", n][...] = sums_tile(gamma, energy)
     reduce_start(r, n)
     sub, lane = iota((8, LANES), 0) < 4, lax.rem(iota((8, LANES), 1), 64)
@@ -539,7 +539,7 @@
             top[2 * e + px] = jnp.where(sub, tops[px], 0.0)
         return 0
 
-    lax.fori_loop(0, 9, fold, 0)
+    lax.fori_loop(0, 9, fold, 0, unroll=9)
 
 
 def element_energy(r):
@@ -552,7 +552,7 @@
             energy = energy + chunk_sum(columns[f], products[f] * factor[f : f + 1, :])
         return energy
 
-    return lax.fori_loop(0, 8, body, jnp.zeros((8, LANES), F32))
+    return lax.fori_loop(0, 8, body, jnp.zeros((8, LANES), F32), unroll=8)
 
 
 def square_sum(field):
@@ -563,7 +563,7 @@
                 total = total + held * held
         return total
 
-    return lax.fori_loop(0, 8, body, jnp.zeros((8, LANES), F32))
+    return lax.fori_loop(0, 8, body, jnp.zeros((8, LANES), F32), unroll=8)
 
 
 def sums_tile(gamma, delta):
@@ -586,7 +586,7 @@
         body(e)
         return 0
 
-    lax.fori_loop(0, 9, step, 0)
+    lax.fori_loop(0, 9, step, 0, unroll=9)
 
 
 def cross_device(shift):
@@ -833,7 +833,7 @@
         r.grad[e] = before + pltpu.roll(layer, 4, 0)
         return layer
 
-    r.grad[8] = lax.fori_loop(0, 8, body, jnp.zeros((8, LANES), F32))
+    r.grad[8] = lax.fori_loop(0, 8, body, jnp.zeros((8, LANES), F32), unroll=8)
     role, lane = lax.axis_index("role"), lax.rem(iota((8, LANES), 1), 64)
     rim = jnp.zeros((8, LANES), F32)
     for k in range(9):

time: 79.1 us -> 68.1 us (0.86)
  Pallas kernels: 72 us -> 60.9 us
    pallas_call x1, Pallas kernels: 72 us -> 60.9 us  [on_device(): pl.pallas_call(functools.partial(whole_kernel, names), out_shape=(jax.Sha...]
where the time goes in v7:
time: 68.1 us; the launch traced here: 67.8 us
  Pallas kernels  60.9 us (89%)
  local copies, waits for them, and re-layouts  6.17 us (9%)
    pallas_call x1, Pallas kernels, on_device(): pl.pallas_call(functools.partial(whole_kernel, names), out_shape=(jax.Sha...  60.9 us
    unnamed x12, local copies, waits for them, and re-layouts  6.17 us

profile of v7, /device:TPU:1, one launch (start us, length us, event | category | flops | bytes accessed | tf_op | source)
XLA Modules:
  0.0 67.8 jit_solution(2126887123143463013)
XLA Ops:
  0.6 0.0 copy-start
  0.6 1.0 %copy-done = f32[4,256,128]{2,1,0:T(8,128)S(1)} copy-done((f32[4,256,128]{2,1,0:T(8,128)S(1)}, f32[4,256,128]{2,1,0:T(8,128)}, u32[]{:S(2)}) %copy-start) | copy-done | bytes 524312
  1.7 0.0 copy-start.1
  1.7 1.0 %copy-done.1 = f32[3,16,16,128]{3,2,1,0:T(8,128)S(1)} copy-done((f32[3,16,16,128]{3,2,1,0:T(8,128)S(1)}, f32[3,16,16,128]{3,2,1,0:T(8,128)}, u32[]{:S(2)}) %copy-start.1) | copy-done | bytes 393240
  2.7 0.0 copy-start.2
  2.7 1.0 %copy-done.2 = s32[3,16,16,128]{3,2,1,0:T(8,128)S(1)} copy-done((s32[3,16,16,128]{3,2,1,0:T(8,128)S(1)}, s32[3,16,16,128]{3,2,1,0:T(8,128)}, u32[]{:S(2)}) %copy-start.2) | copy-done | bytes 393240
  3.7 0.0 copy-start.3
  3.7 0.8 %copy-done.3 = f32[112,81]{1,0:T(8,128)S(1)} copy-done((f32[112,81]{1,0:T(8,128)S(1)}, f32[112,81]{1,0:T(8,128)}, u32[]{:S(2)}) %copy-start.3) | copy-done | bytes 36312
  4.5 0.0 copy-start.4
  4.5 0.8 %copy-done.4 = f32[81,81]{1,0:T(8,128)S(1)} copy-done((f32[81,81]{1,0:T(8,128)S(1)}, f32[81,81]{1,0:T(8,128)}, u32[]{:S(2)}) %copy-start.4) | copy-done | bytes 26268
  5.3 60.9 %compliance.1 = (f32[4,256,128]{2,1,0:T(8,128)S(1)}, f32[3,16,16,128]{3,2,1,0:T(8,128)S(1)}) custom-call(f32[4,256,128]{2,1,0:T(8,128)S(1)} %copy-done, f32[3,16,16,128]{3,2,1,0:T(8,128)S(1)} %copy-done.1, s32[3,16,16,128]{3,2,1,0:T(8,128)S(1)} %copy-done.2, f32[81,81]{1,0:T(8,128)S(1)} %copy-done.4, f32[112,81]{1,0:T(8,128)S(1)} %copy-done.3), custom_call_target="tpu_custom_call" | custom-call | tf_op jit(solution)/shard_map/compliance/pallas_call | solution.py:1080
  66.2 0.8 %copy.9 = f32[4,256,128]{2,1,0:T(8,128)} copy(f32[4,256,128]{2,1,0:T(8,128)S(1)} %get-tuple-element.4) | data formatting | bytes 1048576
  67.0 0.7 %copy.10 = f32[3,16,16,128]{3,2,1,0:T(8,128)} copy(f32[3,16,16,128]{3,2,1,0:T(8,128)S(1)} %get-tuple-element.5) | data formatting | bytes 786432
Async XLA Ops:
  0.6 1.0 %copy-start = (f32[4,256,128]{2,1,0:T(8,128)S(1)}, f32[4,256,128]{2,1,0:T(8,128)}, u32[]{:S(2)}) copy-start(f32[4,256,128]{2,1,0:T(8,128)} %refs_0_.1) | copy-start | bytes 1572868
  1.7 1.0 %copy-start.1 = (f32[3,16,16,128]{3,2,1,0:T(8,128)S(1)}, f32[3,16,16,128]{3,2,1,0:T(8,128)}, u32[]{:S(2)}) copy-start(f32[3,16,16,128]{3,2,1,0:T(8,128)} %refs_1_.1) | copy-start | bytes 1179652
  2.7 1.0 %copy-start.2 = (s32[3,16,16,128]{3,2,1,0:T(8,128)S(1)}, s32[3,16,16,128]{3,2,1,0:T(8,128)}, u32[]{:S(2)}) copy-start(s32[3,16,16,128]{3,2,1,0:T(8,128)} %refs_2_.1) | copy-start | bytes 1179652
  3.7 0.8 %copy-start.3 = (f32[112,81]{1,0:T(8,128)S(1)}, f32[112,81]{1,0:T(8,128)}, u32[]{:S(2)}) copy-start(f32[112,81]{1,0:T(8,128)} %constant.2.clone.refs_4_) | copy-start | bytes 108868
  4.5 0.8 %copy-start.4 = (f32[81,81]{1,0:T(8,128)S(1)}, f32[81,81]{1,0:T(8,128)}, u32[]{:S(2)}) copy-start(f32[81,81]{1,0:T(8,128)} %refs_3_.1) | copy-start | bytes 78736
